TPU v7x, 128 devices: a whole 4x4x4 slice. The times are simulated.
128 devices in a mesh: tm: 16 (over z, y_hi, core), space: 8 (over x, y_lo).
Axes of the slice: x: 4, y: 4 (y_hi: 2, y_lo: 2; y = y_hi * 2 + y_lo), z: 4, core: 2. Of those that a mesh axis runs over, the one named last changes fastest.
Arguments:
- rhs: float32 [32, 384, 2048], P('tm', None, 'space'), may hold values from -6 to 6
- material: float32 [2048], P('space'), may hold values from 1 to 4
- modal_rates: float32 [384], replicated, may hold values from 0.25 to 8
- modes_in: float32 [384, 384], replicated, may hold values from -0.3125 to 0.3125
- modes_out: float32 [384, 384], replicated, may hold values from -0.3125 to 0.3125
- face_lift: float32 [6, 384, 96], replicated, may hold values from -0.109375 to 0.109375
- neighbours: int32 [6, 2048], P(None, 'space'), may hold values from 0 to 383, as said below
- halo_send: int32 [2, 1024], P(None, 'space'), may hold values from 0 to 255, as said below
Outputs:
- solution: float32 [32, 384, 2048], P('tm', None, 'space')
Inputs may be any that keep to these rules, and one draw needn't show every extreme that they name: neighbours[f, e] names the element across face f of element e (faces at -x, +x, -y, +y, -z, +z) by its position in e's block of 256; each block is a slab of 2 x 8 x 16 elements, periodic in y and z, numbered in an order of its own. A value 256 + t occurs in rows 0 and 1 only and names the t-th element sent from the block below (row 0) or above (row 1). `halo_send`: in each block of 128 entries, row 0 lists the positions of the slab's elements on its -x side and row 1 those on its +x side, in the order in which the neighbouring slabs' neighbours refer to them; together they name every element of the slab once.
All inputs are finite; a program needn't handle non-finite values.
Results may differ from a plain program's by a relative error of at most 0.00026.
Values sent between devices are 32-bit elements; how exact they have to be, the bound alone decides.
No kernel may reach another device: no remote copies, remote signals or barrier semaphores. Data moves between devices by JAX's collectives and lax.ppermute only.
A program may use at most 64 MiB of HBM per device.

v0:
```python
import math

import jax
import jax.numpy as jnp
from jax import lax
from jax.sharding import PartitionSpec as P

FIELDS = 6
NP = 4
SWEEPS = 2


OPPOSITE = (1, 0, 3, 2, 5, 4)


def padded(cells, sides, width):
    for axis, dim in sides:
        count = lax.axis_size(axis)
        ends = count - 1
        head = lax.slice_in_dim(cells, 0, width, axis=dim)
        tail = lax.slice_in_dim(cells, cells.shape[dim] - width, cells.shape[dim], axis=dim)
        cells = jnp.concatenate(
            [
                lax.ppermute(tail, axis, [(i, (i + 1) % count) for i in range(ends)]),
                cells,
                lax.ppermute(head, axis, [((i + 1) % count, i) for i in range(ends)]),
            ],
            axis=dim,
        )
    return cells


def from_partner(x, axis, bit):
    return lax.ppermute(x, axis, [(i, i ^ 1 << bit) for i in range(lax.axis_size(axis))])


def face_trace(unknowns, which_face):
    leading = unknowns.shape[:-2]
    shaped = unknowns.reshape(leading + (FIELDS, NP, NP, NP, unknowns.shape[-1]))
    node_axis = len(leading) + 1 + which_face // 2
    node_place = 0 if which_face % 2 == 0 else NP - 1
    face_piece = lax.index_in_dim(shaped, node_place, node_axis, keepdims=False)
    return face_piece.reshape(leading + (FIELDS * NP * NP, unknowns.shape[-1]))


def element_solve(given_rhs, lam_real, lam_imag, material, modal_rates, modes_in, modes_out):
    projected = jnp.einsum("mn,cqne->cqme", modes_in, given_rhs, precision=lax.Precision.HIGHEST)
    denom_real = lam_real[:, None, None] * material[None, None, :] + modal_rates[None, :, None]
    denom_imag = (
        lam_imag[:, None, None] * material[None, None, :]
        + jnp.zeros_like(modal_rates)[None, :, None]
    )
    magnitude = denom_real * denom_real + denom_imag * denom_imag
    upper_real = (projected[0] * denom_real + projected[1] * denom_imag) / magnitude
    upper_imag = (projected[1] * denom_real - projected[0] * denom_imag) / magnitude
    divided = jnp.stack([upper_real, upper_imag])
    return jnp.einsum("mn,cqne->cqme", modes_out, divided, precision=lax.Precision.HIGHEST)


def face_coupling(unknowns, neighbours, halo_send, face_lift):
    traces = [face_trace(unknowns, which_face) for which_face in range(6)]
    rim_width = halo_send.shape[1]
    outgoing = jnp.concatenate(
        [jnp.take(traces[0], halo_send[0], axis=3), jnp.take(traces[1], halo_send[1], axis=3)],
        axis=3,
    )
    arrived = padded(outgoing, (("space", 3),), rim_width)
    from_lower = arrived[..., :rim_width]
    from_upper = arrived[..., 3 * rim_width :]
    gathered = []
    for which_face in range(6):
        source = traces[OPPOSITE[which_face]]
        if which_face == 0:
            source = jnp.concatenate([source, from_lower], axis=3)
        elif which_face == 1:
            source = jnp.concatenate([source, from_upper], axis=3)
        gathered.append(jnp.take(source, neighbours[which_face], axis=3))
    return jnp.einsum(
        "fmt,fcqte->cqme", face_lift, jnp.stack(gathered), precision=lax.Precision.HIGHEST
    )


def pair_twiddle(position, bit_level):
    half_size = 1 << bit_level
    offset = jnp.bitwise_and(position, half_size - 1).astype(jnp.float32)
    angles = -math.pi / half_size * offset
    upper_half = jnp.bitwise_and(jnp.right_shift(position, bit_level), 1) == 1
    return (jnp.cos(angles), jnp.sin(angles), upper_half)


def phase_tables(frequencies, slot_index, total_steps):
    phase_index = frequencies[..., None] * slot_index % total_steps
    angles = 2.0 * math.pi / total_steps * phase_index.astype(jnp.float32)
    return (jnp.cos(angles), jnp.sin(angles))


def precise_einsum(pattern, table, values):
    return jnp.einsum(pattern, table, values, precision=lax.Precision.HIGHEST)


def shards(rhs, material, modal_rates, modes_in, modes_out, face_lift, neighbours, halo_send):
    local_steps = rhs.shape[0]
    devices_tm = lax.axis_size("tm")
    total_steps = local_steps * devices_tm
    decay_ratio = 0.1 ** (1.0 / total_steps)
    position = lax.axis_index("tm")
    slot_index = jnp.arange(local_steps, dtype=jnp.int32)
    step_index = position * local_steps + slot_index
    growth = decay_ratio ** step_index.astype(jnp.float32)
    scaled = rhs * growth[:, None, None]
    level_count = devices_tm.bit_length() - 1
    top_level = level_count - 1
    partner = from_partner(scaled, "tm", top_level)
    twiddle_cos, twiddle_sin, upper_half = pair_twiddle(position, top_level)
    difference = partner - scaled
    real_part = jnp.where(upper_half, difference * twiddle_cos, scaled + partner)
    imag_part = jnp.where(upper_half, difference * twiddle_sin, jnp.zeros_like(scaled))
    for bit_level in range(level_count - 2, -1, -1):
        partner = from_partner(jnp.stack([real_part, imag_part]), "tm", bit_level)
        twiddle_cos, twiddle_sin, upper_half = pair_twiddle(position, bit_level)
        diff_real = partner[0] - real_part
        diff_imag = partner[1] - imag_part
        new_real = jnp.where(
            upper_half, diff_real * twiddle_cos - diff_imag * twiddle_sin, real_part + partner[0]
        )
        new_imag = jnp.where(
            upper_half, diff_real * twiddle_sin + diff_imag * twiddle_cos, imag_part + partner[1]
        )
        real_part, imag_part = (new_real, new_imag)
    first_freq = jnp.zeros((), jnp.int32)
    for bit_level in range(level_count):
        digit = jnp.bitwise_and(jnp.right_shift(position, bit_level), 1)
        first_freq = first_freq + jnp.left_shift(digit, level_count - 1 - bit_level)
    local_freq = first_freq + devices_tm * slot_index
    local_cos, local_sin = phase_tables(local_freq, slot_index, total_steps)
    spec_real = precise_einsum("aq,qne->ane", local_cos, real_part) + precise_einsum(
        "aq,qne->ane", local_sin, imag_part
    )
    spec_imag = precise_einsum("aq,qne->ane", local_cos, imag_part) - precise_einsum(
        "aq,qne->ane", local_sin, real_part
    )
    spectrum = jnp.stack([spec_real, spec_imag])
    frequencies = first_freq + devices_tm * slot_index
    freq_angles = 2.0 * math.pi / total_steps * frequencies.astype(jnp.float32)
    lam_real = 1.0 - decay_ratio * jnp.cos(freq_angles)
    lam_imag = decay_ratio * jnp.sin(freq_angles)
    current = element_solve(
        spectrum, lam_real, lam_imag, material, modal_rates, modes_in, modes_out
    )
    for sweep_number in range(SWEEPS):
        corrected = spectrum - face_coupling(current, neighbours, halo_send, face_lift)
        current = element_solve(
            corrected, lam_real, lam_imag, material, modal_rates, modes_in, modes_out
        )
    local_freq = first_freq + devices_tm * slot_index
    local_cos, local_sin = phase_tables(local_freq, slot_index, total_steps)
    real_part = (
        precise_einsum("aq,ane->qne", local_cos, current[0])
        - precise_einsum("aq,ane->qne", local_sin, current[1])
    ) / local_steps
    imag_part = (
        precise_einsum("aq,ane->qne", local_cos, current[1])
        + precise_einsum("aq,ane->qne", local_sin, current[0])
    ) / local_steps
    for bit_level in range(level_count):
        partner = from_partner(jnp.stack([real_part, imag_part]), "tm", bit_level)
        twiddle_cos, twiddle_sin, upper_half = pair_twiddle(position, bit_level)
        other_real = jnp.where(upper_half, real_part, partner[0])
        other_imag = jnp.where(upper_half, imag_part, partner[1])
        keep_real = jnp.where(upper_half, partner[0], real_part)
        keep_imag = jnp.where(upper_half, partner[1], imag_part)
        rotated_real = other_real * twiddle_cos + other_imag * twiddle_sin
        rotated_imag = other_imag * twiddle_cos - other_real * twiddle_sin
        real_part = 0.5 * jnp.where(upper_half, keep_real - rotated_real, keep_real + rotated_real)
        imag_part = 0.5 * jnp.where(upper_half, keep_imag - rotated_imag, keep_imag + rotated_imag)
    return real_part / growth[:, None, None]


def solution(mesh):
    return jax.shard_map(
        shards,
        mesh=mesh,
        in_specs=(
            P("tm", None, "space"),
            P("space"),
            P(),
            P(),
            P(),
            P(),
            P(None, "space"),
            P(None, "space"),
        ),
        out_specs=P("tm", None, "space"),
        check_vma=False,
    )
```

profile of v0, /device:TPU:4, one launch (start us, length us, event | category | flops | bytes accessed | tf_op | source)
XLA Modules:
  0.0 432.2 jit_solution(8385716779802364396)
XLA Ops:
  2.0 4.0 collective-permute-start
  6.1 17.5 %collective-permute-done = f32[2,384,256]{2,0,1:T(2,128)} collective-permute-done((f32[2,384,256]{2,0,1:T(2,128)S(1)}, f32[2,384,256]{2,0,1:T(2,128)}, u32[]{:S(2)}, u32[]{:S(2)}) %collective-permute-start) | collective-permute-done | bytes 786464 | tf_op jit(solution)/shard_map/ppermute | solution.py:34
  29.6 33.9 %collective-permute-done.1 = f32[2,2,384,256]{3,1,2,0:T(2,128)} collective-permute-done((f32[2,2,384,256]{3,1,2,0:T(2,128)}, f32[2,2,384,256]{3,1,2,0:T(2,128)}, u32[]{:S(2)}, u32[]{:S(2)}) %collective-permute-start.1) | collective-permute-done | bytes 1572896 | tf_op jit(solution)/shard_map/ppermute | solution.py:34
  66.9 3.2 collective-permute-start.2
  71.0 32.2 %collective-permute-done.2 = f32[2,2,384,256]{3,1,2,0:T(2,128)} collective-permute-done((f32[2,2,384,256]{3,1,2,0:T(2,128)S(1)}, f32[2,2,384,256]{3,1,2,0:T(2,128)}, u32[]{:S(2)}, u32[]{:S(2)}) %collective-permute-start.2) | collective-permute-done | bytes 1572896 | tf_op jit(solution)/shard_map/ppermute | solution.py:34
  113.9 3.4 fusion.81
  117.3 3.4 fusion.79
  120.7 3.4 fusion.43
  124.1 3.9 fusion.42
  129.4 5.1 %fusion.31 = f32[2,2,384,256]{2,3,1,0:T(8,128)S(1)} fusion(f32[2,2,384,256]{3,1,2,0:T(2,128)S(1)} %pad_maximum_fusion.3, f32[384,384]{1,0:T(8,128)S(1)} %copy-done.5), kind=kOutput, calls=%fused_computation.58 | convolution fusion | flops 1811939328 | bytes 3735552 | tf_op jit(solution)/shard_map/mn,cqne->cqme/dot_general | solution.py:47
  135.6 4.4 %fusion.28 = f32[2,2,384,256]{2,3,1,0:T(8,128)} fusion(f32[1,2,384,256]{2,3,1,0:T(8,128)S(1)} %get-tuple-element.29, f32[1,2,384,256]{2,3,1,0:T(8,128)S(1)} %get-tuple-element.28, f32[384,384]{1,0:T(8,128)S(1)} %copy-done.8), kind=kOutput, calls=%fused_computation.57 | convolution fusion | flops 1812332544 | bytes 3735552 | tf_op jit(solution)/shard_map/mn,cqne->cqme/dot_general | solution.py:57
  150.6 3.4 collective-permute-start.5
  175.2 3.1 gather_fusion.6
  178.3 3.2 gather_fusion.7
  194.0 7.9 %fusion.2 = f32[2,2,256,384,1]{3,2,4,1,0:T(8,128)} fusion(f32[6,2,2,96,256]{3,2,1,4,0:T(2,128)S(1)} %bitcast_dynamic-update-slice_fusion.6, f32[6,384,96]{1,2,0:T(8,128)S(1)} %copy-done), kind=kOutput, calls=%fused_computation.18 | convolution fusion | flops 2717908992 | bytes 4816896 | tf_op jit(solution)/shard_map/fmt,fcqte->cqme/dot_general | solution.py:78
  201.9 3.8 copy.65
  208.2 5.1 %fusion.34 = f32[2,2,384,256]{2,3,1,0:T(8,128)S(1)} fusion(f32[2,2,384,256]{3,1,2,0:T(2,128)S(1)} %bitcast_subtract_fusion.1, f32[384,384]{1,0:T(8,128)S(1)} %copy-done.6), kind=kOutput, calls=%fused_computation.59 | convolution fusion | flops 1811939328 | bytes 3735552 | tf_op jit(solution)/shard_map/mn,cqne->cqme/dot_general | solution.py:47
  214.4 4.2 fusion.25
  229.2 4.3 %collective-permute-start.7 = (f32[2,2,96,128]{2,1,0,3:T(2,128)}, f32[2,2,96,128]{2,1,0,3:T(2,128)}, u32[]{:S(2)}, u32[]{:S(2)}) collective-permute-start(f32[2,2,96,128]{2,1,0,3:T(2,128)} %select_bitcast_fusion), channel_id=1, source_target_pairs={{1,0},{2,1},{3,2},{4,3},{5,4},{6,5},{7,6},{9,8},{10,9},{11,10},{12... | collective-permute-start | bytes 589832 | tf_op jit(solution)/shard_map/ppermute | solution.py:26
  243.0 3.2 gather_fusion.12
  248.1 3.2 gather_fusion.13
  270.5 7.5 %fusion = f32[2,2,256,384,1]{3,2,4,1,0:T(8,128)} fusion(f32[6,2,2,96,256]{3,2,1,4,0:T(2,128)S(1)} %bitcast_dynamic-update-slice_fusion, f32[6,384,96]{1,2,0:T(8,128)S(1)} %copy-done), kind=kOutput, calls=%fused_computation.16 | convolution fusion | flops 2717908992 | bytes 4816896 | tf_op jit(solution)/shard_map/fmt,fcqte->cqme/dot_general | solution.py:78
  278.0 4.1 copy.67
  284.7 5.1 %fusion.37 = f32[2,2,384,256]{2,3,1,0:T(8,128)S(1)} fusion(f32[2,2,384,256]{3,1,2,0:T(2,128)S(1)} %bitcast_subtract_fusion, f32[384,384]{1,0:T(8,128)S(1)} %copy-done.7), kind=kOutput, calls=%fused_computation.60 | convolution fusion | flops 1811939328 | bytes 3735552 | tf_op jit(solution)/shard_map/mn,cqne->cqme/dot_general | solution.py:47
  290.9 3.0 fusion.22
  294.8 3.6 fusion.85
  301.9 3.1 fusion.40
  305.0 3.1 fusion.41
  308.9 3.4 collective-permute-done.8
  317.6 35.0 %collective-permute-done.9 = f32[2,2,384,256]{3,1,2,0:T(2,128)S(1)} collective-permute-done((f32[2,2,384,256]{3,1,2,0:T(2,128)S(1)}, f32[2,2,384,256]{3,1,2,0:T(2,128)S(1)}, u32[]{:S(2)}, u32[]{:S(2)}) %collective-permute-start.9) | collective-permute-done | bytes 1572896 | tf_op jit(solution)/shard_map/ppermute | solution.py:34
  356.1 35.0 %collective-permute-done.10 = f32[2,2,384,256]{3,1,2,0:T(2,128)S(1)} collective-permute-done((f32[2,2,384,256]{3,1,2,0:T(2,128)S(1)}, f32[2,2,384,256]{3,1,2,0:T(2,128)S(1)}, u32[]{:S(2)}, u32[]{:S(2)}) %collective-permute-start.10) | collective-permute-done | bytes 1572896 | tf_op jit(solution)/shard_map/ppermute | solution.py:34
  396.3 33.6 %collective-permute-done.11 = f32[2,2,384,256]{3,1,2,0:T(2,128)S(1)} collective-permute-done((f32[2,2,384,256]{3,1,2,0:T(2,128)S(1)}, f32[2,2,384,256]{3,1,2,0:T(2,128)S(1)}, u32[]{:S(2)}, u32[]{:S(2)}) %collective-permute-start.11) | collective-permute-done | bytes 1572896 | tf_op jit(solution)/shard_map/ppermute | solution.py:34
  (202 shorter events, 138.2 us)
Async XLA Ops:
  0.0 194.0 %copy-start = (f32[6,384,96]{1,2,0:T(8,128)S(1)}, f32[6,384,96]{1,2,0:T(8,128)}, u32[]{:S(2)}) copy-start(f32[6,384,96]{1,2,0:T(8,128)} %param.19) | copy-start | bytes 2654212
  0.0 23.6 %copy-start.11 = (f32[2,384,256]{2,1,0:T(8,128)S(1)}, f32[2,384,256]{2,1,0:T(8,128)}, u32[]{:S(2)}) copy-start(f32[2,384,256]{2,1,0:T(8,128)} %param.14) | copy-start | bytes 2359300
  0.0 25.7 %copy-start.31 = (f32[2]{0:T(128)}, f32[2]{0:T(128)S(1)}, u32[]{:S(2)}) copy-start(f32[2]{0:T(128)S(1)} %convert_power_fusion) | copy-start | bytes 28
  2.0 21.6 %collective-permute-start = (f32[2,384,256]{2,0,1:T(2,128)S(1)}, f32[2,384,256]{2,0,1:T(2,128)}, u32[]{:S(2)}, u32[]{:S(2)}) collective-permute-start(f32[2,384,256]{2,0,1:T(2,128)S(1)} %copy_multiply_fusion), channel_id=1, source_target_pairs={{0,64},{8,72},{16,80},{24,88},{32,96},{40,104},{48,112},{56,120},{... | collective-permute-start | bytes 2359304 | tf_op jit(solution)/shard_map/ppermute | solution.py:34
  27.6 35.9 %collective-permute-start.1 = (f32[2,2,384,256]{3,1,2,0:T(2,128)}, f32[2,2,384,256]{3,1,2,0:T(2,128)}, u32[]{:S(2)}, u32[]{:S(2)}) collective-permute-start(f32[2,2,384,256]{3,1,2,0:T(2,128)} %pad_maximum_fusion), channel_id=1, source_target_pairs={{0,32},{8,40},{16,48},{24,56},{32,0},{40,8},{48,16},{56,24},{64,96... | collective-permute-start | bytes 4718600 | tf_op jit(solution)/shard_map/ppermute | solution.py:34
  66.9 36.3 %collective-permute-start.2 = (f32[2,2,384,256]{3,1,2,0:T(2,128)S(1)}, f32[2,2,384,256]{3,1,2,0:T(2,128)}, u32[]{:S(2)}, u32[]{:S(2)}) collective-permute-start(f32[2,2,384,256]{3,1,2,0:T(2,128)S(1)} %pad_maximum_fusion.1), channel_id=1, source_target_pairs={{0,16},{8,24},{16,0},{24,8},{32,48},{40,56},{48,32},{56,40},{64,80... | collective-permute-start | bytes 4718600 | tf_op jit(solution)/shard_map/ppermute | solution.py:34
  105.7 5.4 %copy-start.43 = (f32[256]{0:T(256)S(1)}, f32[256]{0:T(256)}, u32[]{:S(2)}) copy-start(f32[256]{0:T(256)} %param.15) | copy-start | bytes 3076
  107.6 3.9 collective-permute-start.3
  129.4 5.1 %copy-start.29 = (f32[384]{0:T(512)S(1)}, f32[384]{0:T(512)}, u32[]{:S(2)}) copy-start(f32[384]{0:T(512)} %param.16) | copy-start | bytes 4612
  150.6 30.9 %collective-permute-start.5 = (f32[2,2,96,128]{2,1,0,3:T(2,128)}, f32[2,2,96,128]{2,1,0,3:T(2,128)}, u32[]{:S(2)}, u32[]{:S(2)}) collective-permute-start(f32[2,2,96,128]{2,1,0,3:T(2,128)} %select_bitcast_fusion.2), channel_id=1, source_target_pairs={{1,0},{2,1},{3,2},{4,3},{5,4},{6,5},{7,6},{9,8},{10,9},{11,10},{12... | collective-permute-start | bytes 589832 | tf_op jit(solution)/shard_map/ppermute | solution.py:26
  159.5 25.5 %collective-permute-start.4 = (f32[2,2,96,128]{2,1,0,3:T(2,128)}, f32[2,2,96,128]{2,1,0,3:T(2,128)}, u32[]{:S(2)}, u32[]{:S(2)}) collective-permute-start(f32[2,2,96,128]{2,1,0,3:T(2,128)} %select_bitcast_fusion.3), channel_id=1, source_target_pairs={{0,1},{1,2},{2,3},{3,4},{4,5},{5,6},{6,7},{8,9},{9,10},{10,11},{11... | collective-permute-start | bytes 589832 | tf_op jit(solution)/shard_map/ppermute | solution.py:24
  167.0 3.9 copy-start.16
  167.0 6.0 %copy-start.17 = (f32[2,2,96,256]{2,1,3,0:T(2,128)S(1)}, f32[2,2,96,256]{2,1,3,0:T(2,128)}, u32[]{:S(2)}) copy-start(f32[2,2,96,256]{2,1,3,0:T(2,128)} %copy.36) | copy-start | bytes 1179652
  170.9 10.6 %copy-start.14 = (f32[2,2,96,256]{2,1,3,0:T(2,128)S(1)}, f32[2,2,96,256]{2,1,3,0:T(2,128)}, u32[]{:S(2)}) copy-start(f32[2,2,96,256]{2,1,3,0:T(2,128)} %copy.33) | copy-start | bytes 1179652
  178.3 6.7 %copy-start.15 = (f32[2,2,96,256]{2,1,3,0:T(2,128)S(1)}, f32[2,2,96,256]{2,1,3,0:T(2,128)}, u32[]{:S(2)}) copy-start(f32[2,2,96,256]{2,1,3,0:T(2,128)} %copy.30) | copy-start | bytes 1179652
  186.4 4.8 %copy-start.24 = (f32[256,2,2,96]{3,2,1,0:T(2,128)S(1)}, f32[256,2,2,96]{3,2,1,0:T(2,128)}, u32[]{:S(2)}) copy-start(f32[256,2,2,96]{3,2,1,0:T(2,128)} %gather_fusion.4) | copy-start | bytes 1179652
  188.5 3.9 copy-start.25
  188.5 3.9 copy-start.37
  229.2 30.2 %collective-permute-start.7 = (f32[2,2,96,128]{2,1,0,3:T(2,128)}, f32[2,2,96,128]{2,1,0,3:T(2,128)}, u32[]{:S(2)}, u32[]{:S(2)}) collective-permute-start(f32[2,2,96,128]{2,1,0,3:T(2,128)} %select_bitcast_fusion), channel_id=1, source_target_pairs={{1,0},{2,1},{3,2},{4,3},{5,4},{6,5},{7,6},{9,8},{10,9},{11,10},{12... | collective-permute-start | bytes 589832 | tf_op jit(solution)/shard_map/ppermute | solution.py:26
  239.2 23.7 %collective-permute-start.6 = (f32[2,2,96,128]{2,1,0,3:T(2,128)}, f32[2,2,96,128]{2,1,0,3:T(2,128)}, u32[]{:S(2)}, u32[]{:S(2)}) collective-permute-start(f32[2,2,96,128]{2,1,0,3:T(2,128)} %select_bitcast_fusion.1), channel_id=1, source_target_pairs={{0,1},{1,2},{2,3},{3,4},{4,5},{5,6},{6,7},{8,9},{9,10},{10,11},{11... | collective-permute-start | bytes 589832 | tf_op jit(solution)/shard_map/ppermute | solution.py:24
  252.6 6.8 %copy-start.12 = (f32[2,2,96,256]{2,1,3,0:T(2,128)S(1)}, f32[2,2,96,256]{2,1,3,0:T(2,128)}, u32[]{:S(2)}) copy-start(f32[2,2,96,256]{2,1,3,0:T(2,128)} %copy.45) | copy-start | bytes 1179652
  257.3 5.6 %copy-start.13 = (f32[2,2,96,256]{2,1,3,0:T(2,128)S(1)}, f32[2,2,96,256]{2,1,3,0:T(2,128)}, u32[]{:S(2)}) copy-start(f32[2,2,96,256]{2,1,3,0:T(2,128)} %copy.42) | copy-start | bytes 1179652
  260.8 5.7 %copy-start.41 = (pred[256]{0:T(512)(128)(4,1)S(1)}, pred[256]{0:T(512)(128)(4,1)}, u32[]{:S(2)}) copy-start(pred[256]{0:T(512)(128)(4,1)} %compare_and_fusion) | copy-start | bytes 772
  262.9 5.0 %copy-start.40 = (pred[256]{0:T(512)(128)(4,1)S(1)}, pred[256]{0:T(512)(128)(4,1)}, u32[]{:S(2)}) copy-start(pred[256]{0:T(512)(128)(4,1)} %compare_and_fusion.5) | copy-start | bytes 772
  264.3 4.1 copy-start.18
  264.3 4.1 copy-start.39
  278.0 4.1 copy-start.3
  308.8 3.5 collective-permute-start.8
  314.6 38.0 %collective-permute-start.9 = (f32[2,2,384,256]{3,1,2,0:T(2,128)S(1)}, f32[2,2,384,256]{3,1,2,0:T(2,128)S(1)}, u32[]{:S(2)}, u32[]{:S(2)}) collective-permute-start(f32[2,2,384,256]{3,1,2,0:T(2,128)S(1)} %pad_maximum_fusion.5), channel_id=1, source_target_pairs={{0,16},{8,24},{16,0},{24,8},{32,48},{40,56},{48,32},{56,40},{64,80... | collective-permute-start | bytes 4718600 | tf_op jit(solution)/shard_map/ppermute | solution.py:34
  355.4 35.7 %collective-permute-start.10 = (f32[2,2,384,256]{3,1,2,0:T(2,128)S(1)}, f32[2,2,384,256]{3,1,2,0:T(2,128)S(1)}, u32[]{:S(2)}, u32[]{:S(2)}) collective-permute-start(f32[2,2,384,256]{3,1,2,0:T(2,128)S(1)} %pad_maximum_fusion.6), channel_id=1, source_target_pairs={{0,32},{8,40},{16,48},{24,56},{32,0},{40,8},{48,16},{56,24},{64,96... | collective-permute-start | bytes 4718600 | tf_op jit(solution)/shard_map/ppermute | solution.py:34
  392.9 37.0 %copy-start.32 = (f32[2]{0:T(128)S(1)}, f32[2]{0:T(128)}, u32[]{:S(2)}) copy-start(f32[2]{0:T(128)} %copy-done.31) | copy-start | bytes 28
  393.6 36.3 %collective-permute-start.11 = (f32[2,2,384,256]{3,1,2,0:T(2,128)S(1)}, f32[2,2,384,256]{3,1,2,0:T(2,128)S(1)}, u32[]{:S(2)}, u32[]{:S(2)}) collective-permute-start(f32[2,2,384,256]{3,1,2,0:T(2,128)S(1)} %pad_maximum_fusion.7), channel_id=1, source_target_pairs={{0,64},{8,72},{16,80},{24,88},{32,96},{40,104},{48,112},{56,120},{... | collective-permute-start | bytes 4718600 | tf_op jit(solution)/shard_map/ppermute | solution.py:34
  (24 other events, 53.7 us)
where the time goes:
time: 440 us; the launch traced here: 432 us
  waiting for transfers between devices  191 us (43%)
  local copies, waits for them, and re-layouts  85.9 us (20%)
  matrix products  69 us (16%)
  other arithmetic  57.6 us (13%)
  starting transfers between devices  27.2 us (6%)
    ppermute x8, waiting for transfers between devices, from_partner(): lax.ppermute(x, axis, [(i, i ^ 1 << bit) for i in range(lax.axis_size(axi...  191 us
    gather x12, local copies, waits for them, and re-layouts, face_coupling(): gathered.append(jnp.take(source, neighbours[which_face], axis=3))  29.6 us
    dot_general x8, matrix products, precise_einsum(): return jnp.einsum(pattern, table, values, precision=lax.Precision.HIGHEST)  26.6 us
    another operation x12, local copies, waits for them, and re-layouts, face_trace(): return face_piece.reshape(leading + (FIELDS * NP * NP, unknowns.shape[-1]))  22 us
    dot_general x3, matrix products, element_solve(): jnp.einsum('mn,cqne->cqme', modes_in, given_rhs, precision=lax.Precision....  15.4 us
    dot_general x2, matrix products, face_coupling(): jnp.einsum('fmt,fcqte->cqme', face_lift, jnp.stack(gathered), precision=l...  15.4 us
    ppermute x8, starting transfers between devices, from_partner(): lax.ppermute(x, axis, [(i, i ^ 1 << bit) for i in range(lax.axis_size(axi...  15.1 us
    dot_general x3, matrix products, element_solve(): jnp.einsum('mn,cqne->cqme', modes_out, divided, precision=lax.Precision.H...  11.6 us
  transfers between devices with their start and end apart: 12, of which 8 were waited for; matrix products, arithmetic and copies ran while one was open for 14% of the time, Pallas kernels for 0%

commit v1 on v0

v1 whole, which is shorter than its diff:
```python
import math

import jax
import jax.numpy as jnp
import ml_dtypes
import numpy as np
from jax import lax
from jax.experimental import pallas as pl
from jax.experimental.pallas import tpu as pltpu
from jax.sharding import PartitionSpec as P

NB = 384
NFT = 96
LANES = 128
STEPS = 32
SLAB = 256
SHEET = 16
ROWS = STEPS * SHEET
HALF = ROWS // 2
SLABS = 8
DECAY = 0.1 ** (1.0 / STEPS)

RING = (0, 1, 4, 5, 8, 9, 12, 13, 14, 15, 10, 11, 6, 7, 2, 3)
SHEET_OF = tuple(RING.index(device) for device in range(16))
SAME_CHIP = [(i, i ^ 1) for i in range(16)]
NEXT_CHIP = [(RING[2 * i + 1], RING[(2 * i + 2) % 16]) for i in range(8)]
NEXT_CHIP = NEXT_CHIP + [(b, a) for a, b in NEXT_CHIP]
EVEN_SIDES = [(i, i ^ 1) for i in range(8)]
ODD_SIDES = [(1, 2), (2, 1), (3, 4), (4, 3), (5, 6), (6, 5)]

F32 = jnp.float32
BF16 = jnp.bfloat16
NN = (((1,), (0,)), ((), ()))
NT = (((1,), (1,)), ((), ()))
TN = (((0,), (0,)), ((), ()))


def halves(table):
    high = table.astype(np.float32).astype(ml_dtypes.bfloat16)
    low = (table - high.astype(np.float64)).astype(np.float32).astype(ml_dtypes.bfloat16)
    return high, low


def transform_tables():
    steps = np.arange(STEPS, dtype=np.float64)
    freqs = np.arange(STEPS // 2, dtype=np.float64)
    angles = 2.0 * np.pi / STEPS * np.outer(freqs, steps)
    real, imag = np.cos(angles), -np.sin(angles)
    imag[0] = np.cos(np.pi * steps)
    forward = np.concatenate([real, imag]) * DECAY**steps
    real_back, imag_back = 2.0 * np.cos(angles), -2.0 * np.sin(angles)
    real_back[0] = 1.0
    imag_back[0] = np.cos(np.pi * steps)
    inverse = np.concatenate([real_back, imag_back]).T / STEPS * (DECAY**-steps)[:, None]
    eye = np.eye(SHEET)
    return halves(np.kron(forward, eye)), halves(np.kron(inverse, eye))


def trace_rows():
    pick = np.zeros((6 * LANES, NB), np.float32)
    for face in range(6):
        for lane in range(NFT):
            field, first, second = lane // 16, lane // 4 % 4, lane % 4
            place = [first, second]
            place.insert(face // 2, 0 if face % 2 == 0 else 3)
            pick[face * LANES + lane, field * 64 + place[0] * 16 + place[1] * 4 + place[2]] = 1.0
    return pick.astype(ml_dtypes.bfloat16)


def split(values):
    high = values.astype(BF16)
    low = (values - high.astype(F32)).astype(BF16)
    return high, low


def dot(a, b, dims):
    return lax.dot_general(a, b, dims, preferred_element_type=F32)


def dot3(a, b, dims):
    return dot(a[0], b[0], dims) + (dot(a[0], b[1], dims) + dot(a[1], b[0], dims))


def arrange_kernel(place, chain, nbr, material, rhs, sent, order, sheet_material):
    mine = place[1]

    def upper(slab, element):
        return chain[slab * 8 + lax.shift_right_logical(element, 7), element & 127] & 511

    element = chain[2, 0] & 255
    origin = element
    for slab in range(SLABS - 1):
        label = upper(slab, upper(slab, element) & 255) & 127
        element = chain[(slab + 1) * 8 + 2, label] & 255
        origin = jnp.where(mine == slab + 1, element, origin)

    def across(face, at):
        return nbr[face, at] & 255

    column = [origin]
    for _ in range(15):
        column.append(across(5, column[-1]))
    rows = [column]
    for _ in range(7):
        rows.append([across(3, at) for at in rows[-1]])
    layers = [rows, [[across(1, at) for at in row] for row in rows]]

    sub = lax.broadcasted_iota(jnp.int32, (8, LANES), 0)
    lane = lax.broadcasted_iota(jnp.int32, (8, LANES), 1)
    for device in range(16):
        sheet = SHEET_OF[device]
        low, high = [], []
        for layer in range(2):
            at = jnp.zeros((8, LANES), jnp.int32)
            for row in range(8):
                at = jnp.where(sub == row, layers[layer][row][sheet], at)
            low.append(jnp.where(lane == at, 1.0, 0.0).astype(F32))
            high.append(jnp.where(lane + LANES == at, 1.0, 0.0).astype(F32))
        order[device * 16 : device * 16 + 16, :LANES] = jnp.concatenate(low).astype(BF16)
        order[device * 16 : device * 16 + 16, LANES:] = jnp.concatenate(high).astype(BF16)

    own = order[pl.ds(pl.multiple_of(place[0] * 16, 16), 16), :].astype(F32)
    column_sum = jnp.sum(own * material[...], axis=1, keepdims=True)
    sheet_material[...] = jnp.broadcast_to(column_sum, (16, LANES))
    picks = order[...]
    for step in range(2):
        high, low = split(rhs[step])
        placed = dot(picks, high, NT) + dot(picks, low, NT)
        sent[:, step * 16 : step * 16 + 16, :] = placed.reshape(16, 16, NB)


def prepare_kernel(
    modes_in, modes_out, face_lift, rates, sheet_material, pick,
    in_h, in_l, out_h, out_l, trace_h, trace_l, lift_h, lift_l, same_r, same_i, cross, lift,
):
    in_parts = split(modes_in[...])
    in_h[...], in_l[...] = in_parts
    out_parts = split(modes_out[...])
    out_h[...], out_l[...] = out_parts
    trace_h[...] = dot(pick[...], out_parts[0], NN).astype(BF16)
    trace_l[...] = dot(pick[...], out_parts[1], NN).astype(BF16)
    lift[...] = jnp.zeros_like(lift)
    for face in range(6):
        lift[:, face * LANES : face * LANES + NFT] = face_lift[face]
    lifted = split(dot3(in_parts, split(lift[...]), NN))
    lift_h[...], lift_l[...] = lifted
    for freq in range(16):
        angle = 2.0 * math.pi / STEPS * freq
        rows = slice(freq * 16, freq * 16 + 16)
        own = sheet_material[:, :1]
        real = (1.0 - DECAY * math.cos(angle)) * own + rates[...]
        imag = jnp.broadcast_to((DECAY * math.sin(angle) if freq else 0.0) * own, (16, NB))
        size = real * real + imag * imag
        same = real / size
        same_r[rows, :] = same
        same_i[rows, :] = same if freq else 1.0 / ((1.0 + DECAY) * own + rates[...])
        cross[rows, :] = imag / size


def divided(modal, same_r, same_i, cross):
    real, imag = modal[:HALF], modal[HALF:]
    mixed = cross[...]
    return jnp.concatenate(
        [real * same_r[...] + imag * mixed, imag * same_i[...] - real * mixed]
    )


def send_traces(place, traces, inner, to_chip, to_next, to_even, to_odd):
    core_low = place[0] & 1 == 0
    slab_even = place[1] & 1 == 0
    inner[...] = traces[:, : 4 * LANES]
    below, above = traces[:, 4 * LANES : 5 * LANES], traces[:, 5 * LANES :]
    to_chip[...] = jnp.where(core_low, above, below)
    to_next[...] = jnp.where(core_low, below, above)
    sides = traces[:, : 2 * LANES].reshape(STEPS, 2, 8, 2 * LANES)
    lower = sides[:, 0, :, :LANES].reshape(HALF, LANES)
    upper = sides[:, 1, :, LANES:].reshape(HALF, LANES)
    to_even[...] = jnp.where(slab_even, upper, lower)
    to_odd[...] = jnp.where(slab_even, lower, upper)


def first_kernel(
    place, steps, forward_h, forward_l, in_h, in_l, trace_h, trace_l, same_r, same_i, cross,
    modal, inner, to_chip, to_next, to_even, to_odd,
):
    spectrum = dot3((forward_h[...], forward_l[...]), split(steps[...]), NN)
    start = dot3(split(spectrum), (in_h[...], in_l[...]), NT)
    modal[...] = start
    solved = split(divided(start, same_r, same_i, cross))
    traces = dot3(solved, (trace_h[...], trace_l[...]), NT)
    send_traces(place, traces, inner, to_chip, to_next, to_even, to_odd)


def gathered(place, inner, from_chip, from_next, from_even, from_odd):
    core_low = place[0] & 1 == 0
    slab_even = place[1] & 1 == 0

    def face(which):
        return inner[:, which * LANES : which * LANES + LANES]

    below = jnp.where(slab_even, from_odd[...], from_even[...]).reshape(STEPS, 1, 8, LANES)
    above = jnp.where(slab_even, from_even[...], from_odd[...]).reshape(STEPS, 1, 8, LANES)
    first = face(0).reshape(STEPS, 2, 8, LANES)
    second = face(1).reshape(STEPS, 2, 8, LANES)
    minus_x = jnp.concatenate([below, second[:, :1]], axis=1).reshape(ROWS, LANES)
    plus_x = jnp.concatenate([first[:, 1:], above], axis=1).reshape(ROWS, LANES)
    minus_y = pltpu.roll(face(3).reshape(ROWS // 8, 8, LANES), 1, 1).reshape(ROWS, LANES)
    plus_y = pltpu.roll(face(2).reshape(ROWS // 8, 8, LANES), 7, 1).reshape(ROWS, LANES)
    minus_z = jnp.where(core_low, from_next[...], from_chip[...])
    plus_z = jnp.where(core_low, from_chip[...], from_next[...])
    return jnp.concatenate([minus_x, plus_x, minus_y, plus_y, minus_z, plus_z], axis=1)


def sweep_kernel(
    place, modal, inner, from_chip, from_next, from_even, from_odd,
    lift_h, lift_l, trace_h, trace_l, same_r, same_i, cross,
    inner_out, to_chip, to_next, to_even, to_odd,
):
    faces = split(gathered(place, inner, from_chip, from_next, from_even, from_odd))
    corrected = modal[...] - dot3(faces, (lift_h[...], lift_l[...]), NT)
    solved = split(divided(corrected, same_r, same_i, cross))
    traces = dot3(solved, (trace_h[...], trace_l[...]), NT)
    send_traces(place, traces, inner_out, to_chip, to_next, to_even, to_odd)


def last_kernel(
    place, modal, inner, from_chip, from_next, from_even, from_odd,
    lift_h, lift_l, out_h, out_l, same_r, same_i, cross, inverse_h, inverse_l,
    steps,
):
    faces = split(gathered(place, inner, from_chip, from_next, from_even, from_odd))
    corrected = modal[...] - dot3(faces, (lift_h[...], lift_l[...]), NT)
    solved = split(divided(corrected, same_r, same_i, cross))
    nodal = split(dot3(solved, (out_h[...], out_l[...]), NT))
    steps[...] = dot3((inverse_h[...], inverse_l[...]), nodal, NN)


def restore_kernel(arrived, order, out):
    for step in range(2):
        values = arrived[:, step * 16 : step * 16 + 16, :].reshape(SLAB, NB)
        high, low = split(values)
        picks = order[...]
        out[step] = dot(high, picks, TN) + dot(low, picks, TN)


SMEM = pl.BlockSpec(memory_space=pltpu.SMEM)
VMEM = pl.BlockSpec(memory_space=pltpu.VMEM)


def call(body, outs, scalars, arrays, flops, scratch=()):
    shapes = [jax.ShapeDtypeStruct(shape, kind) for shape, kind in outs]
    moved = sum(math.prod(s) * jnp.dtype(k).itemsize for s, k in outs)
    moved += sum(a.size * a.dtype.itemsize for a in arrays)
    return pl.pallas_call(
        body,
        out_shape=shapes,
        in_specs=[SMEM] * len(scalars) + [VMEM] * len(arrays),
        out_specs=[VMEM] * len(shapes),
        scratch_shapes=list(scratch),
        compiler_params=pltpu.CompilerParams(vmem_limit_bytes=40 * 2**20),
        cost_estimate=pl.CostEstimate(flops=flops, bytes_accessed=moved, transcendentals=0),
    )(*scalars, *arrays)


def shards(rhs, material, modal_rates, modes_in, modes_out, face_lift, neighbours, halo_send):
    (forward_h, forward_l), (inverse_h, inverse_l) = transform_tables()
    pick = trace_rows()
    place = jnp.stack([lax.axis_index("tm"), lax.axis_index("space")]).astype(jnp.int32)

    table = jnp.concatenate(
        [neighbours[1].reshape(2, LANES), halo_send, jnp.zeros((4, LANES), jnp.int32)]
    )
    chain = lax.all_to_all(
        jnp.broadcast_to(table, (SLABS, 8, LANES)), "space", 0, 0, tiled=True
    ).reshape(SLABS * 8, LANES)

    sent, order, sheet_material = call(
        arrange_kernel,
        [((16, 32, NB), F32), ((SLAB, SLAB), BF16), ((16, LANES), F32)],
        [place, chain, neighbours],
        [material.reshape(1, SLAB), rhs],
        2 * 4 * 256 * 256 * 384,
    )
    arrived = lax.all_to_all(sent, "tm", 0, 0, tiled=True).reshape(ROWS, NB)
    square = [((NB, NB), BF16)] * 4
    in_h, in_l, out_h, out_l, trace_h, trace_l, lift_h, lift_l, same_r, same_i, cross = call(
        prepare_kernel,
        square + [((6 * LANES, NB), BF16)] * 2 + [((NB, 6 * LANES), BF16)] * 2 + [((HALF, NB), F32)] * 3,
        [],
        [modes_in, modes_out, face_lift, modal_rates.reshape(1, NB), sheet_material, jnp.asarray(pick)],
        2 * 5 * 384 * 384 * 768,
        [pltpu.VMEM((NB, 6 * LANES), F32)],
    )

    halo = [((ROWS, 4 * LANES), F32)] + [((ROWS, LANES), F32)] * 2 + [((HALF, LANES), F32)] * 2

    def exchange(to_chip, to_next, to_even, to_odd):
        return [
            lax.ppermute(to_chip, "tm", SAME_CHIP),
            lax.ppermute(to_next, "tm", NEXT_CHIP),
            lax.ppermute(to_even, "space", EVEN_SIDES),
            lax.ppermute(to_odd, "space", ODD_SIDES),
        ]

    coefficients = [same_r, same_i, cross]
    modal, inner, *outgoing = call(
        first_kernel,
        [((ROWS, NB), F32)] + halo,
        [place],
        [arrived, jnp.asarray(forward_h), jnp.asarray(forward_l), in_h, in_l, trace_h, trace_l] + coefficients,
        2 * 3 * 512 * 384 * (512 + 384 + 768),
    )
    incoming = exchange(*outgoing)
    inner, *outgoing = call(
        sweep_kernel,
        halo,
        [place],
        [modal, inner, *incoming, lift_h, lift_l, trace_h, trace_l] + coefficients,
        2 * 3 * 512 * 384 * (768 + 768),
    )
    incoming = exchange(*outgoing)
    (steps,) = call(
        last_kernel,
        [((ROWS, NB), F32)],
        [place],
        [modal, inner, *incoming, lift_h, lift_l, out_h, out_l]
        + coefficients
        + [jnp.asarray(inverse_h), jnp.asarray(inverse_l)],
        2 * 3 * 512 * 384 * (768 + 512 + 384),
    )
    back = lax.all_to_all(steps.reshape(16, 32, NB), "tm", 0, 0, tiled=True)
    (out,) = call(
        restore_kernel, [((2, NB, SLAB), F32)], [], [back, order], 2 * 4 * 256 * 256 * 384
    )
    return out


def solution(mesh):
    return jax.shard_map(
        shards,
        mesh=mesh,
        in_specs=(
            P("tm", None, "space"),
            P("space"),
            P(),
            P(),
            P(),
            P(),
            P(None, "space"),
            P(None, "space"),
        ),
        out_specs=P("tm", None, "space"),
        check_vma=False,
    )
```

time: 440 us -> 107 us (0.24); the launches traced: 432 us -> 105 us
  waiting for transfers between devices: 191 us -> 17 us
  matrix products: 69 us -> 0 us
  local copies, waits for them, and re-layouts: 85.9 us -> 22.3 us
  other arithmetic: 57.6 us -> 0.82 us
  blocking collectives: 0 us -> 19.8 us
  Pallas kernels: 0 us -> 18.5 us
    ppermute x12 -> x8, waiting for transfers between devices: 191 us -> 9.59 us  [the longest x2 9.58 us: exchange(): lax.ppermute(to_even, 'space', EVEN_SIDES)]
    dot_general x16 -> x0, matrix products: 69 us -> none  [the longest x8 26.6 us: precise_einsum(): return jnp.einsum(pattern, table, values, precision=lax.Precision.HIGHEST)]
    gather x16 -> x0, local copies, waits for them, and re-layouts: 37.8 us -> none  [the longest x12 29.6 us: face_coupling(): gathered.append(jnp.take(source, neighbours[which_face], axis=3))]
    another operation x12 -> x0, local copies, waits for them, and re-layouts: 22 us -> none  [face_trace(): return face_piece.reshape(leading + (FIELDS * NP * NP, unknowns.shape[-1]))]
    all_to_all x0 -> x1, blocking collectives: none -> 19.8 us  [shards(): back = lax.all_to_all(steps.reshape(16, 32, NB), 'tm', 0, 0, tiled=True)]
    pallas_call x0 -> x6, Pallas kernels: none -> 18.5 us  [call(): pl.pallas_call(body, out_shape=shapes, in_specs=[SMEM] * len(scalars) + [...]
    unnamed x88 -> x67, local copies, waits for them, and re-layouts: 2.88 us -> 20.9 us
    select_n x14 -> x0, other arithmetic: 15.6 us -> none  [the longest x3 7.43 us: shards(): jnp.where(upper_half, diff_real * twiddle_sin + diff_imag * twiddle_cos,...]
  transfers between devices with their start and end apart: 12 -> 10, of which waited for: 8 -> 4; matrix products, arithmetic and copies ran while one was open for 14% -> 0% of each run, Pallas kernels for 0% -> 2%
where the time goes in v1:
time: 107 us; the launch traced here: 105 us
  starting transfers between devices  26.5 us (25%)
  local copies, waits for them, and re-layouts  22.3 us (21%)
  blocking collectives  19.8 us (19%)
  Pallas kernels  18.5 us (17%)
  waiting for transfers between devices  17 us (16%)
    unnamed x67, local copies, waits for them, and re-layouts  20.9 us
    all_to_all x1, blocking collectives, shards(): back = lax.all_to_all(steps.reshape(16, 32, NB), 'tm', 0, 0, tiled=True)  19.8 us
    pallas_call x6, Pallas kernels, call(): pl.pallas_call(body, out_shape=shapes, in_specs=[SMEM] * len(scalars) + [...  18.5 us
    ppermute x2, starting transfers between devices, exchange(): lax.ppermute(to_odd, 'space', ODD_SIDES)  9.64 us
    ppermute x2, waiting for transfers between devices, exchange(): lax.ppermute(to_even, 'space', EVEN_SIDES)  9.58 us
    all_to_all x1, starting transfers between devices, shards(): arrived = lax.all_to_all(sent, 'tm', 0, 0, tiled=True).reshape(ROWS, NB)  7.75 us
    all_to_all x1, starting transfers between devices, shards(): lax.all_to_all(jnp.broadcast_to(table, (SLABS, 8, LANES)), 'space', 0, 0,...  5.82 us
    all_to_all x1, waiting for transfers between devices, shards(): lax.all_to_all(jnp.broadcast_to(table, (SLABS, 8, LANES)), 'space', 0, 0,...  3.87 us
  transfers between devices with their start and end apart: 10, of which 4 were waited for; matrix products, arithmetic and copies ran while one was open for 0% of the time, Pallas kernels for 2%

profile of v1, /device:TPU:4, one launch (start us, length us, event | category | flops | bytes accessed | tf_op | source)
XLA Modules:
  0.0 105.2 jit_solution(8117651155550379324)
XLA Ops:
  2.1 5.8 %all-to-all-start = ((s32[8,8,128]{2,1,0:T(8,128)}), s32[8,8,128]{2,1,0:T(8,128)S(1)}, u32[]{:S(2)}, u32[]{:S(2)}) async-start(s32[8,8,128]{2,1,0:T(8,128)} %broadcast_in_dim.7), calls=%async_computation | async-start | bytes 65536 | tf_op jit(solution)/shard_map/all_to_all | solution.py:273
  8.0 3.9 %all-to-all-done = s32[8,8,128]{2,1,0:T(8,128)S(1)} async-done(((s32[8,8,128]{2,1,0:T(8,128)}), s32[8,8,128]{2,1,0:T(8,128)S(1)}, u32[]{:S(2)}, u32[]{:S(2)}) %all-to-all-start) | async-done | bytes 32800 | tf_op jit(solution)/shard_map/all_to_all | solution.py:273
  11.9 1.1 %copy-done = f32[2,384,256]{2,1,0:T(8,128)S(1)} copy-done((f32[2,384,256]{2,1,0:T(8,128)S(1)}, f32[2,384,256]{2,1,0:T(8,128)}, u32[]{:S(2)}) %copy-start) | copy-done | bytes 786456
  14.4 3.0 %shard_map.127 = (f32[16,32,384]{2,1,0:T(8,128)}, bf16[256,256]{1,0:T(8,128)(2,1)S(1)}, f32[16,128]{1,0:T(8,128)S(1)}) custom-call(s32[2]{0:T(128)S(1)} %pad_add_fusion.place, s32[64,128]{1,0:T(8,128)S(1)} %bitcast.9, s32[6,256]{1,0:T(8,128)S(1)} %copy-done.14, f32[1,256]{1,0:T(1,128)S(1)} %bitcast.10, f32[2,384,256]{2,1,0:T(8,128)S(1)} %copy-done), custom_call_target="tpu_custom_call" | custom-call | flops 201326592 | bytes 1713152 | tf_op jit(solution)/shard_map/pallas_call | solution.py:254
  18.1 7.8 %all-to-all-start.1 = ((f32[16,32,384]{2,1,0:T(8,128)}), f32[16,32,384]{2,1,0:T(8,128)S(1)}, u32[]{:S(2)}, u32[]{:S(2)}) async-start(f32[16,32,384]{2,1,0:T(8,128)} %get-tuple-element.30), calls=%async_computation.1 | async-start | bytes 1572864 | tf_op jit(solution)/shard_map/all_to_all | solution.py:284
  26.3 1.1 %copy-done.16 = f32[384,384]{1,0:T(8,128)S(1)} copy-done((f32[384,384]{1,0:T(8,128)S(1)}, f32[384,384]{1,0:T(8,128)}, u32[]{:S(2)}) %copy-start.16) | copy-done | bytes 589848
  27.3 1.1 %copy-done.17 = f32[384,384]{1,0:T(8,128)S(1)} copy-done((f32[384,384]{1,0:T(8,128)S(1)}, f32[384,384]{1,0:T(8,128)}, u32[]{:S(2)}) %copy-start.17) | copy-done | bytes 589848
  28.4 1.1 %copy-done.18 = bf16[768,384]{1,0:T(8,128)(2,1)S(1)} copy-done((bf16[768,384]{1,0:T(8,128)(2,1)S(1)}, bf16[768,384]{1,0:T(8,128)(2,1)}, u32[]{:S(2)}) %copy-start.18) | copy-done | bytes 589848
  29.5 2.0 %shard_map.128 = (bf16[384,384]{1,0:T(8,128)(2,1)S(1)}, bf16[384,384]{1,0:T(8,128)(2,1)S(1)}, bf16[384,384]{1,0:T(8,128)(2,1)S(1)}, bf16[384,384]{1,0:T(8,128)(2...) custom-call(f32[384,384]{1,0:T(8,128)S(1)} %copy-done.16, ...), custom_call_target="tpu_custom_call" | custom-call | flops 1132462080 | bytes 7382528 | tf_op jit(solution)/shard_map/pallas_call | solution.py:254
  32.2 0.8 copy-done.5
  34.4 0.8 copy-done.21
  35.2 0.8 copy-done.24
  37.5 3.5 %all-to-all-done.1 = f32[16,32,384]{2,1,0:T(8,128)S(1)} async-done(((f32[16,32,384]{2,1,0:T(8,128)}), f32[16,32,384]{2,1,0:T(8,128)S(1)}, u32[]{:S(2)}, u32[]{:S(2)}) %all-to-all-start.1) | async-done | bytes 786464 | tf_op jit(solution)/shard_map/all_to_all | solution.py:284
  41.0 1.0 copy-done.4
  42.0 1.0 copy-done.6
  43.0 1.0 copy-done.19
  44.1 1.0 copy-done.20
  45.1 1.1 %copy-done.22 = bf16[768,384]{1,0:T(8,128)(2,1)S(1)} copy-done((bf16[768,384]{1,0:T(8,128)(2,1)S(1)}, bf16[768,384]{1,0:T(8,128)(2,1)}, u32[]{:S(2)}) %copy-start.22) | copy-done | bytes 589848
  46.2 1.1 %copy-done.25 = bf16[768,384]{1,0:T(8,128)(2,1)S(1)} copy-done((bf16[768,384]{1,0:T(8,128)(2,1)S(1)}, bf16[768,384]{1,0:T(8,128)(2,1)}, u32[]{:S(2)}) %copy-start.25) | copy-done | bytes 589848
  47.2 1.0 copy-done.28
  48.2 1.0 copy-done.30
  49.2 4.4 %shard_map.129 = (f32[512,384]{1,0:T(8,128)S(1)}, f32[512,512]{1,0:T(8,128)S(1)}, f32[512,128]{1,0:T(8,128)S(1)}, f32[512,128]{1,0:T(8,128)S(1)}, f32[256,128]{1,0:T(8,128)S(1)}, /*index=5*/f32[256,128]{1,0:T(8,128)S(1)}) custom-call(s32[2]{0:T(128)S(1)} %pad_add_fusion.place, f32[512,384]{1,0:T(8,128)S(1)} %bitcast.8, bf16[512,512]{1,0:T(8,128)(2,1)S(1)} %copy-done.20, ...), custom_call_target="tpu_custom_call" | custom-call | flops 1962934272 | bytes 7405568 | tf_op jit(solution)/shard_map/pallas_call | solution.py:254
  53.7 0.9 collective-permute-start.1
  54.6 4.7 %collective-permute-start.3 = (f32[256,128]{1,0:T(8,128)S(1)}, f32[256,128]{1,0:T(8,128)S(1)}, u32[]{:S(2)}, u32[]{:S(2)}) collective-permute-start(f32[256,128]{1,0:T(8,128)S(1)} %get-tuple-element.44), channel_id=1, source_target_pairs={{1,2},{2,1},{3,4},{4,3},{5,6},{6,5},{9,10},{10,9},{11,12},{12,11},... | collective-permute-start | bytes 393224 | tf_op jit(solution)/shard_map/ppermute | solution.py:302
  59.3 5.1 %collective-permute-done.2.from_even = f32[256,128]{1,0:T(8,128)S(1)} collective-permute-done((f32[256,128]{1,0:T(8,128)S(1)}, f32[256,128]{1,0:T(8,128)S(1)}, u32[]{:S(2)}, u32[]{:S(2)}) %collective-permute-start.2) | collective-permute-done | bytes 131104 | tf_op jit(solution)/shard_map/ppermute | solution.py:301
  64.6 3.9 %shard_map.130 = (f32[512,512]{1,0:T(8,128)S(1)}, f32[512,128]{1,0:T(8,128)S(1)}, f32[512,128]{1,0:T(8,128)S(1)}, f32[256,128]{1,0:T(8,128)S(1)}, f32[256,128]{1,0:T(8,128)S(1)}) custom-call(s32[2]{0:T(128)S(1)} %pad_add_fusion.place, f32[512,384]{1,0:T(8,128)S(1)} %get-tuple-element.39.modal, f32[512,512]{1,0:T(8,128)S(1)} %get-tuple-element.40.inner, ...), custom_call_target="tpu_custom_call" | custom-call | flops 1811939328 | bytes 7995392 | tf_op jit(solution)/shard_map/pallas_call | solution.py:254
  68.6 2.2 %collective-permute-start.5 = (f32[512,128]{1,0:T(8,128)S(1)}, f32[512,128]{1,0:T(8,128)S(1)}, u32[]{:S(2)}, u32[]{:S(2)}) collective-permute-start(f32[512,128]{1,0:T(8,128)S(1)} %get-tuple-element.49), channel_id=1, source_target_pairs={{8,32},{40,64},{72,96},{104,112},{120,80},{88,48},{56,16},{24,0},{... | collective-permute-start | bytes 786440 | tf_op jit(solution)/shard_map/ppermute | solution.py:300
  70.7 4.9 %collective-permute-start.7 = (f32[256,128]{1,0:T(8,128)S(1)}, f32[256,128]{1,0:T(8,128)S(1)}, u32[]{:S(2)}, u32[]{:S(2)}) collective-permute-start(f32[256,128]{1,0:T(8,128)S(1)} %get-tuple-element.51), channel_id=1, source_target_pairs={{1,2},{2,1},{3,4},{4,3},{5,6},{6,5},{9,10},{10,9},{11,12},{12,11},... | collective-permute-start | bytes 393224 | tf_op jit(solution)/shard_map/ppermute | solution.py:302
  75.6 4.4 %collective-permute-done.6.from_even = f32[256,128]{1,0:T(8,128)S(1)} collective-permute-done((f32[256,128]{1,0:T(8,128)S(1)}, f32[256,128]{1,0:T(8,128)S(1)}, u32[]{:S(2)}, u32[]{:S(2)}) %collective-permute-start.6) | collective-permute-done | bytes 131104 | tf_op jit(solution)/shard_map/ppermute | solution.py:301
  80.1 3.9 %shard_map.131 = f32[512,384]{1,0:T(8,128)S(1)} custom-call(s32[2]{0:T(128)S(1)} %pad_add_fusion.place, f32[512,384]{1,0:T(8,128)S(1)} %get-tuple-element.39.modal, f32[512,512]{1,0:T(8,128)S(1)} %get-tuple-element.47.inner, f32[512,128]{1,0:T(8,128)S(1)} %collective-permute-done.4.from_chip, f32[512,128]{1,0:T(8,128)S(1)} %collective-permute-done.5.from_next, ...), custom_call_target="tpu_custom_call" | custom-call | flops 1962934272 | bytes 7405568 | tf_op jit(solution)/shard_map/pallas_call | solution.py:254
  84.1 19.8 %all_to_all.15.arrived = f32[16,32,384]{2,1,0:T(8,128)S(1)} all-to-all(f32[16,32,384]{2,1,0:T(8,128)S(1)} %bitcast.7), channel_id=1, replica_groups=mesh['tm'=16,'space'=8] {'tm'}, dimensions={0} | all-to-all | bytes 1572864 | tf_op jit(solution)/shard_map/all_to_all | solution.py:331
  103.9 1.3 %shard_map.132 = f32[2,384,256]{2,1,0:T(8,128)} custom-call(f32[16,32,384]{2,1,0:T(8,128)S(1)} %all_to_all.15.arrived, bf16[256,256]{1,0:T(8,128)(2,1)S(1)} %copy-done.13), custom_call_target="tpu_custom_call" | custom-call | flops 201326592 | bytes 1703936 | tf_op jit(solution)/shard_map/pallas_call | solution.py:254
  (69 shorter events, 8.5 us)
Async XLA Ops:
  2.1 9.8 %all-to-all-start = ((s32[8,8,128]{2,1,0:T(8,128)}), s32[8,8,128]{2,1,0:T(8,128)S(1)}, u32[]{:S(2)}, u32[]{:S(2)}) async-start(s32[8,8,128]{2,1,0:T(8,128)} %broadcast_in_dim.7), calls=%async_computation | async-start | bytes 65536 | tf_op jit(solution)/shard_map/all_to_all | solution.py:273
  11.9 1.1 %copy-start = (f32[2,384,256]{2,1,0:T(8,128)S(1)}, f32[2,384,256]{2,1,0:T(8,128)}, u32[]{:S(2)}) copy-start(f32[2,384,256]{2,1,0:T(8,128)} %rhs.1) | copy-start | bytes 2359300
  14.4 11.4 %copy-start.32 = (f32[384]{0:T(512)S(1)}, f32[384]{0:T(512)}, u32[]{:S(2)}) copy-start(f32[384]{0:T(512)} %param.15) | copy-start | bytes 4612
  14.4 11.5 %copy-start.31 = (f32[6,384,96]{1,2,0:T(8,128)S(1)}, f32[6,384,96]{1,2,0:T(8,128)}, u32[]{:S(2)}) copy-start(f32[6,384,96]{1,2,0:T(8,128)} %param.18) | copy-start | bytes 2654212
  18.1 22.9 %all-to-all-start.1 = ((f32[16,32,384]{2,1,0:T(8,128)}), f32[16,32,384]{2,1,0:T(8,128)S(1)}, u32[]{:S(2)}, u32[]{:S(2)}) async-start(f32[16,32,384]{2,1,0:T(8,128)} %get-tuple-element.30), calls=%async_computation.1 | async-start | bytes 1572864 | tf_op jit(solution)/shard_map/all_to_all | solution.py:284
  26.3 1.1 %copy-start.16 = (f32[384,384]{1,0:T(8,128)S(1)}, f32[384,384]{1,0:T(8,128)}, u32[]{:S(2)}) copy-start(f32[384,384]{1,0:T(8,128)} %modes_in.1) | copy-start | bytes 1769476
  27.3 1.1 %copy-start.17 = (f32[384,384]{1,0:T(8,128)S(1)}, f32[384,384]{1,0:T(8,128)}, u32[]{:S(2)}) copy-start(f32[384,384]{1,0:T(8,128)} %modes_out.1) | copy-start | bytes 1769476
  28.4 1.1 %copy-start.18 = (bf16[768,384]{1,0:T(8,128)(2,1)S(1)}, bf16[768,384]{1,0:T(8,128)(2,1)}, u32[]{:S(2)}) copy-start(bf16[768,384]{1,0:T(8,128)(2,1)} %constant.21.clone.pick) | copy-start | bytes 1769476
  41.0 1.0 copy-start.4
  42.0 1.0 copy-start.6
  43.0 1.0 copy-start.19
  44.1 1.0 copy-start.20
  45.1 1.1 %copy-start.22 = (bf16[768,384]{1,0:T(8,128)(2,1)S(1)}, bf16[768,384]{1,0:T(8,128)(2,1)}, u32[]{:S(2)}) copy-start(bf16[768,384]{1,0:T(8,128)(2,1)} %copy-done.21) | copy-start | bytes 1769476
  46.2 1.1 %copy-start.25 = (bf16[768,384]{1,0:T(8,128)(2,1)S(1)}, bf16[768,384]{1,0:T(8,128)(2,1)}, u32[]{:S(2)}) copy-start(bf16[768,384]{1,0:T(8,128)(2,1)} %copy-done.24) | copy-start | bytes 1769476
  47.2 1.0 copy-start.28
  48.2 1.0 copy-start.30
  49.2 15.3 %copy-start.7 = (f32[256,384]{1,0:T(8,128)S(1)}, f32[256,384]{1,0:T(8,128)}, u32[]{:S(2)}) copy-start(f32[256,384]{1,0:T(8,128)} %copy-done.5) | copy-start | bytes 1179652
  49.2 15.3 %copy-start.23 = (bf16[768,384]{1,0:T(8,128)(2,1)S(1)}, bf16[768,384]{1,0:T(8,128)(2,1)}, u32[]{:S(2)}) copy-start(bf16[768,384]{1,0:T(8,128)(2,1)} %copy-done.21) | copy-start | bytes 1769476
  49.2 15.3 %copy-start.26 = (bf16[768,384]{1,0:T(8,128)(2,1)S(1)}, bf16[768,384]{1,0:T(8,128)(2,1)}, u32[]{:S(2)}) copy-start(bf16[768,384]{1,0:T(8,128)(2,1)} %copy-done.24) | copy-start | bytes 1769476
  53.6 10.9 %collective-permute-start = (f32[512,128]{1,0:T(8,128)S(1)}, f32[512,128]{1,0:T(8,128)S(1)}, u32[]{:S(2)}, u32[]{:S(2)}) collective-permute-start(f32[512,128]{1,0:T(8,128)S(1)} %get-tuple-element.41), channel_id=1, source_target_pairs={{0,8},{8,0},{16,24},{24,16},{32,40},{40,32},{48,56},{56,48},{64,72... | collective-permute-start | bytes 786440 | tf_op jit(solution)/shard_map/ppermute | solution.py:299
  53.7 10.8 %collective-permute-start.1 = (f32[512,128]{1,0:T(8,128)S(1)}, f32[512,128]{1,0:T(8,128)S(1)}, u32[]{:S(2)}, u32[]{:S(2)}) collective-permute-start(f32[512,128]{1,0:T(8,128)S(1)} %get-tuple-element.42), channel_id=1, source_target_pairs={{8,32},{40,64},{72,96},{104,112},{120,80},{88,48},{56,16},{24,0},{... | collective-permute-start | bytes 786440 | tf_op jit(solution)/shard_map/ppermute | solution.py:300
  54.6 9.9 %collective-permute-start.2 = (f32[256,128]{1,0:T(8,128)S(1)}, f32[256,128]{1,0:T(8,128)S(1)}, u32[]{:S(2)}, u32[]{:S(2)}) collective-permute-start(f32[256,128]{1,0:T(8,128)S(1)} %get-tuple-element.43), channel_id=1, source_target_pairs={{0,1},{1,0},{2,3},{3,2},{4,5},{5,4},{6,7},{7,6},{8,9},{9,8},{10,11... | collective-permute-start | bytes 393224 | tf_op jit(solution)/shard_map/ppermute | solution.py:301
  54.6 9.9 %collective-permute-start.3 = (f32[256,128]{1,0:T(8,128)S(1)}, f32[256,128]{1,0:T(8,128)S(1)}, u32[]{:S(2)}, u32[]{:S(2)}) collective-permute-start(f32[256,128]{1,0:T(8,128)S(1)} %get-tuple-element.44), channel_id=1, source_target_pairs={{1,2},{2,1},{3,4},{4,3},{5,6},{6,5},{9,10},{10,9},{11,12},{12,11},... | collective-permute-start | bytes 393224 | tf_op jit(solution)/shard_map/ppermute | solution.py:302
  64.5 15.6 %copy-start.1 = (bf16[512,512]{1,0:T(8,128)(2,1)S(1)}, bf16[512,512]{1,0:T(8,128)(2,1)}, u32[]{:S(2)}) copy-start(bf16[512,512]{1,0:T(8,128)(2,1)} %constant.25.clone.inverse_l) | copy-start | bytes 1572868
  64.5 15.6 %copy-start.2 = (bf16[512,512]{1,0:T(8,128)(2,1)S(1)}, bf16[512,512]{1,0:T(8,128)(2,1)}, u32[]{:S(2)}) copy-start(bf16[512,512]{1,0:T(8,128)(2,1)} %constant.24.clone.inverse_h) | copy-start | bytes 1572868
  64.5 15.6 %copy-start.9 = (bf16[384,384]{1,0:T(8,128)(2,1)S(1)}, bf16[384,384]{1,0:T(8,128)(2,1)}, u32[]{:S(2)}) copy-start(bf16[384,384]{1,0:T(8,128)(2,1)} %copy-done.8) | copy-start | bytes 884740
  64.6 15.6 %copy-start.11 = (bf16[384,384]{1,0:T(8,128)(2,1)S(1)}, bf16[384,384]{1,0:T(8,128)(2,1)}, u32[]{:S(2)}) copy-start(bf16[384,384]{1,0:T(8,128)(2,1)} %copy-done.10) | copy-start | bytes 884740
  68.5 11.6 %collective-permute-start.4 = (f32[512,128]{1,0:T(8,128)S(1)}, f32[512,128]{1,0:T(8,128)S(1)}, u32[]{:S(2)}, u32[]{:S(2)}) collective-permute-start(f32[512,128]{1,0:T(8,128)S(1)} %get-tuple-element.48), channel_id=1, source_target_pairs={{0,8},{8,0},{16,24},{24,16},{32,40},{40,32},{48,56},{56,48},{64,72... | collective-permute-start | bytes 786440 | tf_op jit(solution)/shard_map/ppermute | solution.py:299
  68.6 11.5 %collective-permute-start.5 = (f32[512,128]{1,0:T(8,128)S(1)}, f32[512,128]{1,0:T(8,128)S(1)}, u32[]{:S(2)}, u32[]{:S(2)}) collective-permute-start(f32[512,128]{1,0:T(8,128)S(1)} %get-tuple-element.49), channel_id=1, source_target_pairs={{8,32},{40,64},{72,96},{104,112},{120,80},{88,48},{56,16},{24,0},{... | collective-permute-start | bytes 786440 | tf_op jit(solution)/shard_map/ppermute | solution.py:300
  70.7 9.4 %collective-permute-start.6 = (f32[256,128]{1,0:T(8,128)S(1)}, f32[256,128]{1,0:T(8,128)S(1)}, u32[]{:S(2)}, u32[]{:S(2)}) collective-permute-start(f32[256,128]{1,0:T(8,128)S(1)} %get-tuple-element.50), channel_id=1, source_target_pairs={{0,1},{1,0},{2,3},{3,2},{4,5},{5,4},{6,7},{7,6},{8,9},{9,8},{10,11... | collective-permute-start | bytes 393224 | tf_op jit(solution)/shard_map/ppermute | solution.py:301
  70.7 9.4 %collective-permute-start.7 = (f32[256,128]{1,0:T(8,128)S(1)}, f32[256,128]{1,0:T(8,128)S(1)}, u32[]{:S(2)}, u32[]{:S(2)}) collective-permute-start(f32[256,128]{1,0:T(8,128)S(1)} %get-tuple-element.51), channel_id=1, source_target_pairs={{1,2},{2,1},{3,4},{4,3},{5,6},{6,5},{9,10},{10,9},{11,12},{12,11},... | collective-permute-start | bytes 393224 | tf_op jit(solution)/shard_map/ppermute | solution.py:302
  84.0 19.8 %copy-start.13 = (bf16[256,256]{1,0:T(8,128)(2,1)S(1)}, bf16[256,256]{1,0:T(8,128)(2,1)}, u32[]{:S(2)}) copy-start(bf16[256,256]{1,0:T(8,128)(2,1)} %copy-done.12) | copy-start | bytes 393220
  (11 other events, 8.1 us)

commit v2 on v1

v2 whole, which is shorter than its diff:
```python
import math

import jax
import jax.numpy as jnp
import ml_dtypes
import numpy as np
from jax import lax
from jax.experimental import pallas as pl
from jax.experimental.pallas import tpu as pltpu
from jax.sharding import PartitionSpec as P

NB = 384
NFT = 96
LANES = 128
STEPS = 32
SLAB = 256
SHEET = 16
ROWS = STEPS * SHEET
HALF = ROWS // 2
SLABS = 8
DECAY = 0.1 ** (1.0 / STEPS)

RING = (0, 1, 4, 5, 8, 9, 12, 13, 14, 15, 10, 11, 6, 7, 2, 3)
SHEET_OF = tuple(RING.index(device) for device in range(16))
SAME_CHIP = [(i, i ^ 1) for i in range(16)]
NEXT_CHIP = [(RING[2 * i + 1], RING[(2 * i + 2) % 16]) for i in range(8)]
NEXT_CHIP = NEXT_CHIP + [(b, a) for a, b in NEXT_CHIP]
EVEN_SIDES = [(i, i ^ 1) for i in range(8)]
ODD_SIDES = [(1, 2), (2, 1), (3, 4), (4, 3), (5, 6), (6, 5)]

F32 = jnp.float32
BF16 = jnp.bfloat16
NN = (((1,), (0,)), ((), ()))
NT = (((1,), (1,)), ((), ()))
TN = (((0,), (0,)), ((), ()))


def real_fft(steps):
    count = len(steps)
    if count == 2:
        return [(steps[0] + steps[1], None), (steps[0] - steps[1], None)]
    even, odd = real_fft(steps[0::2]), real_fft(steps[1::2])
    out = [None] * (count // 2 + 1)
    out[0] = (even[0][0] + odd[0][0], None)
    out[count // 2] = (even[0][0] - odd[0][0], None)
    out[count // 4] = (even[count // 4][0], -odd[count // 4][0])
    for freq in range(1, count // 4):
        cos, sin = math.cos(2.0 * math.pi * freq / count), math.sin(2.0 * math.pi * freq / count)
        real, imag = odd[freq]
        turned_real, turned_imag = real * cos + imag * sin, imag * cos - real * sin
        real, imag = even[freq]
        out[freq] = (real + turned_real, imag + turned_imag)
        out[count // 2 - freq] = (real - turned_real, turned_imag - imag)
    return out


def real_ifft(freqs):
    count = 2 * (len(freqs) - 1)
    first, last = freqs[0][0], freqs[-1][0]
    if count == 2:
        return [first + last, first - last]
    even, odd = [None] * (count // 4 + 1), [None] * (count // 4 + 1)
    even[0], odd[0] = (first + last, None), (first - last, None)
    middle = freqs[count // 4]
    even[-1], odd[-1] = (2.0 * middle[0], None), (-2.0 * middle[1], None)
    for freq in range(1, count // 4):
        cos, sin = math.cos(2.0 * math.pi * freq / count), math.sin(2.0 * math.pi * freq / count)
        (real, imag), (other_real, other_imag) = freqs[freq], freqs[count // 2 - freq]
        even[freq] = (real + other_real, imag - other_imag)
        real, imag = real - other_real, imag + other_imag
        odd[freq] = (real * cos - imag * sin, imag * cos + real * sin)
    out = [None] * count
    out[0::2], out[1::2] = real_ifft(even), real_ifft(odd)
    return out


def tiles():
    for block in range(SHEET // 8):
        for lane in range(0, NB, LANES):
            yield lambda row: (slice(row * SHEET + block * 8, row * SHEET + block * 8 + 8), slice(lane, lane + LANES))


def to_frequencies(steps, spectrum):
    for at in tiles():
        freqs = real_fft([steps[at(n)] * DECAY**n for n in range(STEPS)])
        for freq in range(16):
            spectrum[at(freq)] = freqs[freq][0]
            spectrum[at(16 + freq)] = freqs[freq][1] if freq else freqs[16][0]


def to_steps(spectrum, steps):
    for at in tiles():
        pairs = [(spectrum[at(freq)], spectrum[at(16 + freq)]) for freq in range(16)]
        freqs = [(pairs[0][0], None)] + pairs[1:] + [(pairs[0][1], None)]
        for n, value in enumerate(real_ifft(freqs)):
            steps[at(n)] = value * (DECAY**-n / STEPS)


def trace_rows():
    pick = np.zeros((6 * LANES, NB), np.float32)
    for face in range(6):
        for lane in range(NFT):
            field, first, second = lane // 16, lane // 4 % 4, lane % 4
            place = [first, second]
            place.insert(face // 2, 0 if face % 2 == 0 else 3)
            pick[face * LANES + lane, field * 64 + place[0] * 16 + place[1] * 4 + place[2]] = 1.0
    return pick.astype(ml_dtypes.bfloat16)


def split(values):
    high = values.astype(BF16)
    low = (values - high.astype(F32)).astype(BF16)
    return high, low


def dot(a, b, dims):
    return lax.dot_general(a, b, dims, preferred_element_type=F32)


def dot3(a, b, dims):
    return dot(a[0], b[0], dims) + (dot(a[0], b[1], dims) + dot(a[1], b[0], dims))


def table_kernel(place, nbr, halo, table):
    upper = place[1] >= SLABS // 2
    steps = jnp.where(upper, nbr[1:2, :], nbr[0:1, :])
    labels = jnp.where(upper, halo[0:1, :], halo[1:2, :])
    rows = [steps[:, :LANES], steps[:, LANES:], labels, labels, nbr[1:2, :LANES], nbr[1:2, LANES:], labels, labels]
    packed = jnp.concatenate(rows)
    for member in range(SLABS // 2):
        table[member] = packed


def order_kernel(nbr, halo, rhs, placed, order, spot):
    def across(face, at):
        return nbr[face, at] & 255

    column = [halo[0, 0] & 255]
    for _ in range(15):
        column.append(across(5, column[-1]))
    rows = [column]
    for _ in range(7):
        rows.append([across(3, at) for at in rows[-1]])
    layers = [rows, [[across(1, at) for at in row] for row in rows]]
    for row in range(8):
        for sheet in range(16):
            spot[rows[row][sheet]] = row * 16 + sheet

    sub = lax.broadcasted_iota(jnp.int32, (8, LANES), 0)
    lane = lax.broadcasted_iota(jnp.int32, (8, LANES), 1)
    for sheet in range(16):
        for layer in range(2):
            at = jnp.zeros((8, LANES), jnp.int32)
            for row in range(8):
                at = jnp.where(sub == row, layers[layer][row][sheet], at)
            order[sheet * 2 + layer, :, :LANES] = jnp.where(lane == at, 1.0, 0.0).astype(F32)
            order[sheet * 2 + layer, :, LANES:] = jnp.where(lane + LANES == at, 1.0, 0.0).astype(F32)

    picks = order[...].reshape(SLAB, SLAB).astype(BF16)
    for step in range(2):
        high, low = split(rhs[step])
        values = dot(picks, high, NT) + dot(picks, low, NT)
        placed[step] = values.reshape(32, 8, NB)


def align_kernel(place, chain, spot, tables, placed, sent, shift):
    group = lax.shift_right_logical(place[1], 2)
    member = place[1] & 3

    def step(slab, at):
        return chain[slab * 8 + lax.shift_right_logical(at, 7), at & 127]

    upper_rows = tables[28:30, :]
    index = lax.broadcasted_iota(jnp.int32, (2, LANES), 0) * LANES + lax.broadcasted_iota(jnp.int32, (2, LANES), 1)
    facing = jnp.sum(jnp.where(upper_rows == SLAB, index, 0)) & 255
    near = jnp.where(group == 0, facing, chain[2, 0] & 255)
    origin = near
    for hop in range(4):
        slab = jnp.where(group == 0, 3 - hop, hop)
        far = step(slab, near) & 255
        origin = jnp.where(slab == member, jnp.where(group == 0, far, near), origin)
        if hop < 3:
            label = step(slab, far) & 127
            ahead = jnp.where(group == 0, 2 - hop, hop + 1)
            near = chain[ahead * 8 + 2, label] & 255
    found = spot[origin] & 127
    first_row, first_sheet = lax.shift_right_logical(found, 4), found & 15
    shift[0] = (8 - first_row) & 7
    shift[1] = first_sheet
    for device in range(16):
        sheet = (SHEET_OF[device] + first_sheet) & 15
        for at in range(2):
            values = placed[at, pl.ds(sheet * 2, 2)]
            values = pltpu.roll(values, (8 - first_row) & 7, 1)
            sent[device, at * 16 : at * 16 + 16, :] = values.reshape(16, NB)


def prepare_kernel(
    place, shift, placed_order, material, modes_in, modes_out, face_lift, rates, pick,
    order, in_h, in_l, out_h, out_l, trace_h, trace_l, lift_h, lift_l, same_r, same_i, cross, lift,
):
    for device in range(16):
        sheet = (SHEET_OF[device] + shift[1]) & 15
        picks = pltpu.roll(placed_order[pl.ds(sheet * 2, 2)], shift[0], 1)
        order[device * 16 : device * 16 + 16, :] = picks.reshape(16, SLAB).astype(BF16)
    own_picks = order[pl.ds(pl.multiple_of(place[0] * 16, 16), 16), :].astype(F32)
    own = jnp.sum(own_picks * material[...], axis=1, keepdims=True)
    in_parts = split(modes_in[...])
    in_h[...], in_l[...] = in_parts
    out_parts = split(modes_out[...])
    out_h[...], out_l[...] = out_parts
    trace_h[...] = dot(pick[...], out_parts[0], NN).astype(BF16)
    trace_l[...] = dot(pick[...], out_parts[1], NN).astype(BF16)
    lift[...] = jnp.zeros_like(lift)
    for face in range(6):
        lift[:, face * LANES : face * LANES + NFT] = face_lift[face]
    lifted = split(dot3(in_parts, split(lift[...]), NN))
    lift_h[...], lift_l[...] = lifted
    for freq in range(16):
        angle = 2.0 * math.pi / STEPS * freq
        rows = slice(freq * 16, freq * 16 + 16)
        real = (1.0 - DECAY * math.cos(angle)) * own + rates[...]
        imag = jnp.broadcast_to((DECAY * math.sin(angle) if freq else 0.0) * own, (16, NB))
        size = real * real + imag * imag
        same = real / size
        same_r[rows, :] = same
        same_i[rows, :] = same if freq else 1.0 / ((1.0 + DECAY) * own + rates[...])
        cross[rows, :] = imag / size


def divided(modal, same_r, same_i, cross):
    real, imag = modal[:HALF], modal[HALF:]
    mixed = cross[...]
    return jnp.concatenate(
        [real * same_r[...] + imag * mixed, imag * same_i[...] - real * mixed]
    )


def pack(values):
    quarter = values.shape[0] // 4
    lane = lax.broadcasted_iota(jnp.int32, (quarter, LANES), 1)
    tail = values[3 * quarter :]
    parts = []
    for part in range(3):
        moved = pltpu.roll(tail, NFT - 32 * part, 1)
        parts.append(jnp.where(lane < NFT, values[part * quarter : (part + 1) * quarter], moved))
    return jnp.concatenate(parts)


def unpack(packed):
    quarter = packed.shape[0] // 3
    lane = lax.broadcasted_iota(jnp.int32, (quarter, LANES), 1)
    moved = [pltpu.roll(packed[part * quarter : (part + 1) * quarter], 32 + 32 * part, 1) for part in range(3)]
    tail = jnp.where(lane < 32, moved[0], jnp.where(lane < 64, moved[1], moved[2]))
    return jnp.concatenate([packed, tail])


def send_traces(place, traces, inner, to_chip, to_next, to_even, to_odd):
    core_low = place[0] & 1 == 0
    slab_even = place[1] & 1 == 0
    inner[...] = traces[:, : 4 * LANES]
    below, above = traces[:, 4 * LANES : 5 * LANES], traces[:, 5 * LANES :]
    to_chip[...] = pack(jnp.where(core_low, above, below))
    to_next[...] = pack(jnp.where(core_low, below, above))
    sides = traces[:, : 2 * LANES].reshape(STEPS, 2, 8, 2 * LANES)
    lower = sides[:, 0, :, :LANES].reshape(HALF, LANES)
    upper = sides[:, 1, :, LANES:].reshape(HALF, LANES)
    to_even[...] = pack(jnp.where(slab_even, upper, lower))
    to_odd[...] = pack(jnp.where(slab_even, lower, upper))


def first_kernel(
    place, steps, in_h, in_l, trace_h, trace_l, same_r, same_i, cross,
    modal, inner, to_chip, to_next, to_even, to_odd, spectrum,
):
    to_frequencies(steps, spectrum)
    start = dot3(split(spectrum[...]), (in_h[...], in_l[...]), NT)
    modal[...] = start
    solved = split(divided(start, same_r, same_i, cross))
    traces = dot3(solved, (trace_h[...], trace_l[...]), NT)
    send_traces(place, traces, inner, to_chip, to_next, to_even, to_odd)


def gathered(place, inner, from_chip, from_next, from_even, from_odd):
    core_low = place[0] & 1 == 0
    slab_even = place[1] & 1 == 0

    def face(which):
        return inner[:, which * LANES : which * LANES + LANES]

    below = unpack(jnp.where(slab_even, from_odd[...], from_even[...])).reshape(STEPS, 1, 8, LANES)
    above = unpack(jnp.where(slab_even, from_even[...], from_odd[...])).reshape(STEPS, 1, 8, LANES)
    first = face(0).reshape(STEPS, 2, 8, LANES)
    second = face(1).reshape(STEPS, 2, 8, LANES)
    minus_x = jnp.concatenate([below, second[:, :1]], axis=1).reshape(ROWS, LANES)
    plus_x = jnp.concatenate([first[:, 1:], above], axis=1).reshape(ROWS, LANES)
    minus_y = pltpu.roll(face(3).reshape(ROWS // 8, 8, LANES), 1, 1).reshape(ROWS, LANES)
    plus_y = pltpu.roll(face(2).reshape(ROWS // 8, 8, LANES), 7, 1).reshape(ROWS, LANES)
    minus_z = unpack(jnp.where(core_low, from_next[...], from_chip[...]))
    plus_z = unpack(jnp.where(core_low, from_chip[...], from_next[...]))
    return jnp.concatenate([minus_x, plus_x, minus_y, plus_y, minus_z, plus_z], axis=1)


def sweep_kernel(
    place, modal, inner, from_chip, from_next, from_even, from_odd,
    lift_h, lift_l, trace_h, trace_l, same_r, same_i, cross,
    inner_out, to_chip, to_next, to_even, to_odd,
):
    faces = split(gathered(place, inner, from_chip, from_next, from_even, from_odd))
    corrected = modal[...] - dot3(faces, (lift_h[...], lift_l[...]), NT)
    solved = split(divided(corrected, same_r, same_i, cross))
    traces = dot3(solved, (trace_h[...], trace_l[...]), NT)
    send_traces(place, traces, inner_out, to_chip, to_next, to_even, to_odd)


def last_kernel(
    place, modal, inner, from_chip, from_next, from_even, from_odd,
    lift_h, lift_l, out_h, out_l, same_r, same_i, cross,
    steps, spectrum,
):
    faces = split(gathered(place, inner, from_chip, from_next, from_even, from_odd))
    corrected = modal[...] - dot3(faces, (lift_h[...], lift_l[...]), NT)
    solved = split(divided(corrected, same_r, same_i, cross))
    spectrum[...] = dot3(solved, (out_h[...], out_l[...]), NT)
    to_steps(spectrum, steps)


def restore_kernel(arrived, order, out):
    for step in range(2):
        values = arrived[:, step * 16 : step * 16 + 16, :].reshape(SLAB, NB)
        high, low = split(values)
        picks = order[...]
        out[step] = dot(high, picks, TN) + dot(low, picks, TN)


SMEM = pl.BlockSpec(memory_space=pltpu.SMEM)
VMEM = pl.BlockSpec(memory_space=pltpu.VMEM)


def call(body, outs, scalars, arrays, flops, scratch=(), scalar_outs=(), megabytes=16):
    outs = [jax.ShapeDtypeStruct(shape, kind) for shape, kind in outs]
    scalar_outs = [jax.ShapeDtypeStruct(shape, jnp.int32) for shape in scalar_outs]
    moved = sum(a.size * a.dtype.itemsize for a in [*outs, *arrays])
    return pl.pallas_call(
        body,
        out_shape=outs + scalar_outs,
        in_specs=[SMEM] * len(scalars) + [VMEM] * len(arrays),
        out_specs=[VMEM] * len(outs) + [SMEM] * len(scalar_outs),
        scratch_shapes=list(scratch),
        compiler_params=pltpu.CompilerParams(vmem_limit_bytes=megabytes * 2**20),
        cost_estimate=pl.CostEstimate(flops=flops, bytes_accessed=moved, transcendentals=0),
    )(*scalars, *arrays)


def shards(rhs, material, modal_rates, modes_in, modes_out, face_lift, neighbours, halo_send):
    place = jnp.stack([lax.axis_index("tm"), lax.axis_index("space")]).astype(jnp.int32)
    (table,) = call(table_kernel, [((4, 8, LANES), jnp.int32)], [place], [neighbours, halo_send], 10**4)
    chain = lax.all_to_all(
        table, "space", 0, 0, tiled=True, axis_index_groups=[[0, 1, 2, 3], [4, 5, 6, 7]]
    ).reshape(32, LANES)
    placed, placed_order, spot = call(
        order_kernel,
        [((2, 32, 8, NB), F32), ((32, 8, SLAB), F32)],
        [neighbours, halo_send],
        [rhs],
        2 * 4 * 256 * 256 * 384,
        scalar_outs=[(SLAB,)],
    )
    sent, shift = call(
        align_kernel, [((16, 32, NB), F32)], [place, chain, spot], [chain, placed], 10**6, scalar_outs=[(2,)]
    )
    arrived = lax.all_to_all(sent, "tm", 0, 0, tiled=True).reshape(ROWS, NB)
    order, in_h, in_l, out_h, out_l, trace_h, trace_l, lift_h, lift_l, same_r, same_i, cross = call(
        prepare_kernel,
        [((SLAB, SLAB), BF16)]
        + [((NB, NB), BF16)] * 4
        + [((6 * LANES, NB), BF16)] * 2
        + [((NB, 6 * LANES), BF16)] * 2
        + [((HALF, NB), F32)] * 3,
        [place, shift],
        [placed_order, material.reshape(1, SLAB), modes_in, modes_out, face_lift, modal_rates.reshape(1, NB)]
        + [jnp.asarray(trace_rows())],
        2 * 5 * 384 * 384 * 768,
        [pltpu.VMEM((NB, 6 * LANES), F32)],
    )

    faces = [((ROWS, 4 * LANES), F32)] + [((ROWS * 3 // 4, LANES), F32)] * 2 + [((HALF * 3 // 4, LANES), F32)] * 2

    def exchange(to_chip, to_next, to_even, to_odd):
        from_odd = lax.ppermute(to_odd, "space", ODD_SIDES)
        from_even = lax.ppermute(to_even, "space", EVEN_SIDES)
        from_next = lax.ppermute(to_next, "tm", NEXT_CHIP)
        from_chip = lax.ppermute(to_chip, "tm", SAME_CHIP)
        return from_chip, from_next, from_even, from_odd

    coefficients = [same_r, same_i, cross]
    modal, inner, *outgoing = call(
        first_kernel,
        [((ROWS, NB), F32)] + faces,
        [place],
        [arrived, in_h, in_l, trace_h, trace_l] + coefficients,
        2 * 3 * 512 * 384 * (384 + 768),
        [pltpu.VMEM((ROWS, NB), F32)],
    )
    incoming = exchange(*outgoing)
    inner, *outgoing = call(
        sweep_kernel,
        faces,
        [place],
        [modal, inner, *incoming, lift_h, lift_l, trace_h, trace_l] + coefficients,
        2 * 3 * 512 * 384 * (768 + 768),
    )
    incoming = exchange(*outgoing)
    (steps,) = call(
        last_kernel,
        [((ROWS, NB), F32)],
        [place],
        [modal, inner, *incoming, lift_h, lift_l, out_h, out_l] + coefficients,
        2 * 3 * 512 * 384 * (768 + 384),
        [pltpu.VMEM((ROWS, NB), F32)],
    )
    back = lax.all_to_all(steps.reshape(16, 32, NB), "tm", 0, 0, tiled=True)
    (out,) = call(
        restore_kernel, [((2, NB, SLAB), F32)], [], [back, order], 2 * 4 * 256 * 256 * 384
    )
    return out


def solution(mesh):
    return jax.shard_map(
        shards,
        mesh=mesh,
        in_specs=(
            P("tm", None, "space"),
            P("space"),
            P(),
            P(),
            P(),
            P(),
            P(None, "space"),
            P(None, "space"),
        ),
        out_specs=P("tm", None, "space"),
        check_vma=False,
    )
```

time: 107 us -> 97 us (0.907)
  waiting for transfers between devices: 17 us -> 8.46 us
  starting transfers between devices: 26.5 us -> 24.9 us
  Pallas kernels: 18.5 us -> 19.9 us
    all_to_all x1, waiting for transfers between devices: 3.87 us -> 0.21 us  [shards(): lax.all_to_all(table, 'space', 0, 0, tiled=True, axis_index_groups=[[0, 1...]
    all_to_all x1, waiting for transfers between devices: 3.55 us -> 1.03 us  [shards(): arrived = lax.all_to_all(sent, 'tm', 0, 0, tiled=True).reshape(ROWS, NB)]
    ppermute x8, waiting for transfers between devices: 9.59 us -> 7.22 us  [the longest x2 4.36 us: exchange(): from_even = lax.ppermute(to_even, 'space', EVEN_SIDES)]
    all_to_all x1, starting transfers between devices: 5.82 us -> 3.48 us  [shards(): lax.all_to_all(table, 'space', 0, 0, tiled=True, axis_index_groups=[[0, 1...]
    pallas_call x6 -> x8, Pallas kernels: 18.5 us -> 19.9 us  [call(): pl.pallas_call(body, out_shape=outs + scalar_outs, in_specs=[SMEM] * len(...]
  transfers between devices with their start and end apart: 10 -> 10, of which waited for: 4 -> 6; matrix products, arithmetic and copies ran while one was open for 0% -> 0% of each run, Pallas kernels for 2% -> 5%
where the time goes in v2:
time: 97 us; the launch traced here: 95.9 us
  starting transfers between devices  24.9 us (26%)
  local copies, waits for them, and re-layouts  21.4 us (22%)
  blocking collectives  20.8 us (21%)
  Pallas kernels  19.9 us (21%)
  waiting for transfers between devices  8.46 us (9%)
    unnamed x67, local copies, waits for them, and re-layouts  21.4 us
    all_to_all x1, blocking collectives, shards(): back = lax.all_to_all(steps.reshape(16, 32, NB), 'tm', 0, 0, tiled=True)  20.8 us
    pallas_call x8, Pallas kernels, call(): pl.pallas_call(body, out_shape=outs + scalar_outs, in_specs=[SMEM] * len(...  19.9 us
    all_to_all x1, starting transfers between devices, shards(): arrived = lax.all_to_all(sent, 'tm', 0, 0, tiled=True).reshape(ROWS, NB)  7.81 us
    ppermute x2, starting transfers between devices, exchange(): from_odd = lax.ppermute(to_odd, 'space', ODD_SIDES)  7.57 us
    ppermute x2, starting transfers between devices, exchange(): from_next = lax.ppermute(to_next, 'tm', NEXT_CHIP)  4.66 us
    ppermute x2, waiting for transfers between devices, exchange(): from_even = lax.ppermute(to_even, 'space', EVEN_SIDES)  4.36 us
    all_to_all x1, starting transfers between devices, shards(): lax.all_to_all(table, 'space', 0, 0, tiled=True, axis_index_groups=[[0, 1...  3.48 us
  transfers between devices with their start and end apart: 10, of which 6 were waited for; matrix products, arithmetic and copies ran while one was open for 0% of the time, Pallas kernels for 5%

profile of v2, /device:TPU:4, one launch (start us, length us, event | category | flops | bytes accessed | tf_op | source)
XLA Modules:
  0.0 95.9 jit_solution(3957214476088747264)
XLA Ops:
  1.5 1.2 %shard_map.91 = s32[4,8,128]{2,1,0:T(8,128)} custom-call(s32[2]{0:T(128)S(1)} %pad_add_fusion.place, s32[6,256]{1,0:T(8,128)S(1)} %copy-done.11, s32[2,128]{1,0:T(2,128)S(1)} %copy-done.13), custom_call_target="tpu_custom_call" | custom-call | flops 10000 | bytes 23552 | tf_op jit(solution)/shard_map/pallas_call | solution.py:344
  2.6 3.5 %all-to-all-start = ((s32[4,8,128]{2,1,0:T(8,128)}), s32[4,8,128]{2,1,0:T(8,128)S(1)}, u32[]{:S(2)}, u32[]{:S(2)}) async-start(s32[4,8,128]{2,1,0:T(8,128)} %shard_map.91), calls=%async_computation | async-start | bytes 32768 | tf_op jit(solution)/shard_map/all_to_all | solution.py:358
  6.1 1.1 %copy-done = f32[2,384,256]{2,1,0:T(8,128)S(1)} copy-done((f32[2,384,256]{2,1,0:T(8,128)S(1)}, f32[2,384,256]{2,1,0:T(8,128)}, u32[]{:S(2)}) %copy-start) | copy-done | bytes 786456
  8.6 2.0 %shard_map.92 = (f32[2,32,8,384]{3,2,1,0:T(8,128)S(1)}, f32[32,8,256]{2,1,0:T(8,128)S(1)}, s32[256]{0:T(256)S(1)}) custom-call(s32[6,256]{1,0:T(8,128)S(1)} %copy-done.12, s32[2,128]{1,0:T(2,128)S(1)} %copy-done.14, f32[2,384,256]{2,1,0:T(8,128)S(1)} %copy-done), custom_call_target="tpu_custom_call" | custom-call | flops 201326592 | bytes 1835008 | tf_op jit(solution)/shard_map/pallas_call | solution.py:344
  10.8 2.0 %shard_map.93 = (f32[16,32,384]{2,1,0:T(8,128)}, s32[2]{0:T(128)S(1)}) custom-call(s32[2]{0:T(128)S(1)} %pad_add_fusion.place, s32[32,128]{1,0:T(8,128)S(1)} %bitcast.8, s32[256]{0:T(256)S(1)} %get-tuple-element.33.spot, s32[32,128]{1,0:T(8,128)S(1)} %bitcast.9, f32[2,32,8,384]{3,2,1,0:T(8,128)S(1)} %get-tuple-element.34.placed), custom_call_target="tpu_custom_call" | custom-call | flops 1000000 | bytes 1589248 | tf_op jit(solution)/shard_map/pallas_call | solution.py:344
  12.8 7.8 %all-to-all-start.1 = ((f32[16,32,384]{2,1,0:T(8,128)}), f32[16,32,384]{2,1,0:T(8,128)S(1)}, u32[]{:S(2)}, u32[]{:S(2)}) async-start(f32[16,32,384]{2,1,0:T(8,128)} %get-tuple-element.35), calls=%async_computation.1 | async-start | bytes 1572864 | tf_op jit(solution)/shard_map/all_to_all | solution.py:372
  21.3 1.1 %copy-done.15 = f32[384,384]{1,0:T(8,128)S(1)} copy-done((f32[384,384]{1,0:T(8,128)S(1)}, f32[384,384]{1,0:T(8,128)}, u32[]{:S(2)}) %copy-start.15) | copy-done | bytes 589848
  22.4 1.1 %copy-done.16 = f32[384,384]{1,0:T(8,128)S(1)} copy-done((f32[384,384]{1,0:T(8,128)S(1)}, f32[384,384]{1,0:T(8,128)}, u32[]{:S(2)}) %copy-start.16) | copy-done | bytes 589848
  23.4 0.9 copy-done.18
  24.4 1.1 %copy-done.20 = bf16[768,384]{1,0:T(8,128)(2,1)S(1)} copy-done((bf16[768,384]{1,0:T(8,128)(2,1)S(1)}, bf16[768,384]{1,0:T(8,128)(2,1)}, u32[]{:S(2)}) %copy-start.20) | copy-done | bytes 589848
  25.4 2.6 %shard_map.94 = (bf16[256,256]{1,0:T(8,128)(2,1)S(1)}, bf16[384,384]{1,0:T(8,128)(2,1)S(1)}, bf16[384,384]{1,0:T(8,128)(2,1)S(1)}, bf16[384,384]{1,0:T(8,128)(2,...) custom-call(s32[2]{0:T(128)S(1)} %pad_add_fusion.place, ...), custom_call_target="tpu_custom_call" | custom-call | flops 1132462080 | bytes 7768576 | tf_op jit(solution)/shard_map/pallas_call | solution.py:344
  34.7 1.0 %all-to-all-done.1 = f32[16,32,384]{2,1,0:T(8,128)S(1)} async-done(((f32[16,32,384]{2,1,0:T(8,128)}), f32[16,32,384]{2,1,0:T(8,128)S(1)}, u32[]{:S(2)}, u32[]{:S(2)}) %all-to-all-start.1) | async-done | bytes 786464 | tf_op jit(solution)/shard_map/all_to_all | solution.py:372
  35.8 1.0 %copy-done.2 = f32[256,384]{1,0:T(8,128)S(1)} copy-done((f32[256,384]{1,0:T(8,128)S(1)}, f32[256,384]{1,0:T(8,128)}, u32[]{:S(2)}) %copy-start.2) | copy-done | bytes 393240
  36.8 1.0 %copy-done.4 = f32[256,384]{1,0:T(8,128)S(1)} copy-done((f32[256,384]{1,0:T(8,128)S(1)}, f32[256,384]{1,0:T(8,128)}, u32[]{:S(2)}) %copy-start.4) | copy-done | bytes 393240
  37.8 1.1 %copy-done.22 = bf16[768,384]{1,0:T(8,128)(2,1)S(1)} copy-done((bf16[768,384]{1,0:T(8,128)(2,1)S(1)}, bf16[768,384]{1,0:T(8,128)(2,1)}, u32[]{:S(2)}) %copy-start.22) | copy-done | bytes 589848
  38.8 1.1 %copy-done.25 = bf16[768,384]{1,0:T(8,128)(2,1)S(1)} copy-done((bf16[768,384]{1,0:T(8,128)(2,1)S(1)}, bf16[768,384]{1,0:T(8,128)(2,1)}, u32[]{:S(2)}) %copy-start.25) | copy-done | bytes 589848
  39.9 1.0 %copy-done.28 = bf16[384,384]{1,0:T(8,128)(2,1)S(1)} copy-done((bf16[384,384]{1,0:T(8,128)(2,1)S(1)}, bf16[384,384]{1,0:T(8,128)(2,1)}, u32[]{:S(2)}) %copy-start.28) | copy-done | bytes 294936
  40.9 1.0 %copy-done.30 = bf16[384,384]{1,0:T(8,128)(2,1)S(1)} copy-done((bf16[384,384]{1,0:T(8,128)(2,1)S(1)}, bf16[384,384]{1,0:T(8,128)(2,1)}, u32[]{:S(2)}) %copy-start.30) | copy-done | bytes 294936
  41.8 3.8 %shard_map.95 = (f32[512,384]{1,0:T(8,128)S(1)}, f32[512,512]{1,0:T(8,128)S(1)}, f32[384,128]{1,0:T(8,128)S(1)}, f32[384,128]{1,0:T(8,128)S(1)}, f32[192,128]{1,0:T(8,128)S(1)}, /*index=5*/f32[192,128]{1,0:T(8,128)S(1)}) custom-call(s32[2]{0:T(128)S(1)} %pad_add_fusion.place, f32[512,384]{1,0:T(8,128)S(1)} %bitcast.7, bf16[384,384]{1,0:T(8,128)(2,1)S(1)} %copy-done.28, ...), custom_call_target="tpu_custom_call" | custom-call | flops 1358954496 | bytes 6160384 | tf_op jit(solution)/shard_map/pallas_call | solution.py:344
  45.7 2.5 %collective-permute-start.1 = (f32[384,128]{1,0:T(8,128)S(1)}, f32[384,128]{1,0:T(8,128)S(1)}, u32[]{:S(2)}, u32[]{:S(2)}) collective-permute-start(f32[384,128]{1,0:T(8,128)S(1)} %get-tuple-element.48), channel_id=1, source_target_pairs={{8,32},{40,64},{72,96},{104,112},{120,80},{88,48},{56,16},{24,0},{... | collective-permute-start | bytes 589832 | tf_op jit(solution)/shard_map/ppermute | solution.py:392
  48.2 1.2 %collective-permute-start.2 = (f32[192,128]{1,0:T(8,128)S(1)}, f32[192,128]{1,0:T(8,128)S(1)}, u32[]{:S(2)}, u32[]{:S(2)}) collective-permute-start(f32[192,128]{1,0:T(8,128)S(1)} %get-tuple-element.49), channel_id=1, source_target_pairs={{0,1},{1,0},{2,3},{3,2},{4,5},{5,4},{6,7},{7,6},{8,9},{9,8},{10,11... | collective-permute-start | bytes 294920 | tf_op jit(solution)/shard_map/ppermute | solution.py:391
  49.4 3.3 %collective-permute-start.3 = (f32[192,128]{1,0:T(8,128)S(1)}, f32[192,128]{1,0:T(8,128)S(1)}, u32[]{:S(2)}, u32[]{:S(2)}) collective-permute-start(f32[192,128]{1,0:T(8,128)S(1)} %get-tuple-element.50), channel_id=1, source_target_pairs={{1,2},{2,1},{3,4},{4,3},{5,6},{6,5},{9,10},{10,9},{11,12},{12,11},... | collective-permute-start | bytes 294920 | tf_op jit(solution)/shard_map/ppermute | solution.py:390
  52.7 2.5 %collective-permute-done.2.from_even = f32[192,128]{1,0:T(8,128)S(1)} collective-permute-done((f32[192,128]{1,0:T(8,128)S(1)}, f32[192,128]{1,0:T(8,128)S(1)}, u32[]{:S(2)}, u32[]{:S(2)}) %collective-permute-start.2) | collective-permute-done | bytes 98336 | tf_op jit(solution)/shard_map/ppermute | solution.py:391
  55.2 1.6 %collective-permute-done.3.from_odd = f32[192,128]{1,0:T(8,128)S(1)} collective-permute-done((f32[192,128]{1,0:T(8,128)S(1)}, f32[192,128]{1,0:T(8,128)S(1)}, u32[]{:S(2)}, u32[]{:S(2)}) %collective-permute-start.3) | collective-permute-done | bytes 98336 | tf_op jit(solution)/shard_map/ppermute | solution.py:390
  56.9 4.1 %shard_map.96 = (f32[512,512]{1,0:T(8,128)S(1)}, f32[384,128]{1,0:T(8,128)S(1)}, f32[384,128]{1,0:T(8,128)S(1)}, f32[192,128]{1,0:T(8,128)S(1)}, f32[192,128]{1,0:T(8,128)S(1)}) custom-call(s32[2]{0:T(128)S(1)} %pad_add_fusion.place, f32[512,384]{1,0:T(8,128)S(1)} %get-tuple-element.45.modal, f32[512,512]{1,0:T(8,128)S(1)} %get-tuple-element.46.inner, ...), custom_call_target="tpu_custom_call" | custom-call | flops 1811939328 | bytes 7602176 | tf_op jit(solution)/shard_map/pallas_call | solution.py:344
  61.0 2.2 %collective-permute-start.5 = (f32[384,128]{1,0:T(8,128)S(1)}, f32[384,128]{1,0:T(8,128)S(1)}, u32[]{:S(2)}, u32[]{:S(2)}) collective-permute-start(f32[384,128]{1,0:T(8,128)S(1)} %get-tuple-element.55), channel_id=1, source_target_pairs={{8,32},{40,64},{72,96},{104,112},{120,80},{88,48},{56,16},{24,0},{... | collective-permute-start | bytes 589832 | tf_op jit(solution)/shard_map/ppermute | solution.py:392
  63.2 4.3 %collective-permute-start.7 = (f32[192,128]{1,0:T(8,128)S(1)}, f32[192,128]{1,0:T(8,128)S(1)}, u32[]{:S(2)}, u32[]{:S(2)}) collective-permute-start(f32[192,128]{1,0:T(8,128)S(1)} %get-tuple-element.57), channel_id=1, source_target_pairs={{1,2},{2,1},{3,4},{4,3},{5,6},{6,5},{9,10},{10,9},{11,12},{12,11},... | collective-permute-start | bytes 294920 | tf_op jit(solution)/shard_map/ppermute | solution.py:390
  67.5 1.9 %collective-permute-done.6.from_even = f32[192,128]{1,0:T(8,128)S(1)} collective-permute-done((f32[192,128]{1,0:T(8,128)S(1)}, f32[192,128]{1,0:T(8,128)S(1)}, u32[]{:S(2)}, u32[]{:S(2)}) %collective-permute-start.6) | collective-permute-done | bytes 98336 | tf_op jit(solution)/shard_map/ppermute | solution.py:391
  69.4 1.2 %collective-permute-done.7.from_odd = f32[192,128]{1,0:T(8,128)S(1)} collective-permute-done((f32[192,128]{1,0:T(8,128)S(1)}, f32[192,128]{1,0:T(8,128)S(1)}, u32[]{:S(2)}, u32[]{:S(2)}) %collective-permute-start.7) | collective-permute-done | bytes 98336 | tf_op jit(solution)/shard_map/ppermute | solution.py:390
  70.6 3.1 %shard_map.97 = f32[512,384]{1,0:T(8,128)S(1)} custom-call(s32[2]{0:T(128)S(1)} %pad_add_fusion.place, f32[512,384]{1,0:T(8,128)S(1)} %get-tuple-element.45.modal, f32[512,512]{1,0:T(8,128)S(1)} %get-tuple-element.53.inner, f32[384,128]{1,0:T(8,128)S(1)} %collective-permute-done.4.from_chip, f32[384,128]{1,0:T(8,128)S(1)} %collective-permute-done.5.from_next, ...), custom_call_target="tpu_custom_call" | custom-call | flops 1358954496 | bytes 6160384 | tf_op jit(solution)/shard_map/pallas_call | solution.py:344
  73.8 20.8 %all_to_all.15.arrived = f32[16,32,384]{2,1,0:T(8,128)S(1)} all-to-all(f32[16,32,384]{2,1,0:T(8,128)S(1)} %bitcast.6), channel_id=1, replica_groups=mesh['tm'=16,'space'=8] {'tm'}, dimensions={0} | all-to-all | bytes 1572864 | tf_op jit(solution)/shard_map/all_to_all | solution.py:422
  94.6 1.3 %shard_map.98 = f32[2,384,256]{2,1,0:T(8,128)} custom-call(f32[16,32,384]{2,1,0:T(8,128)S(1)} %all_to_all.15.arrived, bf16[256,256]{1,0:T(8,128)(2,1)S(1)} %copy-done.10), custom_call_target="tpu_custom_call" | custom-call | flops 201326592 | bytes 1703936 | tf_op jit(solution)/shard_map/pallas_call | solution.py:344
  (66 shorter events, 10.6 us)
Async XLA Ops:
  2.6 8.2 %all-to-all-start = ((s32[4,8,128]{2,1,0:T(8,128)}), s32[4,8,128]{2,1,0:T(8,128)S(1)}, u32[]{:S(2)}, u32[]{:S(2)}) async-start(s32[4,8,128]{2,1,0:T(8,128)} %shard_map.91), calls=%async_computation | async-start | bytes 32768 | tf_op jit(solution)/shard_map/all_to_all | solution.py:358
  6.1 1.1 %copy-start = (f32[2,384,256]{2,1,0:T(8,128)S(1)}, f32[2,384,256]{2,1,0:T(8,128)}, u32[]{:S(2)}) copy-start(f32[2,384,256]{2,1,0:T(8,128)} %rhs.1) | copy-start | bytes 2359300
  10.6 2.2 %copy-start.17 = (f32[32,8,256]{2,1,0:T(8,128)}, f32[32,8,256]{2,1,0:T(8,128)S(1)}, u32[]{:S(2)}) copy-start(f32[32,8,256]{2,1,0:T(8,128)S(1)} %get-tuple-element.37.placed_order) | copy-start | bytes 786436
  10.8 9.8 %copy-start.32 = (f32[384]{0:T(512)S(1)}, f32[384]{0:T(512)}, u32[]{:S(2)}) copy-start(f32[384]{0:T(512)} %param.11) | copy-start | bytes 4612
  10.8 9.8 %copy-start.31 = (f32[6,384,96]{1,2,0:T(8,128)S(1)}, f32[6,384,96]{1,2,0:T(8,128)}, u32[]{:S(2)}) copy-start(f32[6,384,96]{1,2,0:T(8,128)} %param.14) | copy-start | bytes 2654212
  12.8 23.0 %all-to-all-start.1 = ((f32[16,32,384]{2,1,0:T(8,128)}), f32[16,32,384]{2,1,0:T(8,128)S(1)}, u32[]{:S(2)}, u32[]{:S(2)}) async-start(f32[16,32,384]{2,1,0:T(8,128)} %get-tuple-element.35), calls=%async_computation.1 | async-start | bytes 1572864 | tf_op jit(solution)/shard_map/all_to_all | solution.py:372
  21.3 1.1 %copy-start.15 = (f32[384,384]{1,0:T(8,128)S(1)}, f32[384,384]{1,0:T(8,128)}, u32[]{:S(2)}) copy-start(f32[384,384]{1,0:T(8,128)} %modes_in.1) | copy-start | bytes 1769476
  22.4 1.1 %copy-start.16 = (f32[384,384]{1,0:T(8,128)S(1)}, f32[384,384]{1,0:T(8,128)}, u32[]{:S(2)}) copy-start(f32[384,384]{1,0:T(8,128)} %modes_out.1) | copy-start | bytes 1769476
  23.4 0.9 copy-start.18
  24.4 1.1 %copy-start.20 = (bf16[768,384]{1,0:T(8,128)(2,1)S(1)}, bf16[768,384]{1,0:T(8,128)(2,1)}, u32[]{:S(2)}) copy-start(bf16[768,384]{1,0:T(8,128)(2,1)} %constant.11.clone.pick) | copy-start | bytes 1769476
  28.0 0.8 copy-start.1
  31.7 0.8 copy-start.21
  32.5 0.8 copy-start.24
  35.8 1.0 %copy-start.2 = (f32[256,384]{1,0:T(8,128)S(1)}, f32[256,384]{1,0:T(8,128)}, u32[]{:S(2)}) copy-start(f32[256,384]{1,0:T(8,128)} %copy-done.1) | copy-start | bytes 1179652
  36.8 1.0 %copy-start.4 = (f32[256,384]{1,0:T(8,128)S(1)}, f32[256,384]{1,0:T(8,128)}, u32[]{:S(2)}) copy-start(f32[256,384]{1,0:T(8,128)} %copy-done.3) | copy-start | bytes 1179652
  37.8 1.1 %copy-start.22 = (bf16[768,384]{1,0:T(8,128)(2,1)S(1)}, bf16[768,384]{1,0:T(8,128)(2,1)}, u32[]{:S(2)}) copy-start(bf16[768,384]{1,0:T(8,128)(2,1)} %copy-done.21) | copy-start | bytes 1769476
  38.8 1.1 %copy-start.25 = (bf16[768,384]{1,0:T(8,128)(2,1)S(1)}, bf16[768,384]{1,0:T(8,128)(2,1)}, u32[]{:S(2)}) copy-start(bf16[768,384]{1,0:T(8,128)(2,1)} %copy-done.24) | copy-start | bytes 1769476
  39.9 1.0 %copy-start.28 = (bf16[384,384]{1,0:T(8,128)(2,1)S(1)}, bf16[384,384]{1,0:T(8,128)(2,1)}, u32[]{:S(2)}) copy-start(bf16[384,384]{1,0:T(8,128)(2,1)} %copy-done.27) | copy-start | bytes 884740
  40.9 1.0 %copy-start.30 = (bf16[384,384]{1,0:T(8,128)(2,1)S(1)}, bf16[384,384]{1,0:T(8,128)(2,1)}, u32[]{:S(2)}) copy-start(bf16[384,384]{1,0:T(8,128)(2,1)} %copy-done.29) | copy-start | bytes 884740
  41.8 15.0 %copy-start.23 = (bf16[768,384]{1,0:T(8,128)(2,1)S(1)}, bf16[768,384]{1,0:T(8,128)(2,1)}, u32[]{:S(2)}) copy-start(bf16[768,384]{1,0:T(8,128)(2,1)} %copy-done.21) | copy-start | bytes 1769476
  41.8 15.0 %copy-start.26 = (bf16[768,384]{1,0:T(8,128)(2,1)S(1)}, bf16[768,384]{1,0:T(8,128)(2,1)}, u32[]{:S(2)}) copy-start(bf16[768,384]{1,0:T(8,128)(2,1)} %copy-done.24) | copy-start | bytes 1769476
  45.6 11.2 %collective-permute-start = (f32[384,128]{1,0:T(8,128)S(1)}, f32[384,128]{1,0:T(8,128)S(1)}, u32[]{:S(2)}, u32[]{:S(2)}) collective-permute-start(f32[384,128]{1,0:T(8,128)S(1)} %get-tuple-element.47), channel_id=1, source_target_pairs={{0,8},{8,0},{16,24},{24,16},{32,40},{40,32},{48,56},{56,48},{64,72... | collective-permute-start | bytes 589832 | tf_op jit(solution)/shard_map/ppermute | solution.py:393
  45.7 11.1 %collective-permute-start.1 = (f32[384,128]{1,0:T(8,128)S(1)}, f32[384,128]{1,0:T(8,128)S(1)}, u32[]{:S(2)}, u32[]{:S(2)}) collective-permute-start(f32[384,128]{1,0:T(8,128)S(1)} %get-tuple-element.48), channel_id=1, source_target_pairs={{8,32},{40,64},{72,96},{104,112},{120,80},{88,48},{56,16},{24,0},{... | collective-permute-start | bytes 589832 | tf_op jit(solution)/shard_map/ppermute | solution.py:392
  48.2 7.0 %collective-permute-start.2 = (f32[192,128]{1,0:T(8,128)S(1)}, f32[192,128]{1,0:T(8,128)S(1)}, u32[]{:S(2)}, u32[]{:S(2)}) collective-permute-start(f32[192,128]{1,0:T(8,128)S(1)} %get-tuple-element.49), channel_id=1, source_target_pairs={{0,1},{1,0},{2,3},{3,2},{4,5},{5,4},{6,7},{7,6},{8,9},{9,8},{10,11... | collective-permute-start | bytes 294920 | tf_op jit(solution)/shard_map/ppermute | solution.py:391
  49.4 7.4 %collective-permute-start.3 = (f32[192,128]{1,0:T(8,128)S(1)}, f32[192,128]{1,0:T(8,128)S(1)}, u32[]{:S(2)}, u32[]{:S(2)}) collective-permute-start(f32[192,128]{1,0:T(8,128)S(1)} %get-tuple-element.50), channel_id=1, source_target_pairs={{1,2},{2,1},{3,4},{4,3},{5,6},{6,5},{9,10},{10,9},{11,12},{12,11},... | collective-permute-start | bytes 294920 | tf_op jit(solution)/shard_map/ppermute | solution.py:390
  56.8 13.8 %copy-start.6 = (bf16[384,384]{1,0:T(8,128)(2,1)S(1)}, bf16[384,384]{1,0:T(8,128)(2,1)}, u32[]{:S(2)}) copy-start(bf16[384,384]{1,0:T(8,128)(2,1)} %copy-done.5) | copy-start | bytes 884740
  56.9 13.8 %copy-start.8 = (bf16[384,384]{1,0:T(8,128)(2,1)S(1)}, bf16[384,384]{1,0:T(8,128)(2,1)}, u32[]{:S(2)}) copy-start(bf16[384,384]{1,0:T(8,128)(2,1)} %copy-done.7) | copy-start | bytes 884740
  60.9 9.7 %collective-permute-start.4 = (f32[384,128]{1,0:T(8,128)S(1)}, f32[384,128]{1,0:T(8,128)S(1)}, u32[]{:S(2)}, u32[]{:S(2)}) collective-permute-start(f32[384,128]{1,0:T(8,128)S(1)} %get-tuple-element.54), channel_id=1, source_target_pairs={{0,8},{8,0},{16,24},{24,16},{32,40},{40,32},{48,56},{56,48},{64,72... | collective-permute-start | bytes 589832 | tf_op jit(solution)/shard_map/ppermute | solution.py:393
  61.0 9.6 %collective-permute-start.5 = (f32[384,128]{1,0:T(8,128)S(1)}, f32[384,128]{1,0:T(8,128)S(1)}, u32[]{:S(2)}, u32[]{:S(2)}) collective-permute-start(f32[384,128]{1,0:T(8,128)S(1)} %get-tuple-element.55), channel_id=1, source_target_pairs={{8,32},{40,64},{72,96},{104,112},{120,80},{88,48},{56,16},{24,0},{... | collective-permute-start | bytes 589832 | tf_op jit(solution)/shard_map/ppermute | solution.py:392
  63.2 6.2 %collective-permute-start.6 = (f32[192,128]{1,0:T(8,128)S(1)}, f32[192,128]{1,0:T(8,128)S(1)}, u32[]{:S(2)}, u32[]{:S(2)}) collective-permute-start(f32[192,128]{1,0:T(8,128)S(1)} %get-tuple-element.56), channel_id=1, source_target_pairs={{0,1},{1,0},{2,3},{3,2},{4,5},{5,4},{6,7},{7,6},{8,9},{9,8},{10,11... | collective-permute-start | bytes 294920 | tf_op jit(solution)/shard_map/ppermute | solution.py:391
  63.2 7.4 %collective-permute-start.7 = (f32[192,128]{1,0:T(8,128)S(1)}, f32[192,128]{1,0:T(8,128)S(1)}, u32[]{:S(2)}, u32[]{:S(2)}) collective-permute-start(f32[192,128]{1,0:T(8,128)S(1)} %get-tuple-element.57), channel_id=1, source_target_pairs={{1,2},{2,1},{3,4},{4,3},{5,6},{6,5},{9,10},{10,9},{11,12},{12,11},... | collective-permute-start | bytes 294920 | tf_op jit(solution)/shard_map/ppermute | solution.py:390
  73.8 20.8 %copy-start.10 = (bf16[256,256]{1,0:T(8,128)(2,1)S(1)}, bf16[256,256]{1,0:T(8,128)(2,1)}, u32[]{:S(2)}) copy-start(bf16[256,256]{1,0:T(8,128)(2,1)} %copy-done.9) | copy-start | bytes 393220
  (11 other events, 7.7 us)

commit v3 on v2

--- a/solution.py
+++ b/solution.py
@@ -121,7 +121,15 @@
     return dot(a[0], b[0], dims) + (dot(a[0], b[1], dims) + dot(a[1], b[0], dims))
 
 
-def table_kernel(place, nbr, halo, table):
+def table_kernel(place, nbr_far, halo_far, table, nbr, halo, done):
+    copies = [
+        pltpu.make_async_copy(far, near, done.at[at])
+        for at, (far, near) in enumerate([(nbr_far, nbr), (halo_far, halo)])
+    ]
+    for copy in copies:
+        copy.start()
+    for copy in copies:
+        copy.wait()
     upper = place[1] >= SLABS // 2
     steps = jnp.where(upper, nbr[1:2, :], nbr[0:1, :])
     labels = jnp.where(upper, halo[0:1, :], halo[1:2, :])
@@ -131,7 +139,16 @@
         table[member] = packed
 
 
-def order_kernel(nbr, halo, rhs, placed, order, spot):
+def order_kernel(nbr_far, halo_far, rhs_far, placed, order, spot, nbr, halo, rhs, done):
+    copies = [
+        pltpu.make_async_copy(far, near, done.at[at])
+        for at, (far, near) in enumerate([(nbr_far, nbr), (halo_far, halo), (rhs_far, rhs)])
+    ]
+    for copy in copies:
+        copy.start()
+    copies[0].wait()
+    copies[1].wait()
+
     def across(face, at):
         return nbr[face, at] & 255
 
@@ -157,13 +174,19 @@
             order[sheet * 2 + layer, :, LANES:] = jnp.where(lane + LANES == at, 1.0, 0.0).astype(F32)
 
     picks = order[...].reshape(SLAB, SLAB).astype(BF16)
+    copies[2].wait()
     for step in range(2):
         high, low = split(rhs[step])
         values = dot(picks, high, NT) + dot(picks, low, NT)
         placed[step] = values.reshape(32, 8, NB)
 
 
-def align_kernel(place, chain, spot, tables, placed, sent, shift):
+def align_kernel(place, spot, placed, far, sent, shift, chain, tables, done):
+    copies = [pltpu.make_async_copy(far, near, done.at[at]) for at, near in enumerate([chain, tables])]
+    for copy in copies:
+        copy.start()
+    for copy in copies:
+        copy.wait()
     group = lax.shift_right_logical(place[1], 2)
     member = place[1] & 3
 
@@ -177,10 +200,10 @@
     origin = near
     for hop in range(4):
         slab = jnp.where(group == 0, 3 - hop, hop)
-        far = step(slab, near) & 255
-        origin = jnp.where(slab == member, jnp.where(group == 0, far, near), origin)
+        far_side = step(slab, near) & 255
+        origin = jnp.where(slab == member, jnp.where(group == 0, far_side, near), origin)
         if hop < 3:
-            label = step(slab, far) & 127
+            label = step(slab, far_side) & 127
             ahead = jnp.where(group == 0, 2 - hop, hop + 1)
             near = chain[ahead * 8 + 2, label] & 255
     found = spot[origin] & 127
@@ -195,27 +218,31 @@
             sent[device, at * 16 : at * 16 + 16, :] = values.reshape(16, NB)
 
 
-def prepare_kernel(
-    place, shift, placed_order, material, modes_in, modes_out, face_lift, rates, pick,
-    order, in_h, in_l, out_h, out_l, trace_h, trace_l, lift_h, lift_l, same_r, same_i, cross, lift,
-):
+def first_weights(ref):
+    return [ref.at[a:b] for a, b in [(0, 384), (384, 768), (768, 1536), (1536, 2304)]]
+
+
+def second_weights(ref):
+    return [ref.at[a:b] for a, b in [(0, 768), (768, 1536), (1536, 1920), (1920, 2304)]]
+
+
+def prepare_kernel(place, shift, placed_order, material, modes_in, modes_out, face_lift, rates, pick, *refs):
+    order, first_set, factors, second_far, second_set, lift, done = refs
+    in_h, in_l, trace_h, trace_l = first_weights(first_set)
+    lift_h, lift_l, out_h, out_l = second_weights(second_set)
+    same_r, same_i, cross = factors.at[0], factors.at[1], factors.at[2]
+    in_parts = split(modes_in[...])
+    in_h[...], in_l[...] = in_parts
+    out_parts = split(modes_out[...])
+    out_h[...], out_l[...] = out_parts
+    trace_h[...] = dot(pick[...], out_parts[0], NN).astype(BF16)
+    trace_l[...] = dot(pick[...], out_parts[1], NN).astype(BF16)
     for device in range(16):
         sheet = (SHEET_OF[device] + shift[1]) & 15
         picks = pltpu.roll(placed_order[pl.ds(sheet * 2, 2)], shift[0], 1)
         order[device * 16 : device * 16 + 16, :] = picks.reshape(16, SLAB).astype(BF16)
     own_picks = order[pl.ds(pl.multiple_of(place[0] * 16, 16), 16), :].astype(F32)
     own = jnp.sum(own_picks * material[...], axis=1, keepdims=True)
-    in_parts = split(modes_in[...])
-    in_h[...], in_l[...] = in_parts
-    out_parts = split(modes_out[...])
-    out_h[...], out_l[...] = out_parts
-    trace_h[...] = dot(pick[...], out_parts[0], NN).astype(BF16)
-    trace_l[...] = dot(pick[...], out_parts[1], NN).astype(BF16)
-    lift[...] = jnp.zeros_like(lift)
-    for face in range(6):
-        lift[:, face * LANES : face * LANES + NFT] = face_lift[face]
-    lifted = split(dot3(in_parts, split(lift[...]), NN))
-    lift_h[...], lift_l[...] = lifted
     for freq in range(16):
         angle = 2.0 * math.pi / STEPS * freq
         rows = slice(freq * 16, freq * 16 + 16)
@@ -226,13 +253,20 @@
         same_r[rows, :] = same
         same_i[rows, :] = same if freq else 1.0 / ((1.0 + DECAY) * own + rates[...])
         cross[rows, :] = imag / size
-
-
-def divided(modal, same_r, same_i, cross):
+    lift[...] = jnp.zeros_like(lift)
+    for face in range(6):
+        lift[face * LANES : face * LANES + NFT, :] = face_lift[face]
+    lift_h[...], lift_l[...] = split(dot3(split(lift[...]), in_parts, NT))
+    copy = pltpu.make_async_copy(second_set, second_far, done)
+    copy.start()
+    copy.wait()
+
+
+def divided(modal, factors):
     real, imag = modal[:HALF], modal[HALF:]
-    mixed = cross[...]
+    mixed = factors[2]
     return jnp.concatenate(
-        [real * same_r[...] + imag * mixed, imag * same_i[...] - real * mixed]
+        [real * factors[0] + imag * mixed, imag * factors[1] - real * mixed]
     )
 
 
@@ -270,13 +304,14 @@
 
 
 def first_kernel(
-    place, steps, in_h, in_l, trace_h, trace_l, same_r, same_i, cross,
+    place, steps, first_set, factors,
     modal, inner, to_chip, to_next, to_even, to_odd, spectrum,
 ):
+    in_h, in_l, trace_h, trace_l = first_weights(first_set)
     to_frequencies(steps, spectrum)
     start = dot3(split(spectrum[...]), (in_h[...], in_l[...]), NT)
     modal[...] = start
-    solved = split(divided(start, same_r, same_i, cross))
+    solved = split(divided(start, factors))
     traces = dot3(solved, (trace_h[...], trace_l[...]), NT)
     send_traces(place, traces, inner, to_chip, to_next, to_even, to_odd)
 
@@ -302,25 +337,28 @@
 
 
 def sweep_kernel(
-    place, modal, inner, from_chip, from_next, from_even, from_odd,
-    lift_h, lift_l, trace_h, trace_l, same_r, same_i, cross,
+    place, from_chip, from_next, from_even, from_odd, modal, inner,
+    first_set, second_set, factors,
     inner_out, to_chip, to_next, to_even, to_odd,
 ):
+    _, _, trace_h, trace_l = first_weights(first_set)
+    lift_h, lift_l, _, _ = second_weights(second_set)
     faces = split(gathered(place, inner, from_chip, from_next, from_even, from_odd))
-    corrected = modal[...] - dot3(faces, (lift_h[...], lift_l[...]), NT)
-    solved = split(divided(corrected, same_r, same_i, cross))
+    corrected = modal[...] - dot3(faces, (lift_h[...], lift_l[...]), NN)
+    solved = split(divided(corrected, factors))
     traces = dot3(solved, (trace_h[...], trace_l[...]), NT)
     send_traces(place, traces, inner_out, to_chip, to_next, to_even, to_odd)
 
 
 def last_kernel(
-    place, modal, inner, from_chip, from_next, from_even, from_odd,
-    lift_h, lift_l, out_h, out_l, same_r, same_i, cross,
+    place, from_chip, from_next, from_even, from_odd, modal, inner,
+    second_set, factors,
     steps, spectrum,
 ):
+    lift_h, lift_l, out_h, out_l = second_weights(second_set)
     faces = split(gathered(place, inner, from_chip, from_next, from_even, from_odd))
-    corrected = modal[...] - dot3(faces, (lift_h[...], lift_l[...]), NT)
-    solved = split(divided(corrected, same_r, same_i, cross))
+    corrected = modal[...] - dot3(faces, (lift_h[...], lift_l[...]), NN)
+    solved = split(divided(corrected, factors))
     spectrum[...] = dot3(solved, (out_h[...], out_l[...]), NT)
     to_steps(spectrum, steps)
 
@@ -335,56 +373,77 @@
 
 SMEM = pl.BlockSpec(memory_space=pltpu.SMEM)
 VMEM = pl.BlockSpec(memory_space=pltpu.VMEM)
-
-
-def call(body, outs, scalars, arrays, flops, scratch=(), scalar_outs=(), megabytes=16):
-    outs = [jax.ShapeDtypeStruct(shape, kind) for shape, kind in outs]
-    scalar_outs = [jax.ShapeDtypeStruct(shape, jnp.int32) for shape in scalar_outs]
-    moved = sum(a.size * a.dtype.itemsize for a in [*outs, *arrays])
+HBM = pl.BlockSpec(memory_space=pltpu.HBM)
+KEPT = pl.BlockSpec(memory_space=pltpu.VMEM)
+DMA = pltpu.SemaphoreType.DMA
+HELD = ((HBM, pltpu.HBM), (KEPT, pltpu.VMEM))
+
+
+def call(body, ins, outs, flops, scratch=(), megabytes=8):
+    shapes = [jax.ShapeDtypeStruct(shape, kind) for shape, kind, _ in outs]
+    moved = sum(a.size * a.dtype.itemsize for a in shapes + [a for a, _ in ins])
+    for held, space in HELD:
+        ins = [(pltpu.with_memory_space_constraint(a, space) if spec is held else a, spec) for a, spec in ins]
+        shapes = [space(shape, kind) if spec is held else old for old, (shape, kind, spec) in zip(shapes, outs)]
     return pl.pallas_call(
         body,
-        out_shape=outs + scalar_outs,
-        in_specs=[SMEM] * len(scalars) + [VMEM] * len(arrays),
-        out_specs=[VMEM] * len(outs) + [SMEM] * len(scalar_outs),
+        out_shape=shapes,
+        in_specs=[spec for _, spec in ins],
+        out_specs=[spec for _, _, spec in outs],
         scratch_shapes=list(scratch),
         compiler_params=pltpu.CompilerParams(vmem_limit_bytes=megabytes * 2**20),
         cost_estimate=pl.CostEstimate(flops=flops, bytes_accessed=moved, transcendentals=0),
-    )(*scalars, *arrays)
+    )(*[a for a, _ in ins])
 
 
 def shards(rhs, material, modal_rates, modes_in, modes_out, face_lift, neighbours, halo_send):
-    place = jnp.stack([lax.axis_index("tm"), lax.axis_index("space")]).astype(jnp.int32)
-    (table,) = call(table_kernel, [((4, 8, LANES), jnp.int32)], [place], [neighbours, halo_send], 10**4)
+    place = (jnp.stack([lax.axis_index("tm"), lax.axis_index("space")]).astype(jnp.int32), SMEM)
+    (table,) = call(
+        table_kernel,
+        [place, (neighbours, HBM), (halo_send, HBM)],
+        [((4, 8, LANES), jnp.int32, KEPT)],
+        10**4,
+        [pltpu.VMEM(neighbours.shape, jnp.int32), pltpu.VMEM(halo_send.shape, jnp.int32), DMA((2,))],
+    )
     chain = lax.all_to_all(
         table, "space", 0, 0, tiled=True, axis_index_groups=[[0, 1, 2, 3], [4, 5, 6, 7]]
     ).reshape(32, LANES)
     placed, placed_order, spot = call(
         order_kernel,
-        [((2, 32, 8, NB), F32), ((32, 8, SLAB), F32)],
-        [neighbours, halo_send],
-        [rhs],
+        [(neighbours, HBM), (halo_send, HBM), (rhs, HBM)],
+        [((2, 32, 8, NB), F32, KEPT), ((32, 8, SLAB), F32, KEPT), ((SLAB,), jnp.int32, SMEM)],
         2 * 4 * 256 * 256 * 384,
-        scalar_outs=[(SLAB,)],
+        [
+            pltpu.SMEM(neighbours.shape, jnp.int32),
+            pltpu.SMEM(halo_send.shape, jnp.int32),
+            pltpu.VMEM(rhs.shape, F32),
+            DMA((3,)),
+        ],
     )
     sent, shift = call(
-        align_kernel, [((16, 32, NB), F32)], [place, chain, spot], [chain, placed], 10**6, scalar_outs=[(2,)]
+        align_kernel,
+        [place, (spot, SMEM), (placed, KEPT), (chain, VMEM)],
+        [((16, 32, NB), F32, KEPT), ((2,), jnp.int32, SMEM)],
+        10**6,
+        [pltpu.SMEM((32, LANES), jnp.int32), pltpu.VMEM((32, LANES), jnp.int32), DMA((2,))],
     )
     arrived = lax.all_to_all(sent, "tm", 0, 0, tiled=True).reshape(ROWS, NB)
-    order, in_h, in_l, out_h, out_l, trace_h, trace_l, lift_h, lift_l, same_r, same_i, cross = call(
+    weights = [modes_in, modes_out, jnp.swapaxes(face_lift, 1, 2), modal_rates.reshape(1, NB), trace_rows()]
+    prepared = [((SLAB, SLAB), BF16, KEPT), ((2304, NB), BF16, KEPT), ((3, HALF, NB), F32, KEPT), ((2304, NB), BF16, HBM)]
+    order, first_set, factors, second_set = call(
         prepare_kernel,
-        [((SLAB, SLAB), BF16)]
-        + [((NB, NB), BF16)] * 4
-        + [((6 * LANES, NB), BF16)] * 2
-        + [((NB, 6 * LANES), BF16)] * 2
-        + [((HALF, NB), F32)] * 3,
-        [place, shift],
-        [placed_order, material.reshape(1, SLAB), modes_in, modes_out, face_lift, modal_rates.reshape(1, NB)]
-        + [jnp.asarray(trace_rows())],
+        [place, (shift, SMEM), (placed_order, KEPT), (material.reshape(1, SLAB), VMEM)]
+        + [(jnp.asarray(weight), VMEM) for weight in weights],
+        prepared,
         2 * 5 * 384 * 384 * 768,
-        [pltpu.VMEM((NB, 6 * LANES), F32)],
-    )
-
-    faces = [((ROWS, 4 * LANES), F32)] + [((ROWS * 3 // 4, LANES), F32)] * 2 + [((HALF * 3 // 4, LANES), F32)] * 2
+        [pltpu.VMEM((2304, NB), BF16), pltpu.VMEM((6 * LANES, NB), F32), DMA],
+    )
+
+    faces = (
+        [((ROWS, 4 * LANES), F32, KEPT)]
+        + [((ROWS * 3 // 4, LANES), F32, VMEM)] * 2
+        + [((HALF * 3 // 4, LANES), F32, VMEM)] * 2
+    )
 
     def exchange(to_chip, to_next, to_even, to_odd):
         from_odd = lax.ppermute(to_odd, "space", ODD_SIDES)
@@ -393,35 +452,36 @@
         from_chip = lax.ppermute(to_chip, "tm", SAME_CHIP)
         return from_chip, from_next, from_even, from_odd
 
-    coefficients = [same_r, same_i, cross]
     modal, inner, *outgoing = call(
         first_kernel,
-        [((ROWS, NB), F32)] + faces,
-        [place],
-        [arrived, in_h, in_l, trace_h, trace_l] + coefficients,
+        [place, (arrived, VMEM), (first_set, KEPT), (factors, KEPT)],
+        [((ROWS, NB), F32, KEPT)] + faces,
         2 * 3 * 512 * 384 * (384 + 768),
         [pltpu.VMEM((ROWS, NB), F32)],
     )
     incoming = exchange(*outgoing)
     inner, *outgoing = call(
         sweep_kernel,
+        [place]
+        + [(a, VMEM) for a in incoming] + [(a, KEPT) for a in [modal, inner, first_set]] + [(second_set, VMEM), (factors, KEPT)],
         faces,
-        [place],
-        [modal, inner, *incoming, lift_h, lift_l, trace_h, trace_l] + coefficients,
         2 * 3 * 512 * 384 * (768 + 768),
     )
     incoming = exchange(*outgoing)
     (steps,) = call(
         last_kernel,
-        [((ROWS, NB), F32)],
-        [place],
-        [modal, inner, *incoming, lift_h, lift_l, out_h, out_l] + coefficients,
+        [place]
+        + [(a, VMEM) for a in incoming] + [(a, KEPT) for a in [modal, inner]] + [(second_set, VMEM), (factors, KEPT)],
+        [((ROWS, NB), F32, VMEM)],
         2 * 3 * 512 * 384 * (768 + 384),
         [pltpu.VMEM((ROWS, NB), F32)],
     )
     back = lax.all_to_all(steps.reshape(16, 32, NB), "tm", 0, 0, tiled=True)
     (out,) = call(
-        restore_kernel, [((2, NB, SLAB), F32)], [], [back, order], 2 * 4 * 256 * 256 * 384
+        restore_kernel,
+        [(back, VMEM), (order, KEPT)],
+        [((2, NB, SLAB), F32, VMEM)],
+        2 * 4 * 256 * 256 * 384,
     )
     return out
 

time: 97 us -> 88.1 us (0.908)
  local copies, waits for them, and re-layouts: 21.4 us -> 4.37 us
  waiting for transfers between devices: 8.46 us -> 19.2 us
  starting transfers between devices: 24.9 us -> 20.7 us
  Pallas kernels: 19.9 us -> 23.3 us
  blocking collectives: 20.8 us -> 19.7 us
    unnamed x67 -> x14, local copies, waits for them, and re-layouts: 21.4 us -> 4.36 us
    all_to_all x1, waiting for transfers between devices: 1.03 us -> 6.95 us  [shards(): arrived = lax.all_to_all(sent, 'tm', 0, 0, tiled=True).reshape(ROWS, NB)]
    ppermute x2, waiting for transfers between devices: 4.36 us -> 8.58 us  [exchange(): from_even = lax.ppermute(to_even, 'space', EVEN_SIDES)]
    pallas_call x8, Pallas kernels: 19.9 us -> 23.3 us  [call(): pl.pallas_call(body, out_shape=shapes, in_specs=[spec for _, spec in ins]...]
    all_to_all x1, waiting for transfers between devices: 0.21 us -> 2.49 us  [shards(): lax.all_to_all(table, 'space', 0, 0, tiled=True, axis_index_groups=[[0, 1...]
    ppermute x2, starting transfers between devices: 4.66 us -> 2.51 us  [exchange(): from_next = lax.ppermute(to_next, 'tm', NEXT_CHIP)]
    ppermute x2, waiting for transfers between devices: 2.85 us -> 1.13 us  [exchange(): from_odd = lax.ppermute(to_odd, 'space', ODD_SIDES)]
    ppermute x2, starting transfers between devices: 7.57 us -> 6.27 us  [exchange(): from_odd = lax.ppermute(to_odd, 'space', ODD_SIDES)]
  transfers between devices with their start and end apart: 10 -> 10, of which waited for: 6 -> 5; matrix products, arithmetic and copies ran while one was open for 0% -> 0% of each run, Pallas kernels for 5% -> 7%
where the time goes in v3:
time: 88.1 us; the launch traced here: 87.5 us
  Pallas kernels  23.3 us (26%)
  starting transfers between devices  20.7 us (23%)
  blocking collectives  19.7 us (22%)
  waiting for transfers between devices  19.2 us (22%)
  local copies, waits for them, and re-layouts  4.37 us (5%)
    pallas_call x8, Pallas kernels, call(): pl.pallas_call(body, out_shape=shapes, in_specs=[spec for _, spec in ins]...  23.3 us
    all_to_all x1, blocking collectives, shards(): back = lax.all_to_all(steps.reshape(16, 32, NB), 'tm', 0, 0, tiled=True)  19.7 us
    ppermute x2, waiting for transfers between devices, exchange(): from_even = lax.ppermute(to_even, 'space', EVEN_SIDES)  8.58 us
    all_to_all x1, starting transfers between devices, shards(): arrived = lax.all_to_all(sent, 'tm', 0, 0, tiled=True).reshape(ROWS, NB)  7.85 us
    all_to_all x1, waiting for transfers between devices, shards(): arrived = lax.all_to_all(sent, 'tm', 0, 0, tiled=True).reshape(ROWS, NB)  6.95 us
    ppermute x2, starting transfers between devices, exchange(): from_odd = lax.ppermute(to_odd, 'space', ODD_SIDES)  6.27 us
    unnamed x14, local copies, waits for them, and re-layouts  4.36 us
    all_to_all x1, starting transfers between devices, shards(): lax.all_to_all(table, 'space', 0, 0, tiled=True, axis_index_groups=[[0, 1...  3.49 us
  transfers between devices with their start and end apart: 10, of which 5 were waited for; matrix products, arithmetic and copies ran while one was open for 0% of the time, Pallas kernels for 7%

profile of v3, /device:TPU:4, one launch (start us, length us, event | category | flops | bytes accessed | tf_op | source)
XLA Modules:
  0.0 87.5 jit_solution(9064659326030624444)
XLA Ops:
  0.0 0.1 pad_add_fusion.place
  0.1 1.9 %shard_map.92 = s32[4,8,128]{2,1,0:T(8,128)} custom-call(s32[2]{0:T(128)S(1)} %pad_add_fusion.place, s32[6,256]{1,0:T(8,128)} %nbr_far.3, s32[2,128]{1,0:T(2,128)} %halo_far.3), custom_call_target="tpu_custom_call" | custom-call | flops 10000 | bytes 23560 | tf_op jit(solution)/shard_map/pallas_call | solution.py:388
  2.0 3.5 %all-to-all-start = ((s32[4,8,128]{2,1,0:T(8,128)}), s32[4,8,128]{2,1,0:T(8,128)S(1)}, u32[]{:S(2)}, u32[]{:S(2)}) async-start(s32[4,8,128]{2,1,0:T(8,128)} %shard_map.92), calls=%async_computation | async-start | bytes 32768 | tf_op jit(solution)/shard_map/all_to_all | solution.py:408
  5.4 2.2 %shard_map.91 = (f32[2,32,8,384]{3,2,1,0:T(8,128)S(1)}, f32[32,8,256]{2,1,0:T(8,128)S(1)}, s32[256]{0:T(256)S(1)}) custom-call(s32[6,256]{1,0:T(8,128)} %nbr_far.3, s32[2,128]{1,0:T(2,128)} %halo_far.3, f32[2,384,256]{2,1,0:T(8,128)} %rhs_far.1), custom_call_target="tpu_custom_call" | custom-call | flops 201326592 | bytes 1843200 | tf_op jit(solution)/shard_map/pallas_call | solution.py:388
  7.7 2.5 %all-to-all-done = s32[4,8,128]{2,1,0:T(8,128)S(1)} async-done(((s32[4,8,128]{2,1,0:T(8,128)}), s32[4,8,128]{2,1,0:T(8,128)S(1)}, u32[]{:S(2)}, u32[]{:S(2)}) %all-to-all-start) | async-done | bytes 16416 | tf_op jit(solution)/shard_map/all_to_all | solution.py:408
  10.2 2.5 %shard_map.93 = (f32[16,32,384]{2,1,0:T(8,128)}, s32[2]{0:T(128)S(1)}) custom-call(s32[2]{0:T(128)S(1)} %pad_add_fusion.place, s32[256]{0:T(256)S(1)} %get-tuple-element.25.spot, f32[2,32,8,384]{3,2,1,0:T(8,128)S(1)} %get-tuple-element.26.placed, s32[32,128]{1,0:T(8,128)S(1)} %bitcast.8), custom_call_target="tpu_custom_call" | custom-call | flops 1000000 | bytes 1590288 | tf_op jit(solution)/shard_map/pallas_call | solution.py:388
  12.7 7.9 %all-to-all-start.1 = ((f32[16,32,384]{2,1,0:T(8,128)}), f32[16,32,384]{2,1,0:T(8,128)}, u32[]{:S(2)}, u32[]{:S(2)}) async-start(f32[16,32,384]{2,1,0:T(8,128)} %get-tuple-element.27), calls=%async_computation.1 | async-start | bytes 1572864 | tf_op jit(solution)/shard_map/all_to_all | solution.py:430
  20.6 0.0 copy-start.1
  20.6 1.2 %copy-done.1 = f32[6,384,96]{1,2,0:T(8,128)S(1)} copy-done((f32[6,384,96]{1,2,0:T(8,128)S(1)}, f32[6,384,96]{1,2,0:T(8,128)}, u32[]{:S(2)}) %copy-start.1) | copy-done | bytes 884760
  21.7 1.1 %copy-done.2 = f32[384,384]{1,0:T(8,128)S(1)} copy-done((f32[384,384]{1,0:T(8,128)S(1)}, f32[384,384]{1,0:T(8,128)}, u32[]{:S(2)}) %copy-start.2) | copy-done | bytes 589848
  22.8 1.1 %copy-done.3 = f32[384,384]{1,0:T(8,128)S(1)} copy-done((f32[384,384]{1,0:T(8,128)S(1)}, f32[384,384]{1,0:T(8,128)}, u32[]{:S(2)}) %copy-start.3) | copy-done | bytes 589848
  23.9 1.1 %copy-done.5 = bf16[768,384]{1,0:T(8,128)(2,1)S(1)} copy-done((bf16[768,384]{1,0:T(8,128)(2,1)S(1)}, bf16[768,384]{1,0:T(8,128)(2,1)}, u32[]{:S(2)}) %copy-start.5) | copy-done | bytes 589848
  24.9 3.9 %shard_map.94 = (bf16[256,256]{1,0:T(8,128)(2,1)S(1)}, bf16[2304,384]{1,0:T(8,128)(2,1)S(1)}, f32[3,256,384]{2,1,0:T(8,128)S(1)}, bf16[2304,384]{1,0:T(8,128)(2,1)}) custom-call(s32[2]{0:T(128)S(1)} %pad_add_fusion.place, s32[2]{0:T(128)S(1)} %get-tuple-element.28.shift, f32[32,8,256]{2,1,0:T(8,128)S(1)} %get-tuple-element.29.placed_order, ...), custom_call_target="tpu_custom_call" | custom-call | flops 1132462080 | bytes 7768592 | tf_op jit(solution)/shard_map/pallas_call | solution.py:388
  28.8 6.9 %all-to-all-done.1 = f32[16,32,384]{2,1,0:T(8,128)} async-done(((f32[16,32,384]{2,1,0:T(8,128)}), f32[16,32,384]{2,1,0:T(8,128)}, u32[]{:S(2)}, u32[]{:S(2)}) %all-to-all-start.1) | async-done | bytes 786464 | tf_op jit(solution)/shard_map/all_to_all | solution.py:430
  35.8 4.5 %shard_map.95 = (f32[512,384]{1,0:T(8,128)S(1)}, f32[512,512]{1,0:T(8,128)S(1)}, f32[384,128]{1,0:T(8,128)S(1)}, f32[384,128]{1,0:T(8,128)S(1)}, f32[192,128]{1,0:T(8,128)S(1)}, /*index=5*/f32[192,128]{1,0:T(8,128)S(1)}) custom-call(s32[2]{0:T(128)S(1)} %pad_add_fusion.place, f32[512,384]{1,0:T(8,128)} %bitcast.3.steps, ...), custom_call_target="tpu_custom_call" | custom-call | flops 1358954496 | bytes 6160392 | tf_op jit(solution)/shard_map/pallas_call | solution.py:388
  40.3 0.1 collective-permute-start
  40.4 0.9 %collective-permute-start.1 = (f32[384,128]{1,0:T(8,128)S(1)}, f32[384,128]{1,0:T(8,128)S(1)}, u32[]{:S(2)}, u32[]{:S(2)}) collective-permute-start(f32[384,128]{1,0:T(8,128)S(1)} %get-tuple-element.33), channel_id=1, source_target_pairs={{8,32},{40,64},{72,96},{104,112},{120,80},{88,48},{56,16},{24,0},{... | collective-permute-start | bytes 589832 | tf_op jit(solution)/shard_map/ppermute | solution.py:451
  41.3 3.3 %collective-permute-start.3 = (f32[192,128]{1,0:T(8,128)S(1)}, f32[192,128]{1,0:T(8,128)S(1)}, u32[]{:S(2)}, u32[]{:S(2)}) collective-permute-start(f32[192,128]{1,0:T(8,128)S(1)} %get-tuple-element.35), channel_id=1, source_target_pairs={{1,2},{2,1},{3,4},{4,3},{5,6},{6,5},{9,10},{10,9},{11,12},{12,11},... | collective-permute-start | bytes 294920 | tf_op jit(solution)/shard_map/ppermute | solution.py:449
  44.5 4.6 %collective-permute-done.2.from_even = f32[192,128]{1,0:T(8,128)S(1)} collective-permute-done((f32[192,128]{1,0:T(8,128)S(1)}, f32[192,128]{1,0:T(8,128)S(1)}, u32[]{:S(2)}, u32[]{:S(2)}) %collective-permute-start.2) | collective-permute-done | bytes 98336 | tf_op jit(solution)/shard_map/ppermute | solution.py:450
  49.1 0.0 collective-permute-done.3.from_odd
  49.1 0.0 collective-permute-done.from_chip
  49.1 0.0 collective-permute-done.1.from_next
  49.1 4.1 %shard_map.96 = (f32[512,512]{1,0:T(8,128)S(1)}, f32[384,128]{1,0:T(8,128)S(1)}, f32[384,128]{1,0:T(8,128)S(1)}, f32[192,128]{1,0:T(8,128)S(1)}, f32[192,128]{1,0:T(8,128)S(1)}) custom-call(s32[2]{0:T(128)S(1)} %pad_add_fusion.place, f32[384,128]{1,0:T(8,128)S(1)} %collective-permute-done.from_chip, f32[384,128]{1,0:T(8,128)S(1)} %collective-permute-done.1.from_next, ...), custom_call_target="tpu_custom_call" | custom-call | flops 1811939328 | bytes 8781832 | tf_op jit(solution)/shard_map/pallas_call | solution.py:388
  53.3 0.1 collective-permute-start.4
  53.3 1.6 %collective-permute-start.5 = (f32[384,128]{1,0:T(8,128)S(1)}, f32[384,128]{1,0:T(8,128)S(1)}, u32[]{:S(2)}, u32[]{:S(2)}) collective-permute-start(f32[384,128]{1,0:T(8,128)S(1)} %get-tuple-element.40), channel_id=1, source_target_pairs={{8,32},{40,64},{72,96},{104,112},{120,80},{88,48},{56,16},{24,0},{... | collective-permute-start | bytes 589832 | tf_op jit(solution)/shard_map/ppermute | solution.py:451
  55.0 0.4 collective-permute-start.6
  55.4 3.0 %collective-permute-start.7 = (f32[192,128]{1,0:T(8,128)S(1)}, f32[192,128]{1,0:T(8,128)S(1)}, u32[]{:S(2)}, u32[]{:S(2)}) collective-permute-start(f32[192,128]{1,0:T(8,128)S(1)} %get-tuple-element.42), channel_id=1, source_target_pairs={{1,2},{2,1},{3,4},{4,3},{5,6},{6,5},{9,10},{10,9},{11,12},{12,11},... | collective-permute-start | bytes 294920 | tf_op jit(solution)/shard_map/ppermute | solution.py:449
  58.4 4.0 %collective-permute-done.6.from_even = f32[192,128]{1,0:T(8,128)S(1)} collective-permute-done((f32[192,128]{1,0:T(8,128)S(1)}, f32[192,128]{1,0:T(8,128)S(1)}, u32[]{:S(2)}, u32[]{:S(2)}) %collective-permute-start.6) | collective-permute-done | bytes 98336 | tf_op jit(solution)/shard_map/ppermute | solution.py:450
  62.4 1.1 %collective-permute-done.7.from_odd = f32[192,128]{1,0:T(8,128)S(1)} collective-permute-done((f32[192,128]{1,0:T(8,128)S(1)}, f32[192,128]{1,0:T(8,128)S(1)}, u32[]{:S(2)}, u32[]{:S(2)}) %collective-permute-start.7) | collective-permute-done | bytes 98336 | tf_op jit(solution)/shard_map/ppermute | solution.py:449
  63.5 3.0 %shard_map.97 = f32[512,384]{1,0:T(8,128)S(1)} custom-call(s32[2]{0:T(128)S(1)} %pad_add_fusion.place, f32[384,128]{1,0:T(8,128)S(1)} %collective-permute-done.4.from_chip, f32[384,128]{1,0:T(8,128)S(1)} %collective-permute-done.5.from_next, f32[192,128]{1,0:T(8,128)S(1)} %collective-permute-done.6.from_even, ...), custom_call_target="tpu_custom_call" | custom-call | flops 1358954496 | bytes 6160392 | tf_op jit(solution)/shard_map/pallas_call | solution.py:388
  66.5 19.7 %all_to_all.15.arrived = f32[16,32,384]{2,1,0:T(8,128)S(1)} all-to-all(f32[16,32,384]{2,1,0:T(8,128)S(1)} %bitcast.7), channel_id=1, replica_groups=mesh['tm'=16,'space'=8] {'tm'}, dimensions={0} | all-to-all | bytes 1572864 | tf_op jit(solution)/shard_map/all_to_all | solution.py:479
  86.2 1.3 %shard_map.98 = f32[2,384,256]{2,1,0:T(8,128)} custom-call(f32[16,32,384]{2,1,0:T(8,128)S(1)} %all_to_all.15.arrived, bf16[256,256]{1,0:T(8,128)(2,1)S(1)} %get-tuple-element.44.order), custom_call_target="tpu_custom_call" | custom-call | flops 201326592 | bytes 1703936 | tf_op jit(solution)/shard_map/pallas_call | solution.py:388
  (13 shorter events, 0.0 us)
Async XLA Ops:
  0.0 20.5 %copy-start.6 = (f32[384]{0:T(512)S(1)}, f32[384]{0:T(512)}, u32[]{:S(2)}) copy-start(f32[384]{0:T(512)} %param.11) | copy-start | bytes 4612
  0.0 20.6 %copy-start.4 = (f32[256]{0:T(256)S(1)}, f32[256]{0:T(256)}, u32[]{:S(2)}) copy-start(f32[256]{0:T(256)} %param.10) | copy-start | bytes 3076
  2.0 8.2 %all-to-all-start = ((s32[4,8,128]{2,1,0:T(8,128)}), s32[4,8,128]{2,1,0:T(8,128)S(1)}, u32[]{:S(2)}, u32[]{:S(2)}) async-start(s32[4,8,128]{2,1,0:T(8,128)} %shard_map.92), calls=%async_computation | async-start | bytes 32768 | tf_op jit(solution)/shard_map/all_to_all | solution.py:408
  12.7 23.1 %all-to-all-start.1 = ((f32[16,32,384]{2,1,0:T(8,128)}), f32[16,32,384]{2,1,0:T(8,128)}, u32[]{:S(2)}, u32[]{:S(2)}) async-start(f32[16,32,384]{2,1,0:T(8,128)} %get-tuple-element.27), calls=%async_computation.1 | async-start | bytes 1572864 | tf_op jit(solution)/shard_map/all_to_all | solution.py:430
  20.6 1.2 %copy-start.1 = (f32[6,384,96]{1,2,0:T(8,128)S(1)}, f32[6,384,96]{1,2,0:T(8,128)}, u32[]{:S(2)}) copy-start(f32[6,384,96]{1,2,0:T(8,128)} %param.14) | copy-start | bytes 2654212
  21.7 1.1 %copy-start.2 = (f32[384,384]{1,0:T(8,128)S(1)}, f32[384,384]{1,0:T(8,128)}, u32[]{:S(2)}) copy-start(f32[384,384]{1,0:T(8,128)} %modes_in.1) | copy-start | bytes 1769476
  22.8 1.1 %copy-start.3 = (f32[384,384]{1,0:T(8,128)S(1)}, f32[384,384]{1,0:T(8,128)}, u32[]{:S(2)}) copy-start(f32[384,384]{1,0:T(8,128)} %modes_out.1) | copy-start | bytes 1769476
  23.9 1.1 %copy-start.5 = (bf16[768,384]{1,0:T(8,128)(2,1)S(1)}, bf16[768,384]{1,0:T(8,128)(2,1)}, u32[]{:S(2)}) copy-start(bf16[768,384]{1,0:T(8,128)(2,1)} %constant.11.clone.pick) | copy-start | bytes 1769476
  35.8 13.4 %copy-start = (bf16[2304,384]{1,0:T(8,128)(2,1)S(1)}, bf16[2304,384]{1,0:T(8,128)(2,1)}, u32[]{:S(2)}) copy-start(bf16[2304,384]{1,0:T(8,128)(2,1)} %get-tuple-element.38.second_set) | copy-start | bytes 5308420
  40.3 8.9 %collective-permute-start = (f32[384,128]{1,0:T(8,128)S(1)}, f32[384,128]{1,0:T(8,128)S(1)}, u32[]{:S(2)}, u32[]{:S(2)}) collective-permute-start(f32[384,128]{1,0:T(8,128)S(1)} %get-tuple-element.32), channel_id=1, source_target_pairs={{0,8},{8,0},{16,24},{24,16},{32,40},{40,32},{48,56},{56,48},{64,72... | collective-permute-start | bytes 589832 | tf_op jit(solution)/shard_map/ppermute | solution.py:452
  40.4 8.8 %collective-permute-start.1 = (f32[384,128]{1,0:T(8,128)S(1)}, f32[384,128]{1,0:T(8,128)S(1)}, u32[]{:S(2)}, u32[]{:S(2)}) collective-permute-start(f32[384,128]{1,0:T(8,128)S(1)} %get-tuple-element.33), channel_id=1, source_target_pairs={{8,32},{40,64},{72,96},{104,112},{120,80},{88,48},{56,16},{24,0},{... | collective-permute-start | bytes 589832 | tf_op jit(solution)/shard_map/ppermute | solution.py:451
  41.3 7.9 %collective-permute-start.2 = (f32[192,128]{1,0:T(8,128)S(1)}, f32[192,128]{1,0:T(8,128)S(1)}, u32[]{:S(2)}, u32[]{:S(2)}) collective-permute-start(f32[192,128]{1,0:T(8,128)S(1)} %get-tuple-element.34), channel_id=1, source_target_pairs={{0,1},{1,0},{2,3},{3,2},{4,5},{5,4},{6,7},{7,6},{8,9},{9,8},{10,11... | collective-permute-start | bytes 294920 | tf_op jit(solution)/shard_map/ppermute | solution.py:450
  41.3 7.9 %collective-permute-start.3 = (f32[192,128]{1,0:T(8,128)S(1)}, f32[192,128]{1,0:T(8,128)S(1)}, u32[]{:S(2)}, u32[]{:S(2)}) collective-permute-start(f32[192,128]{1,0:T(8,128)S(1)} %get-tuple-element.35), channel_id=1, source_target_pairs={{1,2},{2,1},{3,4},{4,3},{5,6},{6,5},{9,10},{10,9},{11,12},{12,11},... | collective-permute-start | bytes 294920 | tf_op jit(solution)/shard_map/ppermute | solution.py:449
  53.3 10.3 %collective-permute-start.4 = (f32[384,128]{1,0:T(8,128)S(1)}, f32[384,128]{1,0:T(8,128)S(1)}, u32[]{:S(2)}, u32[]{:S(2)}) collective-permute-start(f32[384,128]{1,0:T(8,128)S(1)} %get-tuple-element.39), channel_id=1, source_target_pairs={{0,8},{8,0},{16,24},{24,16},{32,40},{40,32},{48,56},{56,48},{64,72... | collective-permute-start | bytes 589832 | tf_op jit(solution)/shard_map/ppermute | solution.py:452
  53.3 10.2 %collective-permute-start.5 = (f32[384,128]{1,0:T(8,128)S(1)}, f32[384,128]{1,0:T(8,128)S(1)}, u32[]{:S(2)}, u32[]{:S(2)}) collective-permute-start(f32[384,128]{1,0:T(8,128)S(1)} %get-tuple-element.40), channel_id=1, source_target_pairs={{8,32},{40,64},{72,96},{104,112},{120,80},{88,48},{56,16},{24,0},{... | collective-permute-start | bytes 589832 | tf_op jit(solution)/shard_map/ppermute | solution.py:451
  55.0 7.4 %collective-permute-start.6 = (f32[192,128]{1,0:T(8,128)S(1)}, f32[192,128]{1,0:T(8,128)S(1)}, u32[]{:S(2)}, u32[]{:S(2)}) collective-permute-start(f32[192,128]{1,0:T(8,128)S(1)} %get-tuple-element.41), channel_id=1, source_target_pairs={{0,1},{1,0},{2,3},{3,2},{4,5},{5,4},{6,7},{7,6},{8,9},{9,8},{10,11... | collective-permute-start | bytes 294920 | tf_op jit(solution)/shard_map/ppermute | solution.py:450
  55.4 8.1 %collective-permute-start.7 = (f32[192,128]{1,0:T(8,128)S(1)}, f32[192,128]{1,0:T(8,128)S(1)}, u32[]{:S(2)}, u32[]{:S(2)}) collective-permute-start(f32[192,128]{1,0:T(8,128)S(1)} %get-tuple-element.42), channel_id=1, source_target_pairs={{1,2},{2,1},{3,4},{4,3},{5,6},{6,5},{9,10},{10,9},{11,12},{12,11},... | collective-permute-start | bytes 294920 | tf_op jit(solution)/shard_map/ppermute | solution.py:449

commit v4 on v3

--- a/solution.py
+++ b/solution.py
@@ -75,13 +75,15 @@
 
 
 def tiles():
-    for block in range(SHEET // 8):
-        for lane in range(0, NB, LANES):
+    for lane in range(0, NB, LANES):
+        for block in range(SHEET // 8):
             yield lambda row: (slice(row * SHEET + block * 8, row * SHEET + block * 8 + 8), slice(lane, lane + LANES))
 
 
-def to_frequencies(steps, spectrum):
-    for at in tiles():
+def to_frequencies(steps, spectrum, copies):
+    for place, at in enumerate(tiles()):
+        if place % 2 == 0:
+            copies[place // 2].wait()
         freqs = real_fft([steps[at(n)] * DECAY**n for n in range(STEPS)])
         for freq in range(16):
             spectrum[at(freq)] = freqs[freq][0]
@@ -117,8 +119,14 @@
     return lax.dot_general(a, b, dims, preferred_element_type=F32)
 
 
-def dot3(a, b, dims):
-    return dot(a[0], b[0], dims) + (dot(a[0], b[1], dims) + dot(a[1], b[0], dims))
+def dot_rows(a, b):
+    return dot(jnp.concatenate([a[0], a[1], a[0]], 1), jnp.concatenate([b[0], b[0], b[1]], 1), NT)
+
+
+def dot_columns(a, b):
+    width = b[0].shape[1]
+    both = dot(a[0], jnp.concatenate([b[0], b[1]], 1), NN)
+    return both[:, :width] + (both[:, width:] + dot(a[1], b[0], NN))
 
 
 def table_kernel(place, nbr_far, halo_far, table, nbr, halo, done):
@@ -226,8 +234,13 @@
     return [ref.at[a:b] for a, b in [(0, 768), (768, 1536), (1536, 1920), (1920, 2304)]]
 
 
+def face_order(place):
+    core, slab = place[0] & 1, place[1] & 1
+    return [1 - slab, slab, 4 + core, 5 - core, 2, 3]
+
+
 def prepare_kernel(place, shift, placed_order, material, modes_in, modes_out, face_lift, rates, pick, *refs):
-    order, first_set, factors, second_far, second_set, lift, done = refs
+    order, first_set, factors, second_far, second_set, lift, sorted_pick, done = refs
     in_h, in_l, trace_h, trace_l = first_weights(first_set)
     lift_h, lift_l, out_h, out_l = second_weights(second_set)
     same_r, same_i, cross = factors.at[0], factors.at[1], factors.at[2]
@@ -235,8 +248,10 @@
     in_h[...], in_l[...] = in_parts
     out_parts = split(modes_out[...])
     out_h[...], out_l[...] = out_parts
-    trace_h[...] = dot(pick[...], out_parts[0], NN).astype(BF16)
-    trace_l[...] = dot(pick[...], out_parts[1], NN).astype(BF16)
+    for at, face in enumerate(face_order(place)):
+        sorted_pick[at * LANES : (at + 1) * LANES, :] = pick[pl.ds(pl.multiple_of(face * LANES, LANES), LANES), :]
+    trace_h[...] = dot(sorted_pick[...], out_parts[0], NN).astype(BF16)
+    trace_l[...] = dot(sorted_pick[...], out_parts[1], NN).astype(BF16)
     for device in range(16):
         sheet = (SHEET_OF[device] + shift[1]) & 15
         picks = pltpu.roll(placed_order[pl.ds(sheet * 2, 2)], shift[0], 1)
@@ -254,9 +269,9 @@
         same_i[rows, :] = same if freq else 1.0 / ((1.0 + DECAY) * own + rates[...])
         cross[rows, :] = imag / size
     lift[...] = jnp.zeros_like(lift)
-    for face in range(6):
-        lift[face * LANES : face * LANES + NFT, :] = face_lift[face]
-    lift_h[...], lift_l[...] = split(dot3(split(lift[...]), in_parts, NT))
+    for at, face in enumerate(face_order(place)):
+        lift[at * LANES : at * LANES + NFT, :] = face_lift[face]
+    lift_h[...], lift_l[...] = split(dot_rows(split(lift[...]), in_parts))
     copy = pltpu.make_async_copy(second_set, second_far, done)
     copy.start()
     copy.wait()
@@ -289,86 +304,103 @@
     return jnp.concatenate([packed, tail])
 
 
-def send_traces(place, traces, inner, to_chip, to_next, to_even, to_odd):
-    core_low = place[0] & 1 == 0
-    slab_even = place[1] & 1 == 0
-    inner[...] = traces[:, : 4 * LANES]
-    below, above = traces[:, 4 * LANES : 5 * LANES], traces[:, 5 * LANES :]
-    to_chip[...] = pack(jnp.where(core_low, above, below))
-    to_next[...] = pack(jnp.where(core_low, below, above))
-    sides = traces[:, : 2 * LANES].reshape(STEPS, 2, 8, 2 * LANES)
-    lower = sides[:, 0, :, :LANES].reshape(HALF, LANES)
-    upper = sides[:, 1, :, LANES:].reshape(HALF, LANES)
-    to_even[...] = pack(jnp.where(slab_even, upper, lower))
-    to_odd[...] = pack(jnp.where(slab_even, lower, upper))
+def send_traces(place, solved, trace_h, trace_l, traces, solved_h, solved_l, inner, to_chip, to_next, to_even, to_odd):
+    near = 1 - (place[1] & 1)
+    solved_h[...], solved_l[...] = solved
+    wide = 4 * LANES
+    traces[...] = dot_rows(solved, (trace_h[:wide], trace_l[:wide])).reshape(STEPS, 2, 8, wide)
+    to_chip[...] = pack(traces[:, :, :, 3 * LANES :].reshape(ROWS, LANES))
+    to_next[...] = pack(traces[:, :, :, 2 * LANES : 3 * LANES].reshape(ROWS, LANES))
+    to_even[...] = pack(traces[:, near, :, :LANES].reshape(HALF, LANES))
+    to_odd[...] = pack(traces[:, 1 - near, :, LANES : 2 * LANES].reshape(HALF, LANES))
+    inner[0] = traces[:, near, :, LANES : 2 * LANES].reshape(HALF, LANES)
+    inner[1] = traces[:, 1 - near, :, :LANES].reshape(HALF, LANES)
 
 
 def first_kernel(
-    place, steps, first_set, factors,
-    modal, inner, to_chip, to_next, to_even, to_odd, spectrum,
+    place, far, first_set, factors,
+    modal, solved_h, solved_l, inner, to_chip, to_next, to_even, to_odd, steps, spectrum, traces, done,
 ):
+    lanes = [slice(lane, lane + LANES) for lane in range(0, NB, LANES)]
+    copies = [
+        pltpu.make_async_copy(far.at[:, lane], steps.at[:, lane], done.at[at]) for at, lane in enumerate(lanes)
+    ]
+    for copy in copies:
+        copy.start()
     in_h, in_l, trace_h, trace_l = first_weights(first_set)
-    to_frequencies(steps, spectrum)
-    start = dot3(split(spectrum[...]), (in_h[...], in_l[...]), NT)
+    to_frequencies(steps, spectrum, copies)
+    start = dot_rows(split(spectrum[...]), (in_h[...], in_l[...]))
     modal[...] = start
     solved = split(divided(start, factors))
-    traces = dot3(solved, (trace_h[...], trace_l[...]), NT)
-    send_traces(place, traces, inner, to_chip, to_next, to_even, to_odd)
-
-
-def gathered(place, inner, from_chip, from_next, from_even, from_odd):
-    core_low = place[0] & 1 == 0
-    slab_even = place[1] & 1 == 0
-
-    def face(which):
-        return inner[:, which * LANES : which * LANES + LANES]
-
-    below = unpack(jnp.where(slab_even, from_odd[...], from_even[...])).reshape(STEPS, 1, 8, LANES)
-    above = unpack(jnp.where(slab_even, from_even[...], from_odd[...])).reshape(STEPS, 1, 8, LANES)
-    first = face(0).reshape(STEPS, 2, 8, LANES)
-    second = face(1).reshape(STEPS, 2, 8, LANES)
-    minus_x = jnp.concatenate([below, second[:, :1]], axis=1).reshape(ROWS, LANES)
-    plus_x = jnp.concatenate([first[:, 1:], above], axis=1).reshape(ROWS, LANES)
-    minus_y = pltpu.roll(face(3).reshape(ROWS // 8, 8, LANES), 1, 1).reshape(ROWS, LANES)
-    plus_y = pltpu.roll(face(2).reshape(ROWS // 8, 8, LANES), 7, 1).reshape(ROWS, LANES)
-    minus_z = unpack(jnp.where(core_low, from_next[...], from_chip[...]))
-    plus_z = unpack(jnp.where(core_low, from_chip[...], from_next[...]))
-    return jnp.concatenate([minus_x, plus_x, minus_y, plus_y, minus_z, plus_z], axis=1)
+    send_traces(
+        place, solved, trace_h, trace_l, traces, solved_h, solved_l, inner, to_chip, to_next, to_even, to_odd
+    )
+
+
+def inside_kernel(modal, solved_h, solved_l, first_set, second_set, base):
+    _, _, trace_h, trace_l = first_weights(first_set)
+    lift_h, lift_l, _, _ = second_weights(second_set)
+    wide = 4 * LANES
+    traces = dot_rows((solved_h[...], solved_l[...]), (trace_h[wide:], trace_l[wide:]))
+    traces = traces.reshape(ROWS // 8, 8, 2 * LANES)
+    minus_y = pltpu.roll(traces[:, :, LANES:], 1, 1).reshape(ROWS, LANES)
+    plus_y = pltpu.roll(traces[:, :, :LANES], 7, 1).reshape(ROWS, LANES)
+    faces = split(jnp.concatenate([minus_y, plus_y], axis=1))
+    base[...] = modal[...] - dot_columns(faces, (lift_h[wide:], lift_l[wide:]))
+
+
+def meet_kernel(place, from_chip, from_next, from_even, base, inner, second_set, out, faces):
+    near = 1 - (place[1] & 1)
+    wide = 4 * LANES
+    lift_h, lift_l, _, _ = second_weights(second_set)
+    faces[:, near, :, :LANES] = unpack(from_even[...]).reshape(STEPS, 8, LANES)
+    faces[:, 1 - near, :, :LANES] = inner[0].reshape(STEPS, 8, LANES)
+    faces[:, near, :, LANES : 2 * LANES] = inner[1].reshape(STEPS, 8, LANES)
+    faces[:, 1 - near, :, LANES : 2 * LANES] = jnp.zeros((STEPS, 8, LANES), F32)
+    faces[:, :, :, 2 * LANES : 3 * LANES] = unpack(from_next[...]).reshape(STEPS, 2, 8, LANES)
+    faces[:, :, :, 3 * LANES :] = unpack(from_chip[...]).reshape(STEPS, 2, 8, LANES)
+    coupled = dot_columns(split(faces[...].reshape(ROWS, wide)), (lift_h[:wide], lift_l[:wide]))
+    out[...] = (base[...] - coupled).reshape(STEPS, 2, 8, NB)
+
+
+def corrected(place, from_odd, base, lift_h, lift_l, modes):
+    near = 1 - (place[1] & 1)
+    rows = slice(LANES, 2 * LANES)
+    coupled = dot_columns(split(unpack(from_odd[...])), (lift_h[rows], lift_l[rows]))
+    modes[:, near] = base[:, near]
+    modes[:, 1 - near] = base[:, 1 - near] - coupled.reshape(STEPS, 8, NB)
+    return modes[...].reshape(ROWS, NB)
 
 
 def sweep_kernel(
-    place, from_chip, from_next, from_even, from_odd, modal, inner,
-    first_set, second_set, factors,
-    inner_out, to_chip, to_next, to_even, to_odd,
+    place, from_odd, base, first_set, second_set, factors,
+    solved_h, solved_l, inner_out, to_chip, to_next, to_even, to_odd, modes, traces,
 ):
     _, _, trace_h, trace_l = first_weights(first_set)
     lift_h, lift_l, _, _ = second_weights(second_set)
-    faces = split(gathered(place, inner, from_chip, from_next, from_even, from_odd))
-    corrected = modal[...] - dot3(faces, (lift_h[...], lift_l[...]), NN)
-    solved = split(divided(corrected, factors))
-    traces = dot3(solved, (trace_h[...], trace_l[...]), NT)
-    send_traces(place, traces, inner_out, to_chip, to_next, to_even, to_odd)
-
-
-def last_kernel(
-    place, from_chip, from_next, from_even, from_odd, modal, inner,
-    second_set, factors,
-    steps, spectrum,
-):
+    solved = split(divided(corrected(place, from_odd, base, lift_h, lift_l, modes), factors))
+    send_traces(
+        place, solved, trace_h, trace_l, traces, solved_h, solved_l, inner_out, to_chip, to_next, to_even, to_odd
+    )
+
+
+def last_kernel(place, from_odd, base, second_set, factors, steps, modes, spectrum):
     lift_h, lift_l, out_h, out_l = second_weights(second_set)
-    faces = split(gathered(place, inner, from_chip, from_next, from_even, from_odd))
-    corrected = modal[...] - dot3(faces, (lift_h[...], lift_l[...]), NN)
-    solved = split(divided(corrected, factors))
-    spectrum[...] = dot3(solved, (out_h[...], out_l[...]), NT)
+    solved = split(divided(corrected(place, from_odd, base, lift_h, lift_l, modes), factors))
+    spectrum[...] = dot_rows(solved, (out_h[...], out_l[...]))
     to_steps(spectrum, steps)
 
 
-def restore_kernel(arrived, order, out):
+def restore_kernel(arrived, order, far, out, done):
+    copies = [pltpu.make_async_copy(out.at[step], far.at[step], done.at[step]) for step in range(2)]
     for step in range(2):
         values = arrived[:, step * 16 : step * 16 + 16, :].reshape(SLAB, NB)
         high, low = split(values)
         picks = order[...]
         out[step] = dot(high, picks, TN) + dot(low, picks, TN)
+        copies[step].start()
+    for copy in copies:
+        copy.wait()
 
 
 SMEM = pl.BlockSpec(memory_space=pltpu.SMEM)
@@ -436,14 +468,16 @@
         + [(jnp.asarray(weight), VMEM) for weight in weights],
         prepared,
         2 * 5 * 384 * 384 * 768,
-        [pltpu.VMEM((2304, NB), BF16), pltpu.VMEM((6 * LANES, NB), F32), DMA],
+        [pltpu.VMEM((2304, NB), BF16), pltpu.VMEM((6 * LANES, NB), F32), pltpu.VMEM((6 * LANES, NB), BF16), DMA],
     )
 
     faces = (
-        [((ROWS, 4 * LANES), F32, KEPT)]
+        [((ROWS, NB), BF16, KEPT)] * 2
+        + [((2, HALF, LANES), F32, KEPT)]
         + [((ROWS * 3 // 4, LANES), F32, VMEM)] * 2
         + [((HALF * 3 // 4, LANES), F32, VMEM)] * 2
     )
+    face_scratch = pltpu.VMEM((STEPS, 2, 8, 4 * LANES), F32)
 
     def exchange(to_chip, to_next, to_even, to_odd):
         from_odd = lax.ppermute(to_odd, "space", ODD_SIDES)
@@ -452,36 +486,56 @@
         from_chip = lax.ppermute(to_chip, "tm", SAME_CHIP)
         return from_chip, from_next, from_even, from_odd
 
-    modal, inner, *outgoing = call(
+    def inside(solved_h, solved_l, inner, from_chip, from_next, from_even):
+        (base,) = call(
+            inside_kernel,
+            [(a, KEPT) for a in (modal, solved_h, solved_l, first_set)] + [(second_set, VMEM)],
+            [((ROWS, NB), F32, KEPT)],
+            2 * 3 * 512 * 384 * 512,
+        )
+        (base,) = call(
+            meet_kernel,
+            [place]
+            + [(a, VMEM) for a in (from_chip, from_next, from_even)]
+            + [(base, KEPT), (inner, KEPT), (second_set, VMEM)],
+            [((STEPS, 2, 8, NB), F32, KEPT)],
+            2 * 3 * 512 * 384 * 512,
+            [face_scratch],
+        )
+        return (base, KEPT)
+
+    modal, solved_h, solved_l, inner, *outgoing = call(
         first_kernel,
-        [place, (arrived, VMEM), (first_set, KEPT), (factors, KEPT)],
+        [place, (arrived, HBM), (first_set, KEPT), (factors, KEPT)],
         [((ROWS, NB), F32, KEPT)] + faces,
-        2 * 3 * 512 * 384 * (384 + 768),
-        [pltpu.VMEM((ROWS, NB), F32)],
-    )
-    incoming = exchange(*outgoing)
-    inner, *outgoing = call(
+        2 * 3 * 512 * 384 * (384 + 512),
+        [pltpu.VMEM((ROWS, NB), F32)] * 2 + [face_scratch, DMA((3,))],
+    )
+    *incoming, from_odd = exchange(*outgoing)
+    base = inside(solved_h, solved_l, inner, *incoming)
+    solved_h, solved_l, inner, *outgoing = call(
         sweep_kernel,
-        [place]
-        + [(a, VMEM) for a in incoming] + [(a, KEPT) for a in [modal, inner, first_set]] + [(second_set, VMEM), (factors, KEPT)],
+        [place, (from_odd, VMEM), base, (first_set, KEPT), (second_set, VMEM), (factors, KEPT)],
         faces,
-        2 * 3 * 512 * 384 * (768 + 768),
-    )
-    incoming = exchange(*outgoing)
+        2 * 3 * 512 * 384 * 512,
+        [pltpu.VMEM((STEPS, 2, 8, NB), F32), face_scratch],
+    )
+    *incoming, from_odd = exchange(*outgoing)
+    base = inside(solved_h, solved_l, inner, *incoming)
     (steps,) = call(
         last_kernel,
-        [place]
-        + [(a, VMEM) for a in incoming] + [(a, KEPT) for a in [modal, inner]] + [(second_set, VMEM), (factors, KEPT)],
+        [place, (from_odd, VMEM), base, (second_set, VMEM), (factors, KEPT)],
         [((ROWS, NB), F32, VMEM)],
-        2 * 3 * 512 * 384 * (768 + 384),
-        [pltpu.VMEM((ROWS, NB), F32)],
+        2 * 3 * 512 * 384 * 384,
+        [pltpu.VMEM((STEPS, 2, 8, NB), F32), pltpu.VMEM((ROWS, NB), F32)],
     )
     back = lax.all_to_all(steps.reshape(16, 32, NB), "tm", 0, 0, tiled=True)
     (out,) = call(
         restore_kernel,
         [(back, VMEM), (order, KEPT)],
-        [((2, NB, SLAB), F32, VMEM)],
+        [((2, NB, SLAB), F32, HBM)],
         2 * 4 * 256 * 256 * 384,
+        [pltpu.VMEM((2, NB, SLAB), F32), DMA((2,))],
     )
     return out
 

time: 88.1 us -> 85.2 us (0.967)
  waiting for transfers between devices: 19.2 us -> 13.8 us
  Pallas kernels: 23.3 us -> 25.9 us
    ppermute x2, waiting for transfers between devices: 8.58 us -> 4.23 us  [exchange(): from_even = lax.ppermute(to_even, 'space', EVEN_SIDES)]
    pallas_call x8 -> x12, Pallas kernels: 23.3 us -> 25.9 us  [call(): pl.pallas_call(body, out_shape=shapes, in_specs=[spec for _, spec in ins]...]
    ppermute x2, waiting for transfers between devices: 1.13 us -> 0.01 us  [exchange(): from_odd = lax.ppermute(to_odd, 'space', ODD_SIDES)]
  transfers between devices with their start and end apart: 10 -> 10, of which waited for: 5 -> 4; matrix products, arithmetic and copies ran while one was open for 0% -> 0% of each run, Pallas kernels for 7% -> 15%
where the time goes in v4:
time: 85.2 us; the launch traced here: 84.6 us
  Pallas kernels  25.9 us (30%)
  starting transfers between devices  20.7 us (24%)
  blocking collectives  19.4 us (23%)
  waiting for transfers between devices  13.8 us (16%)
  local copies, waits for them, and re-layouts  4.37 us (5%)
    pallas_call x12, Pallas kernels, call(): pl.pallas_call(body, out_shape=shapes, in_specs=[spec for _, spec in ins]...  25.9 us
    all_to_all x1, blocking collectives, shards(): back = lax.all_to_all(steps.reshape(16, 32, NB), 'tm', 0, 0, tiled=True)  19.4 us
    all_to_all x1, starting transfers between devices, shards(): arrived = lax.all_to_all(sent, 'tm', 0, 0, tiled=True).reshape(ROWS, NB)  7.85 us
    all_to_all x1, waiting for transfers between devices, shards(): arrived = lax.all_to_all(sent, 'tm', 0, 0, tiled=True).reshape(ROWS, NB)  7.05 us
    ppermute x2, starting transfers between devices, exchange(): from_odd = lax.ppermute(to_odd, 'space', ODD_SIDES)  6.68 us
    unnamed x14, local copies, waits for them, and re-layouts  4.36 us
    ppermute x2, waiting for transfers between devices, exchange(): from_even = lax.ppermute(to_even, 'space', EVEN_SIDES)  4.23 us
    all_to_all x1, starting transfers between devices, shards(): lax.all_to_all(table, 'space', 0, 0, tiled=True, axis_index_groups=[[0, 1...  3.49 us
  transfers between devices with their start and end apart: 10, of which 4 were waited for; matrix products, arithmetic and copies ran while one was open for 0% of the time, Pallas kernels for 15%

profile of v4, /device:TPU:4, one launch (start us, length us, event | category | flops | bytes accessed | tf_op | source)
XLA Modules:
  0.0 84.6 jit_solution(2134591373039347815)
XLA Ops:
  0.0 0.1 pad_add_fusion.place
  0.1 1.9 %shard_map.92 = s32[4,8,128]{2,1,0:T(8,128)} custom-call(s32[2]{0:T(128)S(1)} %pad_add_fusion.place, s32[6,256]{1,0:T(8,128)} %nbr_far.3, s32[2,128]{1,0:T(2,128)} %halo_far.3), custom_call_target="tpu_custom_call" | custom-call | flops 10000 | bytes 23560 | tf_op jit(solution)/shard_map/pallas_call | solution.py:420
  2.0 3.5 %all-to-all-start = ((s32[4,8,128]{2,1,0:T(8,128)}), s32[4,8,128]{2,1,0:T(8,128)S(1)}, u32[]{:S(2)}, u32[]{:S(2)}) async-start(s32[4,8,128]{2,1,0:T(8,128)} %shard_map.92), calls=%async_computation | async-start | bytes 32768 | tf_op jit(solution)/shard_map/all_to_all | solution.py:440
  5.4 2.2 %shard_map.91 = (f32[2,32,8,384]{3,2,1,0:T(8,128)S(1)}, f32[32,8,256]{2,1,0:T(8,128)S(1)}, s32[256]{0:T(256)S(1)}) custom-call(s32[6,256]{1,0:T(8,128)} %nbr_far.3, s32[2,128]{1,0:T(2,128)} %halo_far.3, f32[2,384,256]{2,1,0:T(8,128)} %rhs_far.1), custom_call_target="tpu_custom_call" | custom-call | flops 201326592 | bytes 1843200 | tf_op jit(solution)/shard_map/pallas_call | solution.py:420
  7.7 2.5 %all-to-all-done = s32[4,8,128]{2,1,0:T(8,128)S(1)} async-done(((s32[4,8,128]{2,1,0:T(8,128)}), s32[4,8,128]{2,1,0:T(8,128)S(1)}, u32[]{:S(2)}, u32[]{:S(2)}) %all-to-all-start) | async-done | bytes 16416 | tf_op jit(solution)/shard_map/all_to_all | solution.py:440
  10.2 2.5 %shard_map.93 = (f32[16,32,384]{2,1,0:T(8,128)}, s32[2]{0:T(128)S(1)}) custom-call(s32[2]{0:T(128)S(1)} %pad_add_fusion.place, s32[256]{0:T(256)S(1)} %get-tuple-element.29.spot, f32[2,32,8,384]{3,2,1,0:T(8,128)S(1)} %get-tuple-element.30.placed, s32[32,128]{1,0:T(8,128)S(1)} %bitcast.8), custom_call_target="tpu_custom_call" | custom-call | flops 1000000 | bytes 1590288 | tf_op jit(solution)/shard_map/pallas_call | solution.py:420
  12.7 7.9 %all-to-all-start.1 = ((f32[16,32,384]{2,1,0:T(8,128)}), f32[16,32,384]{2,1,0:T(8,128)}, u32[]{:S(2)}, u32[]{:S(2)}) async-start(f32[16,32,384]{2,1,0:T(8,128)} %get-tuple-element.31), calls=%async_computation.1 | async-start | bytes 1572864 | tf_op jit(solution)/shard_map/all_to_all | solution.py:462
  20.6 0.0 copy-start.1
  20.6 1.2 %copy-done.1 = f32[6,384,96]{1,2,0:T(8,128)S(1)} copy-done((f32[6,384,96]{1,2,0:T(8,128)S(1)}, f32[6,384,96]{1,2,0:T(8,128)}, u32[]{:S(2)}) %copy-start.1) | copy-done | bytes 884760
  21.7 1.1 %copy-done.2 = f32[384,384]{1,0:T(8,128)S(1)} copy-done((f32[384,384]{1,0:T(8,128)S(1)}, f32[384,384]{1,0:T(8,128)}, u32[]{:S(2)}) %copy-start.2) | copy-done | bytes 589848
  22.8 1.1 %copy-done.3 = f32[384,384]{1,0:T(8,128)S(1)} copy-done((f32[384,384]{1,0:T(8,128)S(1)}, f32[384,384]{1,0:T(8,128)}, u32[]{:S(2)}) %copy-start.3) | copy-done | bytes 589848
  23.9 1.1 %copy-done.5 = bf16[768,384]{1,0:T(8,128)(2,1)S(1)} copy-done((bf16[768,384]{1,0:T(8,128)(2,1)S(1)}, bf16[768,384]{1,0:T(8,128)(2,1)}, u32[]{:S(2)}) %copy-start.5) | copy-done | bytes 589848
  24.9 3.8 %shard_map.94 = (bf16[256,256]{1,0:T(8,128)(2,1)S(1)}, bf16[2304,384]{1,0:T(8,128)(2,1)S(1)}, f32[3,256,384]{2,1,0:T(8,128)S(1)}, bf16[2304,384]{1,0:T(8,128)(2,1)}) custom-call(s32[2]{0:T(128)S(1)} %pad_add_fusion.place, s32[2]{0:T(128)S(1)} %get-tuple-element.32.shift, f32[32,8,256]{2,1,0:T(8,128)S(1)} %get-tuple-element.33.placed_order, ...), custom_call_target="tpu_custom_call" | custom-call | flops 1132462080 | bytes 7768592 | tf_op jit(solution)/shard_map/pallas_call | solution.py:420
  28.7 7.1 %all-to-all-done.1 = f32[16,32,384]{2,1,0:T(8,128)} async-done(((f32[16,32,384]{2,1,0:T(8,128)}), f32[16,32,384]{2,1,0:T(8,128)}, u32[]{:S(2)}, u32[]{:S(2)}) %all-to-all-start.1) | async-done | bytes 786464 | tf_op jit(solution)/shard_map/all_to_all | solution.py:462
  35.8 3.7 %shard_map.95 = (f32[512,384]{1,0:T(8,128)S(1)}, bf16[512,384]{1,0:T(8,128)(2,1)S(1)}, bf16[512,384]{1,0:T(8,128)(2,1)S(1)}, f32[2,256,128]{2,1,0:T(8,128)S(1)},...) custom-call(s32[2]{0:T(128)S(1)} %pad_add_fusion.place, ...), custom_call_target="tpu_custom_call" | custom-call | flops 1056964608 | bytes 6160392 | tf_op jit(solution)/shard_map/pallas_call | solution.py:420
  39.5 0.1 collective-permute-start.1
  39.6 0.9 %collective-permute-start.2 = (f32[384,128]{1,0:T(8,128)S(1)}, f32[384,128]{1,0:T(8,128)S(1)}, u32[]{:S(2)}, u32[]{:S(2)}) collective-permute-start(f32[384,128]{1,0:T(8,128)S(1)} %get-tuple-element.38), channel_id=1, source_target_pairs={{8,32},{40,64},{72,96},{104,112},{120,80},{88,48},{56,16},{24,0},{... | collective-permute-start | bytes 589832 | tf_op jit(solution)/shard_map/ppermute | solution.py:485
  40.5 0.0 collective-permute-start.3
  40.5 3.2 %collective-permute-start = (f32[192,128]{1,0:T(8,128)S(1)}, f32[192,128]{1,0:T(8,128)S(1)}, u32[]{:S(2)}, u32[]{:S(2)}) collective-permute-start(f32[192,128]{1,0:T(8,128)S(1)} %get-tuple-element.36), channel_id=1, source_target_pairs={{1,2},{2,1},{3,4},{4,3},{5,6},{6,5},{9,10},{10,9},{11,12},{12,11},... | collective-permute-start | bytes 294920 | tf_op jit(solution)/shard_map/ppermute | solution.py:483
  43.8 1.5 %shard_map.96.base = f32[512,384]{1,0:T(8,128)S(1)} custom-call(f32[512,384]{1,0:T(8,128)S(1)} %get-tuple-element.40.modal, bf16[512,384]{1,0:T(8,128)(2,1)S(1)} %get-tuple-element.41.solved_h, bf16[512,384]{1,0:T(8,128)(2,1)S(1)} %get-tuple-element.42.solved_l, bf16[2304,384]{1,0:T(8,128)(2,1)S(1)} %get-tuple-element.34.first_set, bf16[2304,384]{1,0:T(8,128)(2,1)S(1)} %copy-done), custom_call_target="tpu_custom_call" | custom-call | flops 603979776 | bytes 5898240 | tf_op jit(solution)/shard_map/pallas_call | solution.py:420
  45.3 3.1 %collective-permute-done.3.from_even = f32[192,128]{1,0:T(8,128)S(1)} collective-permute-done((f32[192,128]{1,0:T(8,128)S(1)}, f32[192,128]{1,0:T(8,128)S(1)}, u32[]{:S(2)}, u32[]{:S(2)}) %collective-permute-start.3) | collective-permute-done | bytes 98336 | tf_op jit(solution)/shard_map/ppermute | solution.py:484
  48.4 1.6 %shard_map.97.base = f32[32,2,8,384]{3,2,1,0:T(8,128)S(1)} custom-call(s32[2]{0:T(128)S(1)} %pad_add_fusion.place, f32[384,128]{1,0:T(8,128)S(1)} %collective-permute-done.1.from_chip, f32[384,128]{1,0:T(8,128)S(1)} %collective-permute-done.2.from_next, f32[192,128]{1,0:T(8,128)S(1)} %collective-permute-done.3.from_even, f32[512,384]{1,0:T(8,128)S(1)} %shard_map.96.base, ...), custom_call_target="tpu_custom_call" | custom-call | flops 603979776 | bytes 4096008 | tf_op jit(solution)/shard_map/pallas_call | solution.py:420
  50.1 2.2 %shard_map.98 = (bf16[512,384]{1,0:T(8,128)(2,1)S(1)}, bf16[512,384]{1,0:T(8,128)(2,1)S(1)}, f32[2,256,128]{2,1,0:T(8,128)S(1)}, f32[384,128]{1,0:T(8,128)S(1)},...) custom-call(s32[2]{0:T(128)S(1)} %pad_add_fusion.place, ...), custom_call_target="tpu_custom_call" | custom-call | flops 603979776 | bytes 7241736 | tf_op jit(solution)/shard_map/pallas_call | solution.py:420
  52.3 0.1 collective-permute-start.5
  52.4 1.6 %collective-permute-start.6 = (f32[384,128]{1,0:T(8,128)S(1)}, f32[384,128]{1,0:T(8,128)S(1)}, u32[]{:S(2)}, u32[]{:S(2)}) collective-permute-start(f32[384,128]{1,0:T(8,128)S(1)} %get-tuple-element.47), channel_id=1, source_target_pairs={{8,32},{40,64},{72,96},{104,112},{120,80},{88,48},{56,16},{24,0},{... | collective-permute-start | bytes 589832 | tf_op jit(solution)/shard_map/ppermute | solution.py:485
  53.9 3.4 %collective-permute-start.4 = (f32[192,128]{1,0:T(8,128)S(1)}, f32[192,128]{1,0:T(8,128)S(1)}, u32[]{:S(2)}, u32[]{:S(2)}) collective-permute-start(f32[192,128]{1,0:T(8,128)S(1)} %get-tuple-element.45), channel_id=1, source_target_pairs={{1,2},{2,1},{3,4},{4,3},{5,6},{6,5},{9,10},{10,9},{11,12},{12,11},... | collective-permute-start | bytes 294920 | tf_op jit(solution)/shard_map/ppermute | solution.py:483
  57.4 1.5 %shard_map.99.base = f32[512,384]{1,0:T(8,128)S(1)} custom-call(f32[512,384]{1,0:T(8,128)S(1)} %get-tuple-element.40.modal, bf16[512,384]{1,0:T(8,128)(2,1)S(1)} %get-tuple-element.49.solved_h, bf16[512,384]{1,0:T(8,128)(2,1)S(1)} %get-tuple-element.50.solved_l, bf16[2304,384]{1,0:T(8,128)(2,1)S(1)} %get-tuple-element.34.first_set, bf16[2304,384]{1,0:T(8,128)(2,1)S(1)} %copy-done), custom_call_target="tpu_custom_call" | custom-call | flops 603979776 | bytes 5898240 | tf_op jit(solution)/shard_map/pallas_call | solution.py:420
  58.9 1.2 %collective-permute-done.7.from_even = f32[192,128]{1,0:T(8,128)S(1)} collective-permute-done((f32[192,128]{1,0:T(8,128)S(1)}, f32[192,128]{1,0:T(8,128)S(1)}, u32[]{:S(2)}, u32[]{:S(2)}) %collective-permute-start.7) | collective-permute-done | bytes 98336 | tf_op jit(solution)/shard_map/ppermute | solution.py:484
  60.1 1.6 %shard_map.100.base = f32[32,2,8,384]{3,2,1,0:T(8,128)S(1)} custom-call(s32[2]{0:T(128)S(1)} %pad_add_fusion.place, f32[384,128]{1,0:T(8,128)S(1)} %collective-permute-done.5.from_chip, f32[384,128]{1,0:T(8,128)S(1)} %collective-permute-done.6.from_next, f32[192,128]{1,0:T(8,128)S(1)} %collective-permute-done.7.from_even, f32[512,384]{1,0:T(8,128)S(1)} %shard_map.99.base, ...), custom_call_target="tpu_custom_call" | custom-call | flops 603979776 | bytes 4096008 | tf_op jit(solution)/shard_map/pallas_call | solution.py:420
  61.8 2.0 %shard_map.101 = f32[512,384]{1,0:T(8,128)S(1)} custom-call(s32[2]{0:T(128)S(1)} %pad_add_fusion.place, f32[192,128]{1,0:T(8,128)S(1)} %collective-permute-done.4.from_odd, f32[32,2,8,384]{3,2,1,0:T(8,128)S(1)} %shard_map.100.base, bf16[2304,384]{1,0:T(8,128)(2,1)S(1)} %copy-done, f32[3,256,384]{2,1,0:T(8,128)S(1)} %get-tuple-element.35.factors), custom_call_target="tpu_custom_call" | custom-call | flops 452984832 | bytes 4620296 | tf_op jit(solution)/shard_map/pallas_call | solution.py:420
  63.8 19.4 %all_to_all.15.arrived = f32[16,32,384]{2,1,0:T(8,128)S(1)} all-to-all(f32[16,32,384]{2,1,0:T(8,128)S(1)} %bitcast.7), channel_id=1, replica_groups=mesh['tm'=16,'space'=8] {'tm'}, dimensions={0} | all-to-all | bytes 1572864 | tf_op jit(solution)/shard_map/all_to_all | solution.py:532
  83.2 1.3 %shard_map.102 = f32[2,384,256]{2,1,0:T(8,128)} custom-call(f32[16,32,384]{2,1,0:T(8,128)S(1)} %all_to_all.15.arrived, bf16[256,256]{1,0:T(8,128)(2,1)S(1)} %get-tuple-element.52.order), custom_call_target="tpu_custom_call" | custom-call | flops 201326592 | bytes 1703936 | tf_op jit(solution)/shard_map/pallas_call | solution.py:420
  (17 shorter events, 0.0 us)
Async XLA Ops:
  0.0 20.5 %copy-start.6 = (f32[384]{0:T(512)S(1)}, f32[384]{0:T(512)}, u32[]{:S(2)}) copy-start(f32[384]{0:T(512)} %param.11) | copy-start | bytes 4612
  0.0 20.6 %copy-start.4 = (f32[256]{0:T(256)S(1)}, f32[256]{0:T(256)}, u32[]{:S(2)}) copy-start(f32[256]{0:T(256)} %param.10) | copy-start | bytes 3076
  2.0 8.2 %all-to-all-start = ((s32[4,8,128]{2,1,0:T(8,128)}), s32[4,8,128]{2,1,0:T(8,128)S(1)}, u32[]{:S(2)}, u32[]{:S(2)}) async-start(s32[4,8,128]{2,1,0:T(8,128)} %shard_map.92), calls=%async_computation | async-start | bytes 32768 | tf_op jit(solution)/shard_map/all_to_all | solution.py:440
  12.7 23.1 %all-to-all-start.1 = ((f32[16,32,384]{2,1,0:T(8,128)}), f32[16,32,384]{2,1,0:T(8,128)}, u32[]{:S(2)}, u32[]{:S(2)}) async-start(f32[16,32,384]{2,1,0:T(8,128)} %get-tuple-element.31), calls=%async_computation.1 | async-start | bytes 1572864 | tf_op jit(solution)/shard_map/all_to_all | solution.py:462
  20.6 1.2 %copy-start.1 = (f32[6,384,96]{1,2,0:T(8,128)S(1)}, f32[6,384,96]{1,2,0:T(8,128)}, u32[]{:S(2)}) copy-start(f32[6,384,96]{1,2,0:T(8,128)} %param.14) | copy-start | bytes 2654212
  21.7 1.1 %copy-start.2 = (f32[384,384]{1,0:T(8,128)S(1)}, f32[384,384]{1,0:T(8,128)}, u32[]{:S(2)}) copy-start(f32[384,384]{1,0:T(8,128)} %modes_in.1) | copy-start | bytes 1769476
  22.8 1.1 %copy-start.3 = (f32[384,384]{1,0:T(8,128)S(1)}, f32[384,384]{1,0:T(8,128)}, u32[]{:S(2)}) copy-start(f32[384,384]{1,0:T(8,128)} %modes_out.1) | copy-start | bytes 1769476
  23.9 1.1 %copy-start.5 = (bf16[768,384]{1,0:T(8,128)(2,1)S(1)}, bf16[768,384]{1,0:T(8,128)(2,1)}, u32[]{:S(2)}) copy-start(bf16[768,384]{1,0:T(8,128)(2,1)} %constant.11.clone.pick) | copy-start | bytes 1769476
  35.8 8.0 %copy-start = (bf16[2304,384]{1,0:T(8,128)(2,1)S(1)}, bf16[2304,384]{1,0:T(8,128)(2,1)}, u32[]{:S(2)}) copy-start(bf16[2304,384]{1,0:T(8,128)(2,1)} %get-tuple-element.43.second_set) | copy-start | bytes 5308420
  39.5 8.9 %collective-permute-start.1 = (f32[384,128]{1,0:T(8,128)S(1)}, f32[384,128]{1,0:T(8,128)S(1)}, u32[]{:S(2)}, u32[]{:S(2)}) collective-permute-start(f32[384,128]{1,0:T(8,128)S(1)} %get-tuple-element.37), channel_id=1, source_target_pairs={{0,8},{8,0},{16,24},{24,16},{32,40},{40,32},{48,56},{56,48},{64,72... | collective-permute-start | bytes 589832 | tf_op jit(solution)/shard_map/ppermute | solution.py:486
  39.6 8.8 %collective-permute-start.2 = (f32[384,128]{1,0:T(8,128)S(1)}, f32[384,128]{1,0:T(8,128)S(1)}, u32[]{:S(2)}, u32[]{:S(2)}) collective-permute-start(f32[384,128]{1,0:T(8,128)S(1)} %get-tuple-element.38), channel_id=1, source_target_pairs={{8,32},{40,64},{72,96},{104,112},{120,80},{88,48},{56,16},{24,0},{... | collective-permute-start | bytes 589832 | tf_op jit(solution)/shard_map/ppermute | solution.py:485
  40.5 7.9 %collective-permute-start.3 = (f32[192,128]{1,0:T(8,128)S(1)}, f32[192,128]{1,0:T(8,128)S(1)}, u32[]{:S(2)}, u32[]{:S(2)}) collective-permute-start(f32[192,128]{1,0:T(8,128)S(1)} %get-tuple-element.39), channel_id=1, source_target_pairs={{0,1},{1,0},{2,3},{3,2},{4,5},{5,4},{6,7},{7,6},{8,9},{9,8},{10,11... | collective-permute-start | bytes 294920 | tf_op jit(solution)/shard_map/ppermute | solution.py:484
  40.5 9.5 %collective-permute-start = (f32[192,128]{1,0:T(8,128)S(1)}, f32[192,128]{1,0:T(8,128)S(1)}, u32[]{:S(2)}, u32[]{:S(2)}) collective-permute-start(f32[192,128]{1,0:T(8,128)S(1)} %get-tuple-element.36), channel_id=1, source_target_pairs={{1,2},{2,1},{3,4},{4,3},{5,6},{6,5},{9,10},{10,9},{11,12},{12,11},... | collective-permute-start | bytes 294920 | tf_op jit(solution)/shard_map/ppermute | solution.py:483
  52.3 7.8 %collective-permute-start.5 = (f32[384,128]{1,0:T(8,128)S(1)}, f32[384,128]{1,0:T(8,128)S(1)}, u32[]{:S(2)}, u32[]{:S(2)}) collective-permute-start(f32[384,128]{1,0:T(8,128)S(1)} %get-tuple-element.46), channel_id=1, source_target_pairs={{0,8},{8,0},{16,24},{24,16},{32,40},{40,32},{48,56},{56,48},{64,72... | collective-permute-start | bytes 589832 | tf_op jit(solution)/shard_map/ppermute | solution.py:486
  52.4 7.8 %collective-permute-start.6 = (f32[384,128]{1,0:T(8,128)S(1)}, f32[384,128]{1,0:T(8,128)S(1)}, u32[]{:S(2)}, u32[]{:S(2)}) collective-permute-start(f32[384,128]{1,0:T(8,128)S(1)} %get-tuple-element.47), channel_id=1, source_target_pairs={{8,32},{40,64},{72,96},{104,112},{120,80},{88,48},{56,16},{24,0},{... | collective-permute-start | bytes 589832 | tf_op jit(solution)/shard_map/ppermute | solution.py:485
  53.9 6.2 %collective-permute-start.7 = (f32[192,128]{1,0:T(8,128)S(1)}, f32[192,128]{1,0:T(8,128)S(1)}, u32[]{:S(2)}, u32[]{:S(2)}) collective-permute-start(f32[192,128]{1,0:T(8,128)S(1)} %get-tuple-element.48), channel_id=1, source_target_pairs={{0,1},{1,0},{2,3},{3,2},{4,5},{5,4},{6,7},{7,6},{8,9},{9,8},{10,11... | collective-permute-start | bytes 294920 | tf_op jit(solution)/shard_map/ppermute | solution.py:484
  53.9 7.8 %collective-permute-start.4 = (f32[192,128]{1,0:T(8,128)S(1)}, f32[192,128]{1,0:T(8,128)S(1)}, u32[]{:S(2)}, u32[]{:S(2)}) collective-permute-start(f32[192,128]{1,0:T(8,128)S(1)} %get-tuple-element.45), channel_id=1, source_target_pairs={{1,2},{2,1},{3,4},{4,3},{5,6},{6,5},{9,10},{10,9},{11,12},{12,11},... | collective-permute-start | bytes 294920 | tf_op jit(solution)/shard_map/ppermute | solution.py:483

commit v5 on v4

--- a/solution.py
+++ b/solution.py
@@ -80,10 +80,8 @@
             yield lambda row: (slice(row * SHEET + block * 8, row * SHEET + block * 8 + 8), slice(lane, lane + LANES))
 
 
-def to_frequencies(steps, spectrum, copies):
-    for place, at in enumerate(tiles()):
-        if place % 2 == 0:
-            copies[place // 2].wait()
+def to_frequencies(steps, spectrum):
+    for at in tiles():
         freqs = real_fft([steps[at(n)] * DECAY**n for n in range(STEPS)])
         for freq in range(16):
             spectrum[at(freq)] = freqs[freq][0]
@@ -240,7 +238,7 @@
 
 
 def prepare_kernel(place, shift, placed_order, material, modes_in, modes_out, face_lift, rates, pick, *refs):
-    order, first_set, factors, second_far, second_set, lift, sorted_pick, done = refs
+    order, first_set, factors_far, second_far, second_set, factors, lift, sorted_pick, done = refs
     in_h, in_l, trace_h, trace_l = first_weights(first_set)
     lift_h, lift_l, out_h, out_l = second_weights(second_set)
     same_r, same_i, cross = factors.at[0], factors.at[1], factors.at[2]
@@ -268,13 +266,16 @@
         same_r[rows, :] = same
         same_i[rows, :] = same if freq else 1.0 / ((1.0 + DECAY) * own + rates[...])
         cross[rows, :] = imag / size
+    factors_copy = pltpu.make_async_copy(factors, factors_far, done.at[0])
+    factors_copy.start()
     lift[...] = jnp.zeros_like(lift)
     for at, face in enumerate(face_order(place)):
         lift[at * LANES : at * LANES + NFT, :] = face_lift[face]
     lift_h[...], lift_l[...] = split(dot_rows(split(lift[...]), in_parts))
-    copy = pltpu.make_async_copy(second_set, second_far, done)
+    copy = pltpu.make_async_copy(second_set, second_far, done.at[1])
     copy.start()
     copy.wait()
+    factors_copy.wait()
 
 
 def divided(modal, factors):
@@ -318,19 +319,16 @@
 
 
 def first_kernel(
-    place, far, first_set, factors,
-    modal, solved_h, solved_l, inner, to_chip, to_next, to_even, to_odd, steps, spectrum, traces, done,
+    place, steps, first_set, factors_far,
+    modal, solved_h, solved_l, inner, to_chip, to_next, to_even, to_odd, spectrum, traces, factors, done,
 ):
-    lanes = [slice(lane, lane + LANES) for lane in range(0, NB, LANES)]
-    copies = [
-        pltpu.make_async_copy(far.at[:, lane], steps.at[:, lane], done.at[at]) for at, lane in enumerate(lanes)
-    ]
-    for copy in copies:
-        copy.start()
+    factors_copy = pltpu.make_async_copy(factors_far, factors, done)
+    factors_copy.start()
     in_h, in_l, trace_h, trace_l = first_weights(first_set)
-    to_frequencies(steps, spectrum, copies)
+    to_frequencies(steps, spectrum)
     start = dot_rows(split(spectrum[...]), (in_h[...], in_l[...]))
     modal[...] = start
+    factors_copy.wait()
     solved = split(divided(start, factors))
     send_traces(
         place, solved, trace_h, trace_l, traces, solved_h, solved_l, inner, to_chip, to_next, to_even, to_odd
@@ -461,14 +459,14 @@
     )
     arrived = lax.all_to_all(sent, "tm", 0, 0, tiled=True).reshape(ROWS, NB)
     weights = [modes_in, modes_out, jnp.swapaxes(face_lift, 1, 2), modal_rates.reshape(1, NB), trace_rows()]
-    prepared = [((SLAB, SLAB), BF16, KEPT), ((2304, NB), BF16, KEPT), ((3, HALF, NB), F32, KEPT), ((2304, NB), BF16, HBM)]
+    prepared = [((SLAB, SLAB), BF16, KEPT), ((2304, NB), BF16, KEPT), ((3, HALF, NB), F32, HBM), ((2304, NB), BF16, HBM)]
     order, first_set, factors, second_set = call(
         prepare_kernel,
         [place, (shift, SMEM), (placed_order, KEPT), (material.reshape(1, SLAB), VMEM)]
         + [(jnp.asarray(weight), VMEM) for weight in weights],
         prepared,
         2 * 5 * 384 * 384 * 768,
-        [pltpu.VMEM((2304, NB), BF16), pltpu.VMEM((6 * LANES, NB), F32), pltpu.VMEM((6 * LANES, NB), BF16), DMA],
+        [pltpu.VMEM((2304, NB), BF16), pltpu.VMEM((3, HALF, NB), F32), pltpu.VMEM((6 * LANES, NB), F32), pltpu.VMEM((6 * LANES, NB), BF16), DMA((2,))],
     )
 
     faces = (
@@ -506,16 +504,16 @@
 
     modal, solved_h, solved_l, inner, *outgoing = call(
         first_kernel,
-        [place, (arrived, HBM), (first_set, KEPT), (factors, KEPT)],
+        [place, (arrived, VMEM), (first_set, KEPT), (factors, HBM)],
         [((ROWS, NB), F32, KEPT)] + faces,
         2 * 3 * 512 * 384 * (384 + 512),
-        [pltpu.VMEM((ROWS, NB), F32)] * 2 + [face_scratch, DMA((3,))],
+        [pltpu.VMEM((ROWS, NB), F32), face_scratch, pltpu.VMEM((3, HALF, NB), F32), DMA],
     )
     *incoming, from_odd = exchange(*outgoing)
     base = inside(solved_h, solved_l, inner, *incoming)
     solved_h, solved_l, inner, *outgoing = call(
         sweep_kernel,
-        [place, (from_odd, VMEM), base, (first_set, KEPT), (second_set, VMEM), (factors, KEPT)],
+        [place, (from_odd, VMEM), base, (first_set, KEPT), (second_set, VMEM), (factors, VMEM)],
         faces,
         2 * 3 * 512 * 384 * 512,
         [pltpu.VMEM((STEPS, 2, 8, NB), F32), face_scratch],
@@ -524,7 +522,7 @@
     base = inside(solved_h, solved_l, inner, *incoming)
     (steps,) = call(
         last_kernel,
-        [place, (from_odd, VMEM), base, (second_set, VMEM), (factors, KEPT)],
+        [place, (from_odd, VMEM), base, (second_set, VMEM), (factors, VMEM)],
         [((ROWS, NB), F32, VMEM)],
         2 * 3 * 512 * 384 * 384,
         [pltpu.VMEM((STEPS, 2, 8, NB), F32), pltpu.VMEM((ROWS, NB), F32)],

time: 85.2 us -> 84.4 us (level)
  local copies, waits for them, and re-layouts: 4.37 us -> 3.31 us
    unnamed x14 -> x16, local copies, waits for them, and re-layouts: 4.36 us -> 3.31 us
where the time goes in v5:
time: 84.4 us; the launch traced here: 83.9 us
  Pallas kernels  25.6 us (30%)
  starting transfers between devices  20.7 us (25%)
  blocking collectives  19.4 us (23%)
  waiting for transfers between devices  14.4 us (17%)
  local copies, waits for them, and re-layouts  3.31 us (4%)
    pallas_call x12, Pallas kernels, call(): pl.pallas_call(body, out_shape=shapes, in_specs=[spec for _, spec in ins]...  25.6 us
    all_to_all x1, blocking collectives, shards(): back = lax.all_to_all(steps.reshape(16, 32, NB), 'tm', 0, 0, tiled=True)  19.4 us
    all_to_all x1, starting transfers between devices, shards(): arrived = lax.all_to_all(sent, 'tm', 0, 0, tiled=True).reshape(ROWS, NB)  7.81 us
    all_to_all x1, waiting for transfers between devices, shards(): arrived = lax.all_to_all(sent, 'tm', 0, 0, tiled=True).reshape(ROWS, NB)  7.7 us
    ppermute x2, starting transfers between devices, exchange(): from_odd = lax.ppermute(to_odd, 'space', ODD_SIDES)  6.68 us
    ppermute x2, waiting for transfers between devices, exchange(): from_even = lax.ppermute(to_even, 'space', EVEN_SIDES)  4.23 us
    all_to_all x1, starting transfers between devices, shards(): lax.all_to_all(table, 'space', 0, 0, tiled=True, axis_index_groups=[[0, 1...  3.49 us
    unnamed x16, local copies, waits for them, and re-layouts  3.31 us
  transfers between devices with their start and end apart: 10, of which 4 were waited for; matrix products, arithmetic and copies ran while one was open for 0% of the time, Pallas kernels for 15%

profile of v5, /device:TPU:4, one launch (start us, length us, event | category | flops | bytes accessed | tf_op | source)
XLA Modules:
  0.0 83.9 jit_solution(3401085968582927403)
XLA Ops:
  0.0 0.1 pad_add_fusion.place
  0.1 1.9 %shard_map.92 = s32[4,8,128]{2,1,0:T(8,128)} custom-call(s32[2]{0:T(128)S(1)} %pad_add_fusion.place, s32[6,256]{1,0:T(8,128)} %nbr_far.3, s32[2,128]{1,0:T(2,128)} %halo_far.3), custom_call_target="tpu_custom_call" | custom-call | flops 10000 | bytes 23560 | tf_op jit(solution)/shard_map/pallas_call | solution.py:418
  2.0 3.5 %all-to-all-start = ((s32[4,8,128]{2,1,0:T(8,128)}), s32[4,8,128]{2,1,0:T(8,128)S(1)}, u32[]{:S(2)}, u32[]{:S(2)}) async-start(s32[4,8,128]{2,1,0:T(8,128)} %shard_map.92), calls=%async_computation | async-start | bytes 32768 | tf_op jit(solution)/shard_map/all_to_all | solution.py:438
  5.5 2.2 %shard_map.91 = (f32[2,32,8,384]{3,2,1,0:T(8,128)S(1)}, f32[32,8,256]{2,1,0:T(8,128)S(1)}, s32[256]{0:T(256)S(1)}) custom-call(s32[6,256]{1,0:T(8,128)} %nbr_far.3, s32[2,128]{1,0:T(2,128)} %halo_far.3, f32[2,384,256]{2,1,0:T(8,128)} %rhs_far.1), custom_call_target="tpu_custom_call" | custom-call | flops 201326592 | bytes 1843200 | tf_op jit(solution)/shard_map/pallas_call | solution.py:418
  7.7 2.5 %all-to-all-done = s32[4,8,128]{2,1,0:T(8,128)S(1)} async-done(((s32[4,8,128]{2,1,0:T(8,128)}), s32[4,8,128]{2,1,0:T(8,128)S(1)}, u32[]{:S(2)}, u32[]{:S(2)}) %all-to-all-start) | async-done | bytes 16416 | tf_op jit(solution)/shard_map/all_to_all | solution.py:438
  10.2 2.5 %shard_map.93 = (f32[16,32,384]{2,1,0:T(8,128)}, s32[2]{0:T(128)S(1)}) custom-call(s32[2]{0:T(128)S(1)} %pad_add_fusion.place, s32[256]{0:T(256)S(1)} %get-tuple-element.29.spot, f32[2,32,8,384]{3,2,1,0:T(8,128)S(1)} %get-tuple-element.30.placed, s32[32,128]{1,0:T(8,128)S(1)} %bitcast.9), custom_call_target="tpu_custom_call" | custom-call | flops 1000000 | bytes 1590288 | tf_op jit(solution)/shard_map/pallas_call | solution.py:418
  12.7 7.8 %all-to-all-start.1 = ((f32[16,32,384]{2,1,0:T(8,128)}), f32[16,32,384]{2,1,0:T(8,128)S(1)}, u32[]{:S(2)}, u32[]{:S(2)}) async-start(f32[16,32,384]{2,1,0:T(8,128)} %get-tuple-element.31), calls=%async_computation.1 | async-start | bytes 1572864 | tf_op jit(solution)/shard_map/all_to_all | solution.py:460
  20.5 0.0 copy-start.2
  20.6 1.2 %copy-done.2 = f32[6,384,96]{1,2,0:T(8,128)S(1)} copy-done((f32[6,384,96]{1,2,0:T(8,128)S(1)}, f32[6,384,96]{1,2,0:T(8,128)}, u32[]{:S(2)}) %copy-start.2) | copy-done | bytes 884760
  21.7 1.1 %copy-done.4 = f32[384,384]{1,0:T(8,128)S(1)} copy-done((f32[384,384]{1,0:T(8,128)S(1)}, f32[384,384]{1,0:T(8,128)}, u32[]{:S(2)}) %copy-start.4) | copy-done | bytes 589848
  22.8 1.1 %copy-done.6 = bf16[768,384]{1,0:T(8,128)(2,1)S(1)} copy-done((bf16[768,384]{1,0:T(8,128)(2,1)S(1)}, bf16[768,384]{1,0:T(8,128)(2,1)}, u32[]{:S(2)}) %copy-start.6) | copy-done | bytes 589848
  23.8 4.1 %shard_map.94 = (bf16[256,256]{1,0:T(8,128)(2,1)S(1)}, bf16[2304,384]{1,0:T(8,128)(2,1)S(1)}, f32[3,256,384]{2,1,0:T(8,128)}, bf16[2304,384]{1,0:T(8,128)(2,1)}) custom-call(s32[2]{0:T(128)S(1)} %pad_add_fusion.place, s32[2]{0:T(128)S(1)} %get-tuple-element.32.shift, f32[32,8,256]{2,1,0:T(8,128)S(1)} %get-tuple-element.33.placed_order, ...), custom_call_target="tpu_custom_call" | custom-call | flops 1132462080 | bytes 7768592 | tf_op jit(solution)/shard_map/pallas_call | solution.py:418
  28.0 7.7 %all-to-all-done.1 = f32[16,32,384]{2,1,0:T(8,128)S(1)} async-done(((f32[16,32,384]{2,1,0:T(8,128)}), f32[16,32,384]{2,1,0:T(8,128)S(1)}, u32[]{:S(2)}, u32[]{:S(2)}) %all-to-all-start.1) | async-done | bytes 786464 | tf_op jit(solution)/shard_map/all_to_all | solution.py:460
  35.7 3.0 %shard_map.95 = (f32[512,384]{1,0:T(8,128)S(1)}, bf16[512,384]{1,0:T(8,128)(2,1)S(1)}, bf16[512,384]{1,0:T(8,128)(2,1)S(1)}, f32[2,256,128]{2,1,0:T(8,128)S(1)},...) custom-call(s32[2]{0:T(128)S(1)} %pad_add_fusion.place, ...), custom_call_target="tpu_custom_call" | custom-call | flops 1056964608 | bytes 6160392 | tf_op jit(solution)/shard_map/pallas_call | solution.py:418
  38.7 0.1 collective-permute-start.1
  38.8 0.9 %collective-permute-start.2 = (f32[384,128]{1,0:T(8,128)S(1)}, f32[384,128]{1,0:T(8,128)S(1)}, u32[]{:S(2)}, u32[]{:S(2)}) collective-permute-start(f32[384,128]{1,0:T(8,128)S(1)} %get-tuple-element.38), channel_id=1, source_target_pairs={{8,32},{40,64},{72,96},{104,112},{120,80},{88,48},{56,16},{24,0},{... | collective-permute-start | bytes 589832 | tf_op jit(solution)/shard_map/ppermute | solution.py:483
  39.7 0.0 collective-permute-start.3
  39.7 3.2 %collective-permute-start = (f32[192,128]{1,0:T(8,128)S(1)}, f32[192,128]{1,0:T(8,128)S(1)}, u32[]{:S(2)}, u32[]{:S(2)}) collective-permute-start(f32[192,128]{1,0:T(8,128)S(1)} %get-tuple-element.36), channel_id=1, source_target_pairs={{1,2},{2,1},{3,4},{4,3},{5,6},{6,5},{9,10},{10,9},{11,12},{12,11},... | collective-permute-start | bytes 294920 | tf_op jit(solution)/shard_map/ppermute | solution.py:481
  43.0 1.5 %shard_map.96.base = f32[512,384]{1,0:T(8,128)S(1)} custom-call(f32[512,384]{1,0:T(8,128)S(1)} %get-tuple-element.40.modal, bf16[512,384]{1,0:T(8,128)(2,1)S(1)} %get-tuple-element.41.solved_h, bf16[512,384]{1,0:T(8,128)(2,1)S(1)} %get-tuple-element.42.solved_l, bf16[2304,384]{1,0:T(8,128)(2,1)S(1)} %get-tuple-element.34.first_set, bf16[2304,384]{1,0:T(8,128)(2,1)S(1)} %copy-done), custom_call_target="tpu_custom_call" | custom-call | flops 603979776 | bytes 5898240 | tf_op jit(solution)/shard_map/pallas_call | solution.py:418
  44.5 3.1 %collective-permute-done.3.from_even = f32[192,128]{1,0:T(8,128)S(1)} collective-permute-done((f32[192,128]{1,0:T(8,128)S(1)}, f32[192,128]{1,0:T(8,128)S(1)}, u32[]{:S(2)}, u32[]{:S(2)}) %collective-permute-start.3) | collective-permute-done | bytes 98336 | tf_op jit(solution)/shard_map/ppermute | solution.py:482
  47.6 0.0 collective-permute-done.1.from_chip
  47.6 1.6 %shard_map.97.base = f32[32,2,8,384]{3,2,1,0:T(8,128)S(1)} custom-call(s32[2]{0:T(128)S(1)} %pad_add_fusion.place, f32[384,128]{1,0:T(8,128)S(1)} %collective-permute-done.1.from_chip, f32[384,128]{1,0:T(8,128)S(1)} %collective-permute-done.2.from_next, f32[192,128]{1,0:T(8,128)S(1)} %collective-permute-done.3.from_even, f32[512,384]{1,0:T(8,128)S(1)} %shard_map.96.base, ...), custom_call_target="tpu_custom_call" | custom-call | flops 603979776 | bytes 4096008 | tf_op jit(solution)/shard_map/pallas_call | solution.py:418
  49.3 2.2 %shard_map.98 = (bf16[512,384]{1,0:T(8,128)(2,1)S(1)}, bf16[512,384]{1,0:T(8,128)(2,1)S(1)}, f32[2,256,128]{2,1,0:T(8,128)S(1)}, f32[384,128]{1,0:T(8,128)S(1)},...) custom-call(s32[2]{0:T(128)S(1)} %pad_add_fusion.place, ...), custom_call_target="tpu_custom_call" | custom-call | flops 603979776 | bytes 7241736 | tf_op jit(solution)/shard_map/pallas_call | solution.py:418
  51.5 0.1 collective-permute-start.5
  51.6 1.6 %collective-permute-start.6 = (f32[384,128]{1,0:T(8,128)S(1)}, f32[384,128]{1,0:T(8,128)S(1)}, u32[]{:S(2)}, u32[]{:S(2)}) collective-permute-start(f32[384,128]{1,0:T(8,128)S(1)} %get-tuple-element.47), channel_id=1, source_target_pairs={{8,32},{40,64},{72,96},{104,112},{120,80},{88,48},{56,16},{24,0},{... | collective-permute-start | bytes 589832 | tf_op jit(solution)/shard_map/ppermute | solution.py:483
  53.2 3.4 %collective-permute-start.4 = (f32[192,128]{1,0:T(8,128)S(1)}, f32[192,128]{1,0:T(8,128)S(1)}, u32[]{:S(2)}, u32[]{:S(2)}) collective-permute-start(f32[192,128]{1,0:T(8,128)S(1)} %get-tuple-element.45), channel_id=1, source_target_pairs={{1,2},{2,1},{3,4},{4,3},{5,6},{6,5},{9,10},{10,9},{11,12},{12,11},... | collective-permute-start | bytes 294920 | tf_op jit(solution)/shard_map/ppermute | solution.py:481
  56.6 1.5 %shard_map.99.base = f32[512,384]{1,0:T(8,128)S(1)} custom-call(f32[512,384]{1,0:T(8,128)S(1)} %get-tuple-element.40.modal, bf16[512,384]{1,0:T(8,128)(2,1)S(1)} %get-tuple-element.49.solved_h, bf16[512,384]{1,0:T(8,128)(2,1)S(1)} %get-tuple-element.50.solved_l, bf16[2304,384]{1,0:T(8,128)(2,1)S(1)} %get-tuple-element.34.first_set, bf16[2304,384]{1,0:T(8,128)(2,1)S(1)} %copy-done), custom_call_target="tpu_custom_call" | custom-call | flops 603979776 | bytes 5898240 | tf_op jit(solution)/shard_map/pallas_call | solution.py:418
  58.2 1.2 %collective-permute-done.7.from_even = f32[192,128]{1,0:T(8,128)S(1)} collective-permute-done((f32[192,128]{1,0:T(8,128)S(1)}, f32[192,128]{1,0:T(8,128)S(1)}, u32[]{:S(2)}, u32[]{:S(2)}) %collective-permute-start.7) | collective-permute-done | bytes 98336 | tf_op jit(solution)/shard_map/ppermute | solution.py:482
  59.3 1.6 %shard_map.100.base = f32[32,2,8,384]{3,2,1,0:T(8,128)S(1)} custom-call(s32[2]{0:T(128)S(1)} %pad_add_fusion.place, f32[384,128]{1,0:T(8,128)S(1)} %collective-permute-done.5.from_chip, f32[384,128]{1,0:T(8,128)S(1)} %collective-permute-done.6.from_next, f32[192,128]{1,0:T(8,128)S(1)} %collective-permute-done.7.from_even, f32[512,384]{1,0:T(8,128)S(1)} %shard_map.99.base, ...), custom_call_target="tpu_custom_call" | custom-call | flops 603979776 | bytes 4096008 | tf_op jit(solution)/shard_map/pallas_call | solution.py:418
  61.0 2.0 %shard_map.101 = f32[512,384]{1,0:T(8,128)S(1)} custom-call(s32[2]{0:T(128)S(1)} %pad_add_fusion.place, f32[192,128]{1,0:T(8,128)S(1)} %collective-permute-done.4.from_odd, f32[32,2,8,384]{3,2,1,0:T(8,128)S(1)} %shard_map.100.base, bf16[2304,384]{1,0:T(8,128)(2,1)S(1)} %copy-done, f32[3,256,384]{2,1,0:T(8,128)S(1)} %copy-done.1), custom_call_target="tpu_custom_call" | custom-call | flops 452984832 | bytes 4620296 | tf_op jit(solution)/shard_map/pallas_call | solution.py:418
  63.0 19.4 %all_to_all.15.arrived = f32[16,32,384]{2,1,0:T(8,128)S(1)} all-to-all(f32[16,32,384]{2,1,0:T(8,128)S(1)} %bitcast.7), channel_id=1, replica_groups=mesh['tm'=16,'space'=8] {'tm'}, dimensions={0} | all-to-all | bytes 1572864 | tf_op jit(solution)/shard_map/all_to_all | solution.py:530
  82.4 1.3 %shard_map.102 = f32[2,384,256]{2,1,0:T(8,128)} custom-call(f32[16,32,384]{2,1,0:T(8,128)S(1)} %all_to_all.15.arrived, bf16[256,256]{1,0:T(8,128)(2,1)S(1)} %get-tuple-element.52.order), custom_call_target="tpu_custom_call" | custom-call | flops 201326592 | bytes 1703936 | tf_op jit(solution)/shard_map/pallas_call | solution.py:418
  (19 shorter events, 0.0 us)
Async XLA Ops:
  0.0 20.5 %copy-start.7 = (f32[384]{0:T(512)S(1)}, f32[384]{0:T(512)}, u32[]{:S(2)}) copy-start(f32[384]{0:T(512)} %param.11) | copy-start | bytes 4612
  0.0 20.5 %copy-start.3 = (f32[384,384]{1,0:T(8,128)S(1)}, f32[384,384]{1,0:T(8,128)}, u32[]{:S(2)}) copy-start(f32[384,384]{1,0:T(8,128)} %modes_in.1) | copy-start | bytes 1769476
  0.0 20.5 %copy-start.5 = (f32[256]{0:T(256)S(1)}, f32[256]{0:T(256)}, u32[]{:S(2)}) copy-start(f32[256]{0:T(256)} %param.10) | copy-start | bytes 3076
  2.0 8.2 %all-to-all-start = ((s32[4,8,128]{2,1,0:T(8,128)}), s32[4,8,128]{2,1,0:T(8,128)S(1)}, u32[]{:S(2)}, u32[]{:S(2)}) async-start(s32[4,8,128]{2,1,0:T(8,128)} %shard_map.92), calls=%async_computation | async-start | bytes 32768 | tf_op jit(solution)/shard_map/all_to_all | solution.py:438
  12.7 23.0 %all-to-all-start.1 = ((f32[16,32,384]{2,1,0:T(8,128)}), f32[16,32,384]{2,1,0:T(8,128)S(1)}, u32[]{:S(2)}, u32[]{:S(2)}) async-start(f32[16,32,384]{2,1,0:T(8,128)} %get-tuple-element.31), calls=%async_computation.1 | async-start | bytes 1572864 | tf_op jit(solution)/shard_map/all_to_all | solution.py:460
  20.5 1.2 %copy-start.2 = (f32[6,384,96]{1,2,0:T(8,128)S(1)}, f32[6,384,96]{1,2,0:T(8,128)}, u32[]{:S(2)}) copy-start(f32[6,384,96]{1,2,0:T(8,128)} %param.14) | copy-start | bytes 2654212
  21.7 1.1 %copy-start.4 = (f32[384,384]{1,0:T(8,128)S(1)}, f32[384,384]{1,0:T(8,128)}, u32[]{:S(2)}) copy-start(f32[384,384]{1,0:T(8,128)} %modes_out.1) | copy-start | bytes 1769476
  22.8 1.1 %copy-start.6 = (bf16[768,384]{1,0:T(8,128)(2,1)S(1)}, bf16[768,384]{1,0:T(8,128)(2,1)}, u32[]{:S(2)}) copy-start(bf16[768,384]{1,0:T(8,128)(2,1)} %constant.11.clone.pick) | copy-start | bytes 1769476
  35.7 7.3 %copy-start = (bf16[2304,384]{1,0:T(8,128)(2,1)S(1)}, bf16[2304,384]{1,0:T(8,128)(2,1)}, u32[]{:S(2)}) copy-start(bf16[2304,384]{1,0:T(8,128)(2,1)} %get-tuple-element.43.second_set) | copy-start | bytes 5308420
  38.7 8.9 %collective-permute-start.1 = (f32[384,128]{1,0:T(8,128)S(1)}, f32[384,128]{1,0:T(8,128)S(1)}, u32[]{:S(2)}, u32[]{:S(2)}) collective-permute-start(f32[384,128]{1,0:T(8,128)S(1)} %get-tuple-element.37), channel_id=1, source_target_pairs={{0,8},{8,0},{16,24},{24,16},{32,40},{40,32},{48,56},{56,48},{64,72... | collective-permute-start | bytes 589832 | tf_op jit(solution)/shard_map/ppermute | solution.py:484
  38.8 8.8 %collective-permute-start.2 = (f32[384,128]{1,0:T(8,128)S(1)}, f32[384,128]{1,0:T(8,128)S(1)}, u32[]{:S(2)}, u32[]{:S(2)}) collective-permute-start(f32[384,128]{1,0:T(8,128)S(1)} %get-tuple-element.38), channel_id=1, source_target_pairs={{8,32},{40,64},{72,96},{104,112},{120,80},{88,48},{56,16},{24,0},{... | collective-permute-start | bytes 589832 | tf_op jit(solution)/shard_map/ppermute | solution.py:483
  39.7 7.9 %collective-permute-start.3 = (f32[192,128]{1,0:T(8,128)S(1)}, f32[192,128]{1,0:T(8,128)S(1)}, u32[]{:S(2)}, u32[]{:S(2)}) collective-permute-start(f32[192,128]{1,0:T(8,128)S(1)} %get-tuple-element.39), channel_id=1, source_target_pairs={{0,1},{1,0},{2,3},{3,2},{4,5},{5,4},{6,7},{7,6},{8,9},{9,8},{10,11... | collective-permute-start | bytes 294920 | tf_op jit(solution)/shard_map/ppermute | solution.py:482
  39.7 9.5 %collective-permute-start = (f32[192,128]{1,0:T(8,128)S(1)}, f32[192,128]{1,0:T(8,128)S(1)}, u32[]{:S(2)}, u32[]{:S(2)}) collective-permute-start(f32[192,128]{1,0:T(8,128)S(1)} %get-tuple-element.36), channel_id=1, source_target_pairs={{1,2},{2,1},{3,4},{4,3},{5,6},{6,5},{9,10},{10,9},{11,12},{12,11},... | collective-permute-start | bytes 294920 | tf_op jit(solution)/shard_map/ppermute | solution.py:481
  47.6 1.7 %copy-start.1 = (f32[3,256,384]{2,1,0:T(8,128)S(1)}, f32[3,256,384]{2,1,0:T(8,128)}, u32[]{:S(2)}) copy-start(f32[3,256,384]{2,1,0:T(8,128)} %get-tuple-element.35.factors_far.factors) | copy-start | bytes 3538948
  51.5 7.8 %collective-permute-start.5 = (f32[384,128]{1,0:T(8,128)S(1)}, f32[384,128]{1,0:T(8,128)S(1)}, u32[]{:S(2)}, u32[]{:S(2)}) collective-permute-start(f32[384,128]{1,0:T(8,128)S(1)} %get-tuple-element.46), channel_id=1, source_target_pairs={{0,8},{8,0},{16,24},{24,16},{32,40},{40,32},{48,56},{56,48},{64,72... | collective-permute-start | bytes 589832 | tf_op jit(solution)/shard_map/ppermute | solution.py:484
  51.6 7.8 %collective-permute-start.6 = (f32[384,128]{1,0:T(8,128)S(1)}, f32[384,128]{1,0:T(8,128)S(1)}, u32[]{:S(2)}, u32[]{:S(2)}) collective-permute-start(f32[384,128]{1,0:T(8,128)S(1)} %get-tuple-element.47), channel_id=1, source_target_pairs={{8,32},{40,64},{72,96},{104,112},{120,80},{88,48},{56,16},{24,0},{... | collective-permute-start | bytes 589832 | tf_op jit(solution)/shard_map/ppermute | solution.py:483
  53.2 6.2 %collective-permute-start.7 = (f32[192,128]{1,0:T(8,128)S(1)}, f32[192,128]{1,0:T(8,128)S(1)}, u32[]{:S(2)}, u32[]{:S(2)}) collective-permute-start(f32[192,128]{1,0:T(8,128)S(1)} %get-tuple-element.48), channel_id=1, source_target_pairs={{0,1},{1,0},{2,3},{3,2},{4,5},{5,4},{6,7},{7,6},{8,9},{9,8},{10,11... | collective-permute-start | bytes 294920 | tf_op jit(solution)/shard_map/ppermute | solution.py:482
  53.2 7.8 %collective-permute-start.4 = (f32[192,128]{1,0:T(8,128)S(1)}, f32[192,128]{1,0:T(8,128)S(1)}, u32[]{:S(2)}, u32[]{:S(2)}) collective-permute-start(f32[192,128]{1,0:T(8,128)S(1)} %get-tuple-element.45), channel_id=1, source_target_pairs={{1,2},{2,1},{3,4},{4,3},{5,6},{6,5},{9,10},{10,9},{11,12},{12,11},... | collective-permute-start | bytes 294920 | tf_op jit(solution)/shard_map/ppermute | solution.py:481

commit v6 on v5

--- a/solution.py
+++ b/solution.py
@@ -347,11 +347,11 @@
     base[...] = modal[...] - dot_columns(faces, (lift_h[wide:], lift_l[wide:]))
 
 
-def meet_kernel(place, from_chip, from_next, from_even, base, inner, second_set, out, faces):
+def meet_kernel(place, from_chip, from_next, base, inner, second_set, out, faces):
     near = 1 - (place[1] & 1)
     wide = 4 * LANES
     lift_h, lift_l, _, _ = second_weights(second_set)
-    faces[:, near, :, :LANES] = unpack(from_even[...]).reshape(STEPS, 8, LANES)
+    faces[:, near, :, :LANES] = jnp.zeros((STEPS, 8, LANES), F32)
     faces[:, 1 - near, :, :LANES] = inner[0].reshape(STEPS, 8, LANES)
     faces[:, near, :, LANES : 2 * LANES] = inner[1].reshape(STEPS, 8, LANES)
     faces[:, 1 - near, :, LANES : 2 * LANES] = jnp.zeros((STEPS, 8, LANES), F32)
@@ -361,30 +361,30 @@
     out[...] = (base[...] - coupled).reshape(STEPS, 2, 8, NB)
 
 
-def corrected(place, from_odd, base, lift_h, lift_l, modes):
+def corrected(place, from_even, from_odd, base, lift_h, lift_l, modes):
     near = 1 - (place[1] & 1)
-    rows = slice(LANES, 2 * LANES)
-    coupled = dot_columns(split(unpack(from_odd[...])), (lift_h[rows], lift_l[rows]))
-    modes[:, near] = base[:, near]
-    modes[:, 1 - near] = base[:, 1 - near] - coupled.reshape(STEPS, 8, NB)
+    for at, (arrived, layer) in enumerate([(from_even, near), (from_odd, 1 - near)]):
+        rows = slice(at * LANES, (at + 1) * LANES)
+        coupled = dot_columns(split(unpack(arrived[...])), (lift_h[rows], lift_l[rows]))
+        modes[:, layer] = base[:, layer] - coupled.reshape(STEPS, 8, NB)
     return modes[...].reshape(ROWS, NB)
 
 
 def sweep_kernel(
-    place, from_odd, base, first_set, second_set, factors,
+    place, from_even, from_odd, base, first_set, second_set, factors,
     solved_h, solved_l, inner_out, to_chip, to_next, to_even, to_odd, modes, traces,
 ):
     _, _, trace_h, trace_l = first_weights(first_set)
     lift_h, lift_l, _, _ = second_weights(second_set)
-    solved = split(divided(corrected(place, from_odd, base, lift_h, lift_l, modes), factors))
+    solved = split(divided(corrected(place, from_even, from_odd, base, lift_h, lift_l, modes), factors))
     send_traces(
         place, solved, trace_h, trace_l, traces, solved_h, solved_l, inner_out, to_chip, to_next, to_even, to_odd
     )
 
 
-def last_kernel(place, from_odd, base, second_set, factors, steps, modes, spectrum):
+def last_kernel(place, from_even, from_odd, base, second_set, factors, steps, modes, spectrum):
     lift_h, lift_l, out_h, out_l = second_weights(second_set)
-    solved = split(divided(corrected(place, from_odd, base, lift_h, lift_l, modes), factors))
+    solved = split(divided(corrected(place, from_even, from_odd, base, lift_h, lift_l, modes), factors))
     spectrum[...] = dot_rows(solved, (out_h[...], out_l[...]))
     to_steps(spectrum, steps)
 
@@ -484,7 +484,7 @@
         from_chip = lax.ppermute(to_chip, "tm", SAME_CHIP)
         return from_chip, from_next, from_even, from_odd
 
-    def inside(solved_h, solved_l, inner, from_chip, from_next, from_even):
+    def inside(solved_h, solved_l, inner, from_chip, from_next):
         (base,) = call(
             inside_kernel,
             [(a, KEPT) for a in (modal, solved_h, solved_l, first_set)] + [(second_set, VMEM)],
@@ -494,7 +494,7 @@
         (base,) = call(
             meet_kernel,
             [place]
-            + [(a, VMEM) for a in (from_chip, from_next, from_even)]
+            + [(a, VMEM) for a in (from_chip, from_next)]
             + [(base, KEPT), (inner, KEPT), (second_set, VMEM)],
             [((STEPS, 2, 8, NB), F32, KEPT)],
             2 * 3 * 512 * 384 * 512,
@@ -509,20 +509,20 @@
         2 * 3 * 512 * 384 * (384 + 512),
         [pltpu.VMEM((ROWS, NB), F32), face_scratch, pltpu.VMEM((3, HALF, NB), F32), DMA],
     )
-    *incoming, from_odd = exchange(*outgoing)
+    *incoming, from_even, from_odd = exchange(*outgoing)
     base = inside(solved_h, solved_l, inner, *incoming)
     solved_h, solved_l, inner, *outgoing = call(
         sweep_kernel,
-        [place, (from_odd, VMEM), base, (first_set, KEPT), (second_set, VMEM), (factors, VMEM)],
+        [place, (from_even, VMEM), (from_odd, VMEM), base, (first_set, KEPT), (second_set, VMEM), (factors, VMEM)],
         faces,
         2 * 3 * 512 * 384 * 512,
         [pltpu.VMEM((STEPS, 2, 8, NB), F32), face_scratch],
     )
-    *incoming, from_odd = exchange(*outgoing)
+    *incoming, from_even, from_odd = exchange(*outgoing)
     base = inside(solved_h, solved_l, inner, *incoming)
     (steps,) = call(
         last_kernel,
-        [place, (from_odd, VMEM), base, (second_set, VMEM), (factors, VMEM)],
+        [place, (from_even, VMEM), (from_odd, VMEM), base, (second_set, VMEM), (factors, VMEM)],
         [((ROWS, NB), F32, VMEM)],
         2 * 3 * 512 * 384 * 384,
         [pltpu.VMEM((STEPS, 2, 8, NB), F32), pltpu.VMEM((ROWS, NB), F32)],

time: 84.4 us -> 84.1 us (level)
  waiting for transfers between devices: 14.4 us -> 13.1 us
    ppermute x2, waiting for transfers between devices: 4.23 us -> 0.52 us  [exchange(): from_even = lax.ppermute(to_even, 'space', EVEN_SIDES)]
    ppermute x2, waiting for transfers between devices: 0.01 us -> 1.59 us  [exchange(): from_next = lax.ppermute(to_next, 'tm', NEXT_CHIP)]
  transfers between devices with their start and end apart: 10 -> 10, of which waited for: 4 -> 6; matrix products, arithmetic and copies ran while one was open for 0% -> 0% of each run, Pallas kernels for 15% -> 15%
where the time goes in v6:
time: 84.1 us; the launch traced here: 83.6 us
  Pallas kernels  25.8 us (31%)
  starting transfers between devices  21.1 us (25%)
  blocking collectives  19.7 us (23%)
  waiting for transfers between devices  13.1 us (16%)
  local copies, waits for them, and re-layouts  3.31 us (4%)
    pallas_call x12, Pallas kernels, call(): pl.pallas_call(body, out_shape=shapes, in_specs=[spec for _, spec in ins]...  25.8 us
    all_to_all x1, blocking collectives, shards(): back = lax.all_to_all(steps.reshape(16, 32, NB), 'tm', 0, 0, tiled=True)  19.7 us
    all_to_all x1, starting transfers between devices, shards(): arrived = lax.all_to_all(sent, 'tm', 0, 0, tiled=True).reshape(ROWS, NB)  7.81 us
    all_to_all x1, waiting for transfers between devices, shards(): arrived = lax.all_to_all(sent, 'tm', 0, 0, tiled=True).reshape(ROWS, NB)  7.7 us
    ppermute x2, starting transfers between devices, exchange(): from_odd = lax.ppermute(to_odd, 'space', ODD_SIDES)  6.71 us
    all_to_all x1, starting transfers between devices, shards(): lax.all_to_all(table, 'space', 0, 0, tiled=True, axis_index_groups=[[0, 1...  3.49 us
    unnamed x16, local copies, waits for them, and re-layouts  3.31 us
    all_to_all x1, waiting for transfers between devices, shards(): lax.all_to_all(table, 'space', 0, 0, tiled=True, axis_index_groups=[[0, 1...  2.49 us
  transfers between devices with their start and end apart: 10, of which 6 were waited for; matrix products, arithmetic and copies ran while one was open for 0% of the time, Pallas kernels for 15%

profile of v6, /device:TPU:4, one launch (start us, length us, event | category | flops | bytes accessed | tf_op | source)
XLA Modules:
  0.0 83.6 jit_solution(9798830246437193369)
XLA Ops:
  0.0 0.1 pad_add_fusion.place
  0.1 1.9 %shard_map.92 = s32[4,8,128]{2,1,0:T(8,128)} custom-call(s32[2]{0:T(128)S(1)} %pad_add_fusion.place, s32[6,256]{1,0:T(8,128)} %nbr_far.3, s32[2,128]{1,0:T(2,128)} %halo_far.3), custom_call_target="tpu_custom_call" | custom-call | flops 10000 | bytes 23560 | tf_op jit(solution)/shard_map/pallas_call | solution.py:418
  2.0 3.5 %all-to-all-start = ((s32[4,8,128]{2,1,0:T(8,128)}), s32[4,8,128]{2,1,0:T(8,128)S(1)}, u32[]{:S(2)}, u32[]{:S(2)}) async-start(s32[4,8,128]{2,1,0:T(8,128)} %shard_map.92), calls=%async_computation | async-start | bytes 32768 | tf_op jit(solution)/shard_map/all_to_all | solution.py:438
  5.5 2.2 %shard_map.91 = (f32[2,32,8,384]{3,2,1,0:T(8,128)S(1)}, f32[32,8,256]{2,1,0:T(8,128)S(1)}, s32[256]{0:T(256)S(1)}) custom-call(s32[6,256]{1,0:T(8,128)} %nbr_far.3, s32[2,128]{1,0:T(2,128)} %halo_far.3, f32[2,384,256]{2,1,0:T(8,128)} %rhs_far.1), custom_call_target="tpu_custom_call" | custom-call | flops 201326592 | bytes 1843200 | tf_op jit(solution)/shard_map/pallas_call | solution.py:418
  7.7 2.5 %all-to-all-done = s32[4,8,128]{2,1,0:T(8,128)S(1)} async-done(((s32[4,8,128]{2,1,0:T(8,128)}), s32[4,8,128]{2,1,0:T(8,128)S(1)}, u32[]{:S(2)}, u32[]{:S(2)}) %all-to-all-start) | async-done | bytes 16416 | tf_op jit(solution)/shard_map/all_to_all | solution.py:438
  10.2 2.5 %shard_map.93 = (f32[16,32,384]{2,1,0:T(8,128)}, s32[2]{0:T(128)S(1)}) custom-call(s32[2]{0:T(128)S(1)} %pad_add_fusion.place, s32[256]{0:T(256)S(1)} %get-tuple-element.29.spot, f32[2,32,8,384]{3,2,1,0:T(8,128)S(1)} %get-tuple-element.30.placed, s32[32,128]{1,0:T(8,128)S(1)} %bitcast.9), custom_call_target="tpu_custom_call" | custom-call | flops 1000000 | bytes 1590288 | tf_op jit(solution)/shard_map/pallas_call | solution.py:418
  12.7 7.8 %all-to-all-start.1 = ((f32[16,32,384]{2,1,0:T(8,128)}), f32[16,32,384]{2,1,0:T(8,128)S(1)}, u32[]{:S(2)}, u32[]{:S(2)}) async-start(f32[16,32,384]{2,1,0:T(8,128)} %get-tuple-element.31), calls=%async_computation.1 | async-start | bytes 1572864 | tf_op jit(solution)/shard_map/all_to_all | solution.py:460
  20.6 1.2 %copy-done.2 = f32[6,384,96]{1,2,0:T(8,128)S(1)} copy-done((f32[6,384,96]{1,2,0:T(8,128)S(1)}, f32[6,384,96]{1,2,0:T(8,128)}, u32[]{:S(2)}) %copy-start.2) | copy-done | bytes 884760
  21.7 1.1 %copy-done.4 = f32[384,384]{1,0:T(8,128)S(1)} copy-done((f32[384,384]{1,0:T(8,128)S(1)}, f32[384,384]{1,0:T(8,128)}, u32[]{:S(2)}) %copy-start.4) | copy-done | bytes 589848
  22.8 1.1 %copy-done.6 = bf16[768,384]{1,0:T(8,128)(2,1)S(1)} copy-done((bf16[768,384]{1,0:T(8,128)(2,1)S(1)}, bf16[768,384]{1,0:T(8,128)(2,1)}, u32[]{:S(2)}) %copy-start.6) | copy-done | bytes 589848
  23.8 4.1 %shard_map.94 = (bf16[256,256]{1,0:T(8,128)(2,1)S(1)}, bf16[2304,384]{1,0:T(8,128)(2,1)S(1)}, f32[3,256,384]{2,1,0:T(8,128)}, bf16[2304,384]{1,0:T(8,128)(2,1)}) custom-call(s32[2]{0:T(128)S(1)} %pad_add_fusion.place, s32[2]{0:T(128)S(1)} %get-tuple-element.32.shift, f32[32,8,256]{2,1,0:T(8,128)S(1)} %get-tuple-element.33.placed_order, ...), custom_call_target="tpu_custom_call" | custom-call | flops 1132462080 | bytes 7768592 | tf_op jit(solution)/shard_map/pallas_call | solution.py:418
  28.0 7.7 %all-to-all-done.1 = f32[16,32,384]{2,1,0:T(8,128)S(1)} async-done(((f32[16,32,384]{2,1,0:T(8,128)}), f32[16,32,384]{2,1,0:T(8,128)S(1)}, u32[]{:S(2)}, u32[]{:S(2)}) %all-to-all-start.1) | async-done | bytes 786464 | tf_op jit(solution)/shard_map/all_to_all | solution.py:460
  35.7 3.0 %shard_map.95 = (f32[512,384]{1,0:T(8,128)S(1)}, bf16[512,384]{1,0:T(8,128)(2,1)S(1)}, bf16[512,384]{1,0:T(8,128)(2,1)S(1)}, f32[2,256,128]{2,1,0:T(8,128)S(1)},...) custom-call(s32[2]{0:T(128)S(1)} %pad_add_fusion.place, ...), custom_call_target="tpu_custom_call" | custom-call | flops 1056964608 | bytes 6160392 | tf_op jit(solution)/shard_map/pallas_call | solution.py:418
  38.7 0.1 collective-permute-start.2
  38.8 0.9 %collective-permute-start.3 = (f32[384,128]{1,0:T(8,128)S(1)}, f32[384,128]{1,0:T(8,128)S(1)}, u32[]{:S(2)}, u32[]{:S(2)}) collective-permute-start(f32[384,128]{1,0:T(8,128)S(1)} %get-tuple-element.39), channel_id=1, source_target_pairs={{8,32},{40,64},{72,96},{104,112},{120,80},{88,48},{56,16},{24,0},{... | collective-permute-start | bytes 589832 | tf_op jit(solution)/shard_map/ppermute | solution.py:483
  39.7 3.2 %collective-permute-start.1 = (f32[192,128]{1,0:T(8,128)S(1)}, f32[192,128]{1,0:T(8,128)S(1)}, u32[]{:S(2)}, u32[]{:S(2)}) collective-permute-start(f32[192,128]{1,0:T(8,128)S(1)} %get-tuple-element.37), channel_id=1, source_target_pairs={{1,2},{2,1},{3,4},{4,3},{5,6},{6,5},{9,10},{10,9},{11,12},{12,11},... | collective-permute-start | bytes 294920 | tf_op jit(solution)/shard_map/ppermute | solution.py:481
  43.0 1.5 %shard_map.96.base = f32[512,384]{1,0:T(8,128)S(1)} custom-call(f32[512,384]{1,0:T(8,128)S(1)} %get-tuple-element.40.modal, bf16[512,384]{1,0:T(8,128)(2,1)S(1)} %get-tuple-element.41.solved_h, bf16[512,384]{1,0:T(8,128)(2,1)S(1)} %get-tuple-element.42.solved_l, bf16[2304,384]{1,0:T(8,128)(2,1)S(1)} %get-tuple-element.34.first_set, bf16[2304,384]{1,0:T(8,128)(2,1)S(1)} %copy-done), custom_call_target="tpu_custom_call" | custom-call | flops 603979776 | bytes 5898240 | tf_op jit(solution)/shard_map/pallas_call | solution.py:418
  44.5 0.9 %collective-permute-done.3.from_next = f32[384,128]{1,0:T(8,128)S(1)} collective-permute-done((f32[384,128]{1,0:T(8,128)S(1)}, f32[384,128]{1,0:T(8,128)S(1)}, u32[]{:S(2)}, u32[]{:S(2)}) %collective-permute-start.3) | collective-permute-done | bytes 196640 | tf_op jit(solution)/shard_map/ppermute | solution.py:483
  45.5 1.6 %shard_map.97.base = f32[32,2,8,384]{3,2,1,0:T(8,128)S(1)} custom-call(s32[2]{0:T(128)S(1)} %pad_add_fusion.place, f32[384,128]{1,0:T(8,128)S(1)} %collective-permute-done.2.from_chip, f32[384,128]{1,0:T(8,128)S(1)} %collective-permute-done.3.from_next, f32[512,384]{1,0:T(8,128)S(1)} %shard_map.96.base, f32[2,256,128]{2,1,0:T(8,128)S(1)} %get-tuple-element.44.inner, ...), custom_call_target="tpu_custom_call" | custom-call | flops 603979776 | bytes 3997704 | tf_op jit(solution)/shard_map/pallas_call | solution.py:418
  47.1 0.5 collective-permute-done.from_even
  47.6 2.3 %shard_map.98 = (bf16[512,384]{1,0:T(8,128)(2,1)S(1)}, bf16[512,384]{1,0:T(8,128)(2,1)S(1)}, f32[2,256,128]{2,1,0:T(8,128)S(1)}, f32[384,128]{1,0:T(8,128)S(1)},...) custom-call(s32[2]{0:T(128)S(1)} %pad_add_fusion.place, ...), custom_call_target="tpu_custom_call" | custom-call | flops 603979776 | bytes 7340040 | tf_op jit(solution)/shard_map/pallas_call | solution.py:418
  49.9 0.1 collective-permute-start.6
  50.0 1.6 %collective-permute-start.7 = (f32[384,128]{1,0:T(8,128)S(1)}, f32[384,128]{1,0:T(8,128)S(1)}, u32[]{:S(2)}, u32[]{:S(2)}) collective-permute-start(f32[384,128]{1,0:T(8,128)S(1)} %get-tuple-element.48), channel_id=1, source_target_pairs={{8,32},{40,64},{72,96},{104,112},{120,80},{88,48},{56,16},{24,0},{... | collective-permute-start | bytes 589832 | tf_op jit(solution)/shard_map/ppermute | solution.py:483
  51.6 0.5 collective-permute-start.4
  52.0 3.5 %collective-permute-start.5 = (f32[192,128]{1,0:T(8,128)S(1)}, f32[192,128]{1,0:T(8,128)S(1)}, u32[]{:S(2)}, u32[]{:S(2)}) collective-permute-start(f32[192,128]{1,0:T(8,128)S(1)} %get-tuple-element.46), channel_id=1, source_target_pairs={{1,2},{2,1},{3,4},{4,3},{5,6},{6,5},{9,10},{10,9},{11,12},{12,11},... | collective-permute-start | bytes 294920 | tf_op jit(solution)/shard_map/ppermute | solution.py:481
  55.5 1.5 %shard_map.99.base = f32[512,384]{1,0:T(8,128)S(1)} custom-call(f32[512,384]{1,0:T(8,128)S(1)} %get-tuple-element.40.modal, bf16[512,384]{1,0:T(8,128)(2,1)S(1)} %get-tuple-element.49.solved_h, bf16[512,384]{1,0:T(8,128)(2,1)S(1)} %get-tuple-element.50.solved_l, bf16[2304,384]{1,0:T(8,128)(2,1)S(1)} %get-tuple-element.34.first_set, bf16[2304,384]{1,0:T(8,128)(2,1)S(1)} %copy-done), custom_call_target="tpu_custom_call" | custom-call | flops 603979776 | bytes 5898240 | tf_op jit(solution)/shard_map/pallas_call | solution.py:418
  57.1 0.7 collective-permute-done.7.from_next
  57.7 1.6 %shard_map.100.base = f32[32,2,8,384]{3,2,1,0:T(8,128)S(1)} custom-call(s32[2]{0:T(128)S(1)} %pad_add_fusion.place, f32[384,128]{1,0:T(8,128)S(1)} %collective-permute-done.6.from_chip, f32[384,128]{1,0:T(8,128)S(1)} %collective-permute-done.7.from_next, f32[512,384]{1,0:T(8,128)S(1)} %shard_map.99.base, f32[2,256,128]{2,1,0:T(8,128)S(1)} %get-tuple-element.51.inner, ...), custom_call_target="tpu_custom_call" | custom-call | flops 603979776 | bytes 3997704 | tf_op jit(solution)/shard_map/pallas_call | solution.py:418
  59.4 0.8 %collective-permute-done.5.from_odd = f32[192,128]{1,0:T(8,128)S(1)} collective-permute-done((f32[192,128]{1,0:T(8,128)S(1)}, f32[192,128]{1,0:T(8,128)S(1)}, u32[]{:S(2)}, u32[]{:S(2)}) %collective-permute-start.5) | collective-permute-done | bytes 98336 | tf_op jit(solution)/shard_map/ppermute | solution.py:481
  60.2 2.2 %shard_map.101 = f32[512,384]{1,0:T(8,128)S(1)} custom-call(s32[2]{0:T(128)S(1)} %pad_add_fusion.place, f32[192,128]{1,0:T(8,128)S(1)} %collective-permute-done.4.from_even, f32[192,128]{1,0:T(8,128)S(1)} %collective-permute-done.5.from_odd, f32[32,2,8,384]{3,2,1,0:T(8,128)S(1)} %shard_map.100.base, bf16[2304,384]{1,0:T(8,128)(2,1)S(1)} %copy-done, ...), custom_call_target="tpu_custom_call" | custom-call | flops 452984832 | bytes 4718600 | tf_op jit(solution)/shard_map/pallas_call | solution.py:418
  62.4 19.7 %all_to_all.15.arrived = f32[16,32,384]{2,1,0:T(8,128)S(1)} all-to-all(f32[16,32,384]{2,1,0:T(8,128)S(1)} %bitcast.7), channel_id=1, replica_groups=mesh['tm'=16,'space'=8] {'tm'}, dimensions={0} | all-to-all | bytes 1572864 | tf_op jit(solution)/shard_map/all_to_all | solution.py:530
  82.1 1.3 %shard_map.102 = f32[2,384,256]{2,1,0:T(8,128)} custom-call(f32[16,32,384]{2,1,0:T(8,128)S(1)} %all_to_all.15.arrived, bf16[256,256]{1,0:T(8,128)(2,1)S(1)} %get-tuple-element.52.order), custom_call_target="tpu_custom_call" | custom-call | flops 201326592 | bytes 1703936 | tf_op jit(solution)/shard_map/pallas_call | solution.py:418
  (19 shorter events, 0.1 us)
Async XLA Ops:
  0.0 20.5 %copy-start.7 = (f32[384]{0:T(512)S(1)}, f32[384]{0:T(512)}, u32[]{:S(2)}) copy-start(f32[384]{0:T(512)} %param.11) | copy-start | bytes 4612
  0.0 20.5 %copy-start.3 = (f32[384,384]{1,0:T(8,128)S(1)}, f32[384,384]{1,0:T(8,128)}, u32[]{:S(2)}) copy-start(f32[384,384]{1,0:T(8,128)} %modes_in.1) | copy-start | bytes 1769476
  0.0 20.5 %copy-start.5 = (f32[256]{0:T(256)S(1)}, f32[256]{0:T(256)}, u32[]{:S(2)}) copy-start(f32[256]{0:T(256)} %param.10) | copy-start | bytes 3076
  2.0 8.2 %all-to-all-start = ((s32[4,8,128]{2,1,0:T(8,128)}), s32[4,8,128]{2,1,0:T(8,128)S(1)}, u32[]{:S(2)}, u32[]{:S(2)}) async-start(s32[4,8,128]{2,1,0:T(8,128)} %shard_map.92), calls=%async_computation | async-start | bytes 32768 | tf_op jit(solution)/shard_map/all_to_all | solution.py:438
  12.7 23.0 %all-to-all-start.1 = ((f32[16,32,384]{2,1,0:T(8,128)}), f32[16,32,384]{2,1,0:T(8,128)S(1)}, u32[]{:S(2)}, u32[]{:S(2)}) async-start(f32[16,32,384]{2,1,0:T(8,128)} %get-tuple-element.31), calls=%async_computation.1 | async-start | bytes 1572864 | tf_op jit(solution)/shard_map/all_to_all | solution.py:460
  20.5 1.2 %copy-start.2 = (f32[6,384,96]{1,2,0:T(8,128)S(1)}, f32[6,384,96]{1,2,0:T(8,128)}, u32[]{:S(2)}) copy-start(f32[6,384,96]{1,2,0:T(8,128)} %param.14) | copy-start | bytes 2654212
  21.7 1.1 %copy-start.4 = (f32[384,384]{1,0:T(8,128)S(1)}, f32[384,384]{1,0:T(8,128)}, u32[]{:S(2)}) copy-start(f32[384,384]{1,0:T(8,128)} %modes_out.1) | copy-start | bytes 1769476
  22.8 1.1 %copy-start.6 = (bf16[768,384]{1,0:T(8,128)(2,1)S(1)}, bf16[768,384]{1,0:T(8,128)(2,1)}, u32[]{:S(2)}) copy-start(bf16[768,384]{1,0:T(8,128)(2,1)} %constant.11.clone.pick) | copy-start | bytes 1769476
  35.7 7.3 %copy-start = (bf16[2304,384]{1,0:T(8,128)(2,1)S(1)}, bf16[2304,384]{1,0:T(8,128)(2,1)}, u32[]{:S(2)}) copy-start(bf16[2304,384]{1,0:T(8,128)(2,1)} %get-tuple-element.43.second_set) | copy-start | bytes 5308420
  38.7 5.8 %collective-permute-start.2 = (f32[384,128]{1,0:T(8,128)S(1)}, f32[384,128]{1,0:T(8,128)S(1)}, u32[]{:S(2)}, u32[]{:S(2)}) collective-permute-start(f32[384,128]{1,0:T(8,128)S(1)} %get-tuple-element.38), channel_id=1, source_target_pairs={{0,8},{8,0},{16,24},{24,16},{32,40},{40,32},{48,56},{56,48},{64,72... | collective-permute-start | bytes 589832 | tf_op jit(solution)/shard_map/ppermute | solution.py:484
  38.8 6.7 %collective-permute-start.3 = (f32[384,128]{1,0:T(8,128)S(1)}, f32[384,128]{1,0:T(8,128)S(1)}, u32[]{:S(2)}, u32[]{:S(2)}) collective-permute-start(f32[384,128]{1,0:T(8,128)S(1)} %get-tuple-element.39), channel_id=1, source_target_pairs={{8,32},{40,64},{72,96},{104,112},{120,80},{88,48},{56,16},{24,0},{... | collective-permute-start | bytes 589832 | tf_op jit(solution)/shard_map/ppermute | solution.py:483
  39.7 7.9 %collective-permute-start = (f32[192,128]{1,0:T(8,128)S(1)}, f32[192,128]{1,0:T(8,128)S(1)}, u32[]{:S(2)}, u32[]{:S(2)}) collective-permute-start(f32[192,128]{1,0:T(8,128)S(1)} %get-tuple-element.36), channel_id=1, source_target_pairs={{0,1},{1,0},{2,3},{3,2},{4,5},{5,4},{6,7},{7,6},{8,9},{9,8},{10,11... | collective-permute-start | bytes 294920 | tf_op jit(solution)/shard_map/ppermute | solution.py:482
  39.7 7.9 %collective-permute-start.1 = (f32[192,128]{1,0:T(8,128)S(1)}, f32[192,128]{1,0:T(8,128)S(1)}, u32[]{:S(2)}, u32[]{:S(2)}) collective-permute-start(f32[192,128]{1,0:T(8,128)S(1)} %get-tuple-element.37), channel_id=1, source_target_pairs={{1,2},{2,1},{3,4},{4,3},{5,6},{6,5},{9,10},{10,9},{11,12},{12,11},... | collective-permute-start | bytes 294920 | tf_op jit(solution)/shard_map/ppermute | solution.py:481
  45.5 2.1 %copy-start.1 = (f32[3,256,384]{2,1,0:T(8,128)S(1)}, f32[3,256,384]{2,1,0:T(8,128)}, u32[]{:S(2)}) copy-start(f32[3,256,384]{2,1,0:T(8,128)} %get-tuple-element.35.factors_far.factors) | copy-start | bytes 3538948
  49.9 7.2 %collective-permute-start.6 = (f32[384,128]{1,0:T(8,128)S(1)}, f32[384,128]{1,0:T(8,128)S(1)}, u32[]{:S(2)}, u32[]{:S(2)}) collective-permute-start(f32[384,128]{1,0:T(8,128)S(1)} %get-tuple-element.47), channel_id=1, source_target_pairs={{0,8},{8,0},{16,24},{24,16},{32,40},{40,32},{48,56},{56,48},{64,72... | collective-permute-start | bytes 589832 | tf_op jit(solution)/shard_map/ppermute | solution.py:484
  50.0 7.7 %collective-permute-start.7 = (f32[384,128]{1,0:T(8,128)S(1)}, f32[384,128]{1,0:T(8,128)S(1)}, u32[]{:S(2)}, u32[]{:S(2)}) collective-permute-start(f32[384,128]{1,0:T(8,128)S(1)} %get-tuple-element.48), channel_id=1, source_target_pairs={{8,32},{40,64},{72,96},{104,112},{120,80},{88,48},{56,16},{24,0},{... | collective-permute-start | bytes 589832 | tf_op jit(solution)/shard_map/ppermute | solution.py:483
  51.6 7.8 %collective-permute-start.4 = (f32[192,128]{1,0:T(8,128)S(1)}, f32[192,128]{1,0:T(8,128)S(1)}, u32[]{:S(2)}, u32[]{:S(2)}) collective-permute-start(f32[192,128]{1,0:T(8,128)S(1)} %get-tuple-element.45), channel_id=1, source_target_pairs={{0,1},{1,0},{2,3},{3,2},{4,5},{5,4},{6,7},{7,6},{8,9},{9,8},{10,11... | collective-permute-start | bytes 294920 | tf_op jit(solution)/shard_map/ppermute | solution.py:482
  52.0 8.1 %collective-permute-start.5 = (f32[192,128]{1,0:T(8,128)S(1)}, f32[192,128]{1,0:T(8,128)S(1)}, u32[]{:S(2)}, u32[]{:S(2)}) collective-permute-start(f32[192,128]{1,0:T(8,128)S(1)} %get-tuple-element.46), channel_id=1, source_target_pairs={{1,2},{2,1},{3,4},{4,3},{5,6},{6,5},{9,10},{10,9},{11,12},{12,11},... | collective-permute-start | bytes 294920 | tf_op jit(solution)/shard_map/ppermute | solution.py:481

commit v7 on v6

--- a/solution.py
+++ b/solution.py
@@ -139,8 +139,10 @@
     upper = place[1] >= SLABS // 2
     steps = jnp.where(upper, nbr[1:2, :], nbr[0:1, :])
     labels = jnp.where(upper, halo[0:1, :], halo[1:2, :])
-    rows = [steps[:, :LANES], steps[:, LANES:], labels, labels, nbr[1:2, :LANES], nbr[1:2, LANES:], labels, labels]
-    packed = jnp.concatenate(rows)
+    index = lax.broadcasted_iota(jnp.int32, (1, SLAB), 1)
+    facing = jnp.sum(jnp.where(nbr[1:2, :] == SLAB, index, 0), axis=1, keepdims=True)
+    rows = [steps[:, :LANES], steps[:, LANES:], labels, jnp.broadcast_to(facing, (1, LANES))]
+    packed = jnp.concatenate(rows + rows)
     for member in range(SLABS // 2):
         table[member] = packed
 
@@ -187,22 +189,14 @@
         placed[step] = values.reshape(32, 8, NB)
 
 
-def align_kernel(place, spot, placed, far, sent, shift, chain, tables, done):
-    copies = [pltpu.make_async_copy(far, near, done.at[at]) for at, near in enumerate([chain, tables])]
-    for copy in copies:
-        copy.start()
-    for copy in copies:
-        copy.wait()
+def align_kernel(place, spot, chain, placed, sent, shift):
     group = lax.shift_right_logical(place[1], 2)
     member = place[1] & 3
 
     def step(slab, at):
         return chain[slab * 8 + lax.shift_right_logical(at, 7), at & 127]
 
-    upper_rows = tables[28:30, :]
-    index = lax.broadcasted_iota(jnp.int32, (2, LANES), 0) * LANES + lax.broadcasted_iota(jnp.int32, (2, LANES), 1)
-    facing = jnp.sum(jnp.where(upper_rows == SLAB, index, 0)) & 255
-    near = jnp.where(group == 0, facing, chain[2, 0] & 255)
+    near = jnp.where(group == 0, chain[27, 0], chain[2, 0]) & 255
     origin = near
     for hop in range(4):
         slab = jnp.where(group == 0, 3 - hop, hop)
@@ -452,10 +446,9 @@
     )
     sent, shift = call(
         align_kernel,
-        [place, (spot, SMEM), (placed, KEPT), (chain, VMEM)],
+        [place, (spot, SMEM), (chain, SMEM), (placed, KEPT)],
         [((16, 32, NB), F32, KEPT), ((2,), jnp.int32, SMEM)],
         10**6,
-        [pltpu.SMEM((32, LANES), jnp.int32), pltpu.VMEM((32, LANES), jnp.int32), DMA((2,))],
     )
     arrived = lax.all_to_all(sent, "tm", 0, 0, tiled=True).reshape(ROWS, NB)
     weights = [modes_in, modes_out, jnp.swapaxes(face_lift, 1, 2), modal_rates.reshape(1, NB), trace_rows()]

time: 84.1 us -> 83.5 us (level)
  no operation moved by 1% of the time
where the time goes in v7:
time: 83.5 us; the launch traced here: 83 us
  Pallas kernels  25.2 us (30%)
  starting transfers between devices  21.1 us (25%)
  blocking collectives  19.7 us (24%)
  waiting for transfers between devices  13.1 us (16%)
  local copies, waits for them, and re-layouts  3.31 us (4%)
    pallas_call x12, Pallas kernels, call(): pl.pallas_call(body, out_shape=shapes, in_specs=[spec for _, spec in ins]...  25.2 us
    all_to_all x1, blocking collectives, shards(): back = lax.all_to_all(steps.reshape(16, 32, NB), 'tm', 0, 0, tiled=True)  19.7 us
    all_to_all x1, starting transfers between devices, shards(): arrived = lax.all_to_all(sent, 'tm', 0, 0, tiled=True).reshape(ROWS, NB)  7.81 us
    all_to_all x1, waiting for transfers between devices, shards(): arrived = lax.all_to_all(sent, 'tm', 0, 0, tiled=True).reshape(ROWS, NB)  7.7 us
    ppermute x2, starting transfers between devices, exchange(): from_odd = lax.ppermute(to_odd, 'space', ODD_SIDES)  6.71 us
    all_to_all x1, starting transfers between devices, shards(): lax.all_to_all(table, 'space', 0, 0, tiled=True, axis_index_groups=[[0, 1...  3.49 us
    unnamed x16, local copies, waits for them, and re-layouts  3.31 us
    all_to_all x1, waiting for transfers between devices, shards(): lax.all_to_all(table, 'space', 0, 0, tiled=True, axis_index_groups=[[0, 1...  2.49 us
  transfers between devices with their start and end apart: 10, of which 6 were waited for; matrix products, arithmetic and copies ran while one was open for 0% of the time, Pallas kernels for 15%

profile of v7, /device:TPU:4, one launch (start us, length us, event | category | flops | bytes accessed | tf_op | source)
XLA Modules:
  0.0 83.0 jit_solution(14119907118870524944)
XLA Ops:
  0.0 0.1 pad_add_fusion.place
  0.1 2.0 %shard_map.92 = s32[4,8,128]{2,1,0:T(8,128)} custom-call(s32[2]{0:T(128)S(1)} %pad_add_fusion.place, s32[6,256]{1,0:T(8,128)} %nbr_far.3, s32[2,128]{1,0:T(2,128)} %halo_far.3), custom_call_target="tpu_custom_call" | custom-call | flops 10000 | bytes 23560 | tf_op jit(solution)/shard_map/pallas_call | solution.py:412
  2.1 3.5 %all-to-all-start = ((s32[4,8,128]{2,1,0:T(8,128)}), s32[4,8,128]{2,1,0:T(8,128)S(1)}, u32[]{:S(2)}, u32[]{:S(2)}) async-start(s32[4,8,128]{2,1,0:T(8,128)} %shard_map.92), calls=%async_computation | async-start | bytes 32768 | tf_op jit(solution)/shard_map/all_to_all | solution.py:432
  5.5 2.2 %shard_map.91 = (f32[2,32,8,384]{3,2,1,0:T(8,128)S(1)}, f32[32,8,256]{2,1,0:T(8,128)S(1)}, s32[256]{0:T(256)S(1)}) custom-call(s32[6,256]{1,0:T(8,128)} %nbr_far.3, s32[2,128]{1,0:T(2,128)} %halo_far.3, f32[2,384,256]{2,1,0:T(8,128)} %rhs_far.1), custom_call_target="tpu_custom_call" | custom-call | flops 201326592 | bytes 1843200 | tf_op jit(solution)/shard_map/pallas_call | solution.py:412
  7.8 2.5 %all-to-all-done = s32[4,8,128]{2,1,0:T(8,128)S(1)} async-done(((s32[4,8,128]{2,1,0:T(8,128)}), s32[4,8,128]{2,1,0:T(8,128)S(1)}, u32[]{:S(2)}, u32[]{:S(2)}) %all-to-all-start) | async-done | bytes 16416 | tf_op jit(solution)/shard_map/all_to_all | solution.py:432
  10.3 1.8 %shard_map.93 = (f32[16,32,384]{2,1,0:T(8,128)}, s32[2]{0:T(128)S(1)}) custom-call(s32[2]{0:T(128)S(1)} %pad_add_fusion.place, s32[256]{0:T(256)S(1)} %get-tuple-element.29.spot, s32[32,128]{1,0:T(8,128)S(1)} %bitcast.9, f32[2,32,8,384]{3,2,1,0:T(8,128)S(1)} %get-tuple-element.30.placed), custom_call_target="tpu_custom_call" | custom-call | flops 1000000 | bytes 1590288 | tf_op jit(solution)/shard_map/pallas_call | solution.py:412
  12.1 7.8 %all-to-all-start.1 = ((f32[16,32,384]{2,1,0:T(8,128)}), f32[16,32,384]{2,1,0:T(8,128)S(1)}, u32[]{:S(2)}, u32[]{:S(2)}) async-start(f32[16,32,384]{2,1,0:T(8,128)} %get-tuple-element.31), calls=%async_computation.1 | async-start | bytes 1572864 | tf_op jit(solution)/shard_map/all_to_all | solution.py:453
  20.0 1.2 %copy-done.2 = f32[6,384,96]{1,2,0:T(8,128)S(1)} copy-done((f32[6,384,96]{1,2,0:T(8,128)S(1)}, f32[6,384,96]{1,2,0:T(8,128)}, u32[]{:S(2)}) %copy-start.2) | copy-done | bytes 884760
  21.1 1.1 %copy-done.4 = f32[384,384]{1,0:T(8,128)S(1)} copy-done((f32[384,384]{1,0:T(8,128)S(1)}, f32[384,384]{1,0:T(8,128)}, u32[]{:S(2)}) %copy-start.4) | copy-done | bytes 589848
  22.2 1.1 %copy-done.6 = bf16[768,384]{1,0:T(8,128)(2,1)S(1)} copy-done((bf16[768,384]{1,0:T(8,128)(2,1)S(1)}, bf16[768,384]{1,0:T(8,128)(2,1)}, u32[]{:S(2)}) %copy-start.6) | copy-done | bytes 589848
  23.3 4.1 %shard_map.94 = (bf16[256,256]{1,0:T(8,128)(2,1)S(1)}, bf16[2304,384]{1,0:T(8,128)(2,1)S(1)}, f32[3,256,384]{2,1,0:T(8,128)}, bf16[2304,384]{1,0:T(8,128)(2,1)}) custom-call(s32[2]{0:T(128)S(1)} %pad_add_fusion.place, s32[2]{0:T(128)S(1)} %get-tuple-element.32.shift, f32[32,8,256]{2,1,0:T(8,128)S(1)} %get-tuple-element.33.placed_order, ...), custom_call_target="tpu_custom_call" | custom-call | flops 1132462080 | bytes 7768592 | tf_op jit(solution)/shard_map/pallas_call | solution.py:412
  27.4 7.7 %all-to-all-done.1 = f32[16,32,384]{2,1,0:T(8,128)S(1)} async-done(((f32[16,32,384]{2,1,0:T(8,128)}), f32[16,32,384]{2,1,0:T(8,128)S(1)}, u32[]{:S(2)}, u32[]{:S(2)}) %all-to-all-start.1) | async-done | bytes 786464 | tf_op jit(solution)/shard_map/all_to_all | solution.py:453
  35.1 3.0 %shard_map.95 = (f32[512,384]{1,0:T(8,128)S(1)}, bf16[512,384]{1,0:T(8,128)(2,1)S(1)}, bf16[512,384]{1,0:T(8,128)(2,1)S(1)}, f32[2,256,128]{2,1,0:T(8,128)S(1)},...) custom-call(s32[2]{0:T(128)S(1)} %pad_add_fusion.place, ...), custom_call_target="tpu_custom_call" | custom-call | flops 1056964608 | bytes 6160392 | tf_op jit(solution)/shard_map/pallas_call | solution.py:412
  38.1 0.1 collective-permute-start.2
  38.2 0.9 %collective-permute-start.3 = (f32[384,128]{1,0:T(8,128)S(1)}, f32[384,128]{1,0:T(8,128)S(1)}, u32[]{:S(2)}, u32[]{:S(2)}) collective-permute-start(f32[384,128]{1,0:T(8,128)S(1)} %get-tuple-element.39), channel_id=1, source_target_pairs={{8,32},{40,64},{72,96},{104,112},{120,80},{88,48},{56,16},{24,0},{... | collective-permute-start | bytes 589832 | tf_op jit(solution)/shard_map/ppermute | solution.py:476
  39.1 3.2 %collective-permute-start.1 = (f32[192,128]{1,0:T(8,128)S(1)}, f32[192,128]{1,0:T(8,128)S(1)}, u32[]{:S(2)}, u32[]{:S(2)}) collective-permute-start(f32[192,128]{1,0:T(8,128)S(1)} %get-tuple-element.37), channel_id=1, source_target_pairs={{1,2},{2,1},{3,4},{4,3},{5,6},{6,5},{9,10},{10,9},{11,12},{12,11},... | collective-permute-start | bytes 294920 | tf_op jit(solution)/shard_map/ppermute | solution.py:474
  42.4 1.5 %shard_map.96.base = f32[512,384]{1,0:T(8,128)S(1)} custom-call(f32[512,384]{1,0:T(8,128)S(1)} %get-tuple-element.40.modal, bf16[512,384]{1,0:T(8,128)(2,1)S(1)} %get-tuple-element.41.solved_h, bf16[512,384]{1,0:T(8,128)(2,1)S(1)} %get-tuple-element.42.solved_l, bf16[2304,384]{1,0:T(8,128)(2,1)S(1)} %get-tuple-element.34.first_set, bf16[2304,384]{1,0:T(8,128)(2,1)S(1)} %copy-done), custom_call_target="tpu_custom_call" | custom-call | flops 603979776 | bytes 5898240 | tf_op jit(solution)/shard_map/pallas_call | solution.py:412
  44.0 0.9 %collective-permute-done.3.from_next = f32[384,128]{1,0:T(8,128)S(1)} collective-permute-done((f32[384,128]{1,0:T(8,128)S(1)}, f32[384,128]{1,0:T(8,128)S(1)}, u32[]{:S(2)}, u32[]{:S(2)}) %collective-permute-start.3) | collective-permute-done | bytes 196640 | tf_op jit(solution)/shard_map/ppermute | solution.py:476
  44.9 1.6 %shard_map.97.base = f32[32,2,8,384]{3,2,1,0:T(8,128)S(1)} custom-call(s32[2]{0:T(128)S(1)} %pad_add_fusion.place, f32[384,128]{1,0:T(8,128)S(1)} %collective-permute-done.2.from_chip, f32[384,128]{1,0:T(8,128)S(1)} %collective-permute-done.3.from_next, f32[512,384]{1,0:T(8,128)S(1)} %shard_map.96.base, f32[2,256,128]{2,1,0:T(8,128)S(1)} %get-tuple-element.44.inner, ...), custom_call_target="tpu_custom_call" | custom-call | flops 603979776 | bytes 3997704 | tf_op jit(solution)/shard_map/pallas_call | solution.py:412
  46.5 0.5 collective-permute-done.from_even
  47.0 2.3 %shard_map.98 = (bf16[512,384]{1,0:T(8,128)(2,1)S(1)}, bf16[512,384]{1,0:T(8,128)(2,1)S(1)}, f32[2,256,128]{2,1,0:T(8,128)S(1)}, f32[384,128]{1,0:T(8,128)S(1)},...) custom-call(s32[2]{0:T(128)S(1)} %pad_add_fusion.place, ...), custom_call_target="tpu_custom_call" | custom-call | flops 603979776 | bytes 7340040 | tf_op jit(solution)/shard_map/pallas_call | solution.py:412
  49.3 0.1 collective-permute-start.6
  49.4 1.6 %collective-permute-start.7 = (f32[384,128]{1,0:T(8,128)S(1)}, f32[384,128]{1,0:T(8,128)S(1)}, u32[]{:S(2)}, u32[]{:S(2)}) collective-permute-start(f32[384,128]{1,0:T(8,128)S(1)} %get-tuple-element.48), channel_id=1, source_target_pairs={{8,32},{40,64},{72,96},{104,112},{120,80},{88,48},{56,16},{24,0},{... | collective-permute-start | bytes 589832 | tf_op jit(solution)/shard_map/ppermute | solution.py:476
  51.0 0.5 collective-permute-start.4
  51.5 3.5 %collective-permute-start.5 = (f32[192,128]{1,0:T(8,128)S(1)}, f32[192,128]{1,0:T(8,128)S(1)}, u32[]{:S(2)}, u32[]{:S(2)}) collective-permute-start(f32[192,128]{1,0:T(8,128)S(1)} %get-tuple-element.46), channel_id=1, source_target_pairs={{1,2},{2,1},{3,4},{4,3},{5,6},{6,5},{9,10},{10,9},{11,12},{12,11},... | collective-permute-start | bytes 294920 | tf_op jit(solution)/shard_map/ppermute | solution.py:474
  54.9 1.5 %shard_map.99.base = f32[512,384]{1,0:T(8,128)S(1)} custom-call(f32[512,384]{1,0:T(8,128)S(1)} %get-tuple-element.40.modal, bf16[512,384]{1,0:T(8,128)(2,1)S(1)} %get-tuple-element.49.solved_h, bf16[512,384]{1,0:T(8,128)(2,1)S(1)} %get-tuple-element.50.solved_l, bf16[2304,384]{1,0:T(8,128)(2,1)S(1)} %get-tuple-element.34.first_set, bf16[2304,384]{1,0:T(8,128)(2,1)S(1)} %copy-done), custom_call_target="tpu_custom_call" | custom-call | flops 603979776 | bytes 5898240 | tf_op jit(solution)/shard_map/pallas_call | solution.py:412
  56.5 0.7 collective-permute-done.7.from_next
  57.2 1.6 %shard_map.100.base = f32[32,2,8,384]{3,2,1,0:T(8,128)S(1)} custom-call(s32[2]{0:T(128)S(1)} %pad_add_fusion.place, f32[384,128]{1,0:T(8,128)S(1)} %collective-permute-done.6.from_chip, f32[384,128]{1,0:T(8,128)S(1)} %collective-permute-done.7.from_next, f32[512,384]{1,0:T(8,128)S(1)} %shard_map.99.base, f32[2,256,128]{2,1,0:T(8,128)S(1)} %get-tuple-element.51.inner, ...), custom_call_target="tpu_custom_call" | custom-call | flops 603979776 | bytes 3997704 | tf_op jit(solution)/shard_map/pallas_call | solution.py:412
  58.8 0.8 %collective-permute-done.5.from_odd = f32[192,128]{1,0:T(8,128)S(1)} collective-permute-done((f32[192,128]{1,0:T(8,128)S(1)}, f32[192,128]{1,0:T(8,128)S(1)}, u32[]{:S(2)}, u32[]{:S(2)}) %collective-permute-start.5) | collective-permute-done | bytes 98336 | tf_op jit(solution)/shard_map/ppermute | solution.py:474
  59.6 2.2 %shard_map.101 = f32[512,384]{1,0:T(8,128)S(1)} custom-call(s32[2]{0:T(128)S(1)} %pad_add_fusion.place, f32[192,128]{1,0:T(8,128)S(1)} %collective-permute-done.4.from_even, f32[192,128]{1,0:T(8,128)S(1)} %collective-permute-done.5.from_odd, f32[32,2,8,384]{3,2,1,0:T(8,128)S(1)} %shard_map.100.base, bf16[2304,384]{1,0:T(8,128)(2,1)S(1)} %copy-done, ...), custom_call_target="tpu_custom_call" | custom-call | flops 452984832 | bytes 4718600 | tf_op jit(solution)/shard_map/pallas_call | solution.py:412
  61.8 19.7 %all_to_all.15.arrived = f32[16,32,384]{2,1,0:T(8,128)S(1)} all-to-all(f32[16,32,384]{2,1,0:T(8,128)S(1)} %bitcast.7), channel_id=1, replica_groups=mesh['tm'=16,'space'=8] {'tm'}, dimensions={0} | all-to-all | bytes 1572864 | tf_op jit(solution)/shard_map/all_to_all | solution.py:523
  81.5 1.3 %shard_map.102 = f32[2,384,256]{2,1,0:T(8,128)} custom-call(f32[16,32,384]{2,1,0:T(8,128)S(1)} %all_to_all.15.arrived, bf16[256,256]{1,0:T(8,128)(2,1)S(1)} %get-tuple-element.52.order), custom_call_target="tpu_custom_call" | custom-call | flops 201326592 | bytes 1703936 | tf_op jit(solution)/shard_map/pallas_call | solution.py:412
  (19 shorter events, 0.1 us)
Async XLA Ops:
  0.0 19.9 %copy-start.7 = (f32[384]{0:T(512)S(1)}, f32[384]{0:T(512)}, u32[]{:S(2)}) copy-start(f32[384]{0:T(512)} %param.11) | copy-start | bytes 4612
  0.0 19.9 %copy-start.3 = (f32[384,384]{1,0:T(8,128)S(1)}, f32[384,384]{1,0:T(8,128)}, u32[]{:S(2)}) copy-start(f32[384,384]{1,0:T(8,128)} %modes_in.1) | copy-start | bytes 1769476
  0.0 19.9 %copy-start.5 = (f32[256]{0:T(256)S(1)}, f32[256]{0:T(256)}, u32[]{:S(2)}) copy-start(f32[256]{0:T(256)} %param.10) | copy-start | bytes 3076
  2.1 8.2 %all-to-all-start = ((s32[4,8,128]{2,1,0:T(8,128)}), s32[4,8,128]{2,1,0:T(8,128)S(1)}, u32[]{:S(2)}, u32[]{:S(2)}) async-start(s32[4,8,128]{2,1,0:T(8,128)} %shard_map.92), calls=%async_computation | async-start | bytes 32768 | tf_op jit(solution)/shard_map/all_to_all | solution.py:432
  12.1 23.0 %all-to-all-start.1 = ((f32[16,32,384]{2,1,0:T(8,128)}), f32[16,32,384]{2,1,0:T(8,128)S(1)}, u32[]{:S(2)}, u32[]{:S(2)}) async-start(f32[16,32,384]{2,1,0:T(8,128)} %get-tuple-element.31), calls=%async_computation.1 | async-start | bytes 1572864 | tf_op jit(solution)/shard_map/all_to_all | solution.py:453
  20.0 1.2 %copy-start.2 = (f32[6,384,96]{1,2,0:T(8,128)S(1)}, f32[6,384,96]{1,2,0:T(8,128)}, u32[]{:S(2)}) copy-start(f32[6,384,96]{1,2,0:T(8,128)} %param.14) | copy-start | bytes 2654212
  21.1 1.1 %copy-start.4 = (f32[384,384]{1,0:T(8,128)S(1)}, f32[384,384]{1,0:T(8,128)}, u32[]{:S(2)}) copy-start(f32[384,384]{1,0:T(8,128)} %modes_out.1) | copy-start | bytes 1769476
  22.2 1.1 %copy-start.6 = (bf16[768,384]{1,0:T(8,128)(2,1)S(1)}, bf16[768,384]{1,0:T(8,128)(2,1)}, u32[]{:S(2)}) copy-start(bf16[768,384]{1,0:T(8,128)(2,1)} %constant.11.clone.pick) | copy-start | bytes 1769476
  35.1 7.3 %copy-start = (bf16[2304,384]{1,0:T(8,128)(2,1)S(1)}, bf16[2304,384]{1,0:T(8,128)(2,1)}, u32[]{:S(2)}) copy-start(bf16[2304,384]{1,0:T(8,128)(2,1)} %get-tuple-element.43.second_set) | copy-start | bytes 5308420
  38.1 5.8 %collective-permute-start.2 = (f32[384,128]{1,0:T(8,128)S(1)}, f32[384,128]{1,0:T(8,128)S(1)}, u32[]{:S(2)}, u32[]{:S(2)}) collective-permute-start(f32[384,128]{1,0:T(8,128)S(1)} %get-tuple-element.38), channel_id=1, source_target_pairs={{0,8},{8,0},{16,24},{24,16},{32,40},{40,32},{48,56},{56,48},{64,72... | collective-permute-start | bytes 589832 | tf_op jit(solution)/shard_map/ppermute | solution.py:477
  38.2 6.7 %collective-permute-start.3 = (f32[384,128]{1,0:T(8,128)S(1)}, f32[384,128]{1,0:T(8,128)S(1)}, u32[]{:S(2)}, u32[]{:S(2)}) collective-permute-start(f32[384,128]{1,0:T(8,128)S(1)} %get-tuple-element.39), channel_id=1, source_target_pairs={{8,32},{40,64},{72,96},{104,112},{120,80},{88,48},{56,16},{24,0},{... | collective-permute-start | bytes 589832 | tf_op jit(solution)/shard_map/ppermute | solution.py:476
  39.1 7.9 %collective-permute-start = (f32[192,128]{1,0:T(8,128)S(1)}, f32[192,128]{1,0:T(8,128)S(1)}, u32[]{:S(2)}, u32[]{:S(2)}) collective-permute-start(f32[192,128]{1,0:T(8,128)S(1)} %get-tuple-element.36), channel_id=1, source_target_pairs={{0,1},{1,0},{2,3},{3,2},{4,5},{5,4},{6,7},{7,6},{8,9},{9,8},{10,11... | collective-permute-start | bytes 294920 | tf_op jit(solution)/shard_map/ppermute | solution.py:475
  39.1 7.9 %collective-permute-start.1 = (f32[192,128]{1,0:T(8,128)S(1)}, f32[192,128]{1,0:T(8,128)S(1)}, u32[]{:S(2)}, u32[]{:S(2)}) collective-permute-start(f32[192,128]{1,0:T(8,128)S(1)} %get-tuple-element.37), channel_id=1, source_target_pairs={{1,2},{2,1},{3,4},{4,3},{5,6},{6,5},{9,10},{10,9},{11,12},{12,11},... | collective-permute-start | bytes 294920 | tf_op jit(solution)/shard_map/ppermute | solution.py:474
  44.9 2.1 %copy-start.1 = (f32[3,256,384]{2,1,0:T(8,128)S(1)}, f32[3,256,384]{2,1,0:T(8,128)}, u32[]{:S(2)}) copy-start(f32[3,256,384]{2,1,0:T(8,128)} %get-tuple-element.35.factors_far.factors) | copy-start | bytes 3538948
  49.3 7.2 %collective-permute-start.6 = (f32[384,128]{1,0:T(8,128)S(1)}, f32[384,128]{1,0:T(8,128)S(1)}, u32[]{:S(2)}, u32[]{:S(2)}) collective-permute-start(f32[384,128]{1,0:T(8,128)S(1)} %get-tuple-element.47), channel_id=1, source_target_pairs={{0,8},{8,0},{16,24},{24,16},{32,40},{40,32},{48,56},{56,48},{64,72... | collective-permute-start | bytes 589832 | tf_op jit(solution)/shard_map/ppermute | solution.py:477
  49.4 7.7 %collective-permute-start.7 = (f32[384,128]{1,0:T(8,128)S(1)}, f32[384,128]{1,0:T(8,128)S(1)}, u32[]{:S(2)}, u32[]{:S(2)}) collective-permute-start(f32[384,128]{1,0:T(8,128)S(1)} %get-tuple-element.48), channel_id=1, source_target_pairs={{8,32},{40,64},{72,96},{104,112},{120,80},{88,48},{56,16},{24,0},{... | collective-permute-start | bytes 589832 | tf_op jit(solution)/shard_map/ppermute | solution.py:476
  51.0 7.8 %collective-permute-start.4 = (f32[192,128]{1,0:T(8,128)S(1)}, f32[192,128]{1,0:T(8,128)S(1)}, u32[]{:S(2)}, u32[]{:S(2)}) collective-permute-start(f32[192,128]{1,0:T(8,128)S(1)} %get-tuple-element.45), channel_id=1, source_target_pairs={{0,1},{1,0},{2,3},{3,2},{4,5},{5,4},{6,7},{7,6},{8,9},{9,8},{10,11... | collective-permute-start | bytes 294920 | tf_op jit(solution)/shard_map/ppermute | solution.py:475
  51.5 8.1 %collective-permute-start.5 = (f32[192,128]{1,0:T(8,128)S(1)}, f32[192,128]{1,0:T(8,128)S(1)}, u32[]{:S(2)}, u32[]{:S(2)}) collective-permute-start(f32[192,128]{1,0:T(8,128)S(1)} %get-tuple-element.46), channel_id=1, source_target_pairs={{1,2},{2,1},{3,4},{4,3},{5,6},{6,5},{9,10},{10,9},{11,12},{12,11},... | collective-permute-start | bytes 294920 | tf_op jit(solution)/shard_map/ppermute | solution.py:474

commit v8 on v7

--- a/solution.py
+++ b/solution.py
@@ -142,7 +142,7 @@
     index = lax.broadcasted_iota(jnp.int32, (1, SLAB), 1)
     facing = jnp.sum(jnp.where(nbr[1:2, :] == SLAB, index, 0), axis=1, keepdims=True)
     rows = [steps[:, :LANES], steps[:, LANES:], labels, jnp.broadcast_to(facing, (1, LANES))]
-    packed = jnp.concatenate(rows + rows)
+    packed = jnp.concatenate(rows)
     for member in range(SLABS // 2):
         table[member] = packed
 
@@ -194,9 +194,9 @@
     member = place[1] & 3
 
     def step(slab, at):
-        return chain[slab * 8 + lax.shift_right_logical(at, 7), at & 127]
-
-    near = jnp.where(group == 0, chain[27, 0], chain[2, 0]) & 255
+        return chain[slab, lax.shift_right_logical(at, 7), at & 127]
+
+    near = jnp.where(group == 0, chain[3, 3, 0], chain[0, 2, 0]) & 255
     origin = near
     for hop in range(4):
         slab = jnp.where(group == 0, 3 - hop, hop)
@@ -205,7 +205,7 @@
         if hop < 3:
             label = step(slab, far_side) & 127
             ahead = jnp.where(group == 0, 2 - hop, hop + 1)
-            near = chain[ahead * 8 + 2, label] & 255
+            near = chain[ahead, 2, label] & 255
     found = spot[origin] & 127
     first_row, first_sheet = lax.shift_right_logical(found, 4), found & 15
     shift[0] = (8 - first_row) & 7
@@ -425,13 +425,13 @@
     (table,) = call(
         table_kernel,
         [place, (neighbours, HBM), (halo_send, HBM)],
-        [((4, 8, LANES), jnp.int32, KEPT)],
+        [((4, 4, LANES), jnp.int32, KEPT)],
         10**4,
         [pltpu.VMEM(neighbours.shape, jnp.int32), pltpu.VMEM(halo_send.shape, jnp.int32), DMA((2,))],
     )
     chain = lax.all_to_all(
         table, "space", 0, 0, tiled=True, axis_index_groups=[[0, 1, 2, 3], [4, 5, 6, 7]]
-    ).reshape(32, LANES)
+    )
     placed, placed_order, spot = call(
         order_kernel,
         [(neighbours, HBM), (halo_send, HBM), (rhs, HBM)],

time: 83.5 us -> 83.3 us (level)
  no operation moved by 1% of the time
where the time goes in v8:
time: 83.3 us; the launch traced here: 82.8 us
  Pallas kernels  25.1 us (30%)
  starting transfers between devices  21.2 us (25%)
  blocking collectives  19.7 us (24%)
  waiting for transfers between devices  13.1 us (16%)
  local copies, waits for them, and re-layouts  3.31 us (4%)
    pallas_call x12, Pallas kernels, call(): pl.pallas_call(body, out_shape=shapes, in_specs=[spec for _, spec in ins]...  25.1 us
    all_to_all x1, blocking collectives, shards(): back = lax.all_to_all(steps.reshape(16, 32, NB), 'tm', 0, 0, tiled=True)  19.7 us
    all_to_all x1, starting transfers between devices, shards(): arrived = lax.all_to_all(sent, 'tm', 0, 0, tiled=True).reshape(ROWS, NB)  7.8 us
    all_to_all x1, waiting for transfers between devices, shards(): arrived = lax.all_to_all(sent, 'tm', 0, 0, tiled=True).reshape(ROWS, NB)  7.7 us
    ppermute x2, starting transfers between devices, exchange(): from_odd = lax.ppermute(to_odd, 'space', ODD_SIDES)  6.72 us
    all_to_all x1, starting transfers between devices, shards(): lax.all_to_all(table, 'space', 0, 0, tiled=True, axis_index_groups=[[0, 1...  3.49 us
    unnamed x16, local copies, waits for them, and re-layouts  3.31 us
    ppermute x2, starting transfers between devices, exchange(): from_next = lax.ppermute(to_next, 'tm', NEXT_CHIP)  2.51 us
  transfers between devices with their start and end apart: 10, of which 6 were waited for; matrix products, arithmetic and copies ran while one was open for 0% of the time, Pallas kernels for 15%

profile of v8, /device:TPU:4, one launch (start us, length us, event | category | flops | bytes accessed | tf_op | source)
XLA Modules:
  0.0 82.8 jit_solution(4937638581298678546)
XLA Ops:
  0.0 0.1 pad_add_fusion.place
  0.1 1.9 %shard_map.92 = s32[4,4,128]{2,1,0:T(4,128)} custom-call(s32[2]{0:T(128)S(1)} %pad_add_fusion.place, s32[6,256]{1,0:T(8,128)} %nbr_far.3, s32[2,128]{1,0:T(2,128)} %halo_far.3), custom_call_target="tpu_custom_call" | custom-call | flops 10000 | bytes 15368 | tf_op jit(solution)/shard_map/pallas_call | solution.py:412
  2.0 3.5 %all-to-all-start = ((s32[4,4,128]{2,1,0:T(4,128)}), s32[4,4,128]{2,1,0:T(4,128)S(1)}, u32[]{:S(2)}, u32[]{:S(2)}) async-start(s32[4,4,128]{2,1,0:T(4,128)} %shard_map.92), calls=%async_computation | async-start | bytes 16384 | tf_op jit(solution)/shard_map/all_to_all | solution.py:432
  5.5 2.2 %shard_map.91 = (f32[2,32,8,384]{3,2,1,0:T(8,128)S(1)}, f32[32,8,256]{2,1,0:T(8,128)S(1)}, s32[256]{0:T(256)S(1)}) custom-call(s32[6,256]{1,0:T(8,128)} %nbr_far.3, s32[2,128]{1,0:T(2,128)} %halo_far.3, f32[2,384,256]{2,1,0:T(8,128)} %rhs_far.1), custom_call_target="tpu_custom_call" | custom-call | flops 201326592 | bytes 1843200 | tf_op jit(solution)/shard_map/pallas_call | solution.py:412
  7.8 2.5 %all-to-all-done.chain = s32[4,4,128]{2,1,0:T(4,128)S(1)} async-done(((s32[4,4,128]{2,1,0:T(4,128)}), s32[4,4,128]{2,1,0:T(4,128)S(1)}, u32[]{:S(2)}, u32[]{:S(2)}) %all-to-all-start) | async-done | bytes 8224 | tf_op jit(solution)/shard_map/all_to_all | solution.py:432
  10.2 1.7 %shard_map.93 = (f32[16,32,384]{2,1,0:T(8,128)}, s32[2]{0:T(128)S(1)}) custom-call(s32[2]{0:T(128)S(1)} %pad_add_fusion.place, s32[256]{0:T(256)S(1)} %get-tuple-element.29.spot, s32[4,4,128]{2,1,0:T(4,128)S(1)} %all-to-all-done.chain, f32[2,32,8,384]{3,2,1,0:T(8,128)S(1)} %get-tuple-element.30.placed), custom_call_target="tpu_custom_call" | custom-call | flops 1000000 | bytes 1582096 | tf_op jit(solution)/shard_map/pallas_call | solution.py:412
  11.9 7.8 %all-to-all-start.1 = ((f32[16,32,384]{2,1,0:T(8,128)}), f32[16,32,384]{2,1,0:T(8,128)S(1)}, u32[]{:S(2)}, u32[]{:S(2)}) async-start(f32[16,32,384]{2,1,0:T(8,128)} %get-tuple-element.31), calls=%async_computation.1 | async-start | bytes 1572864 | tf_op jit(solution)/shard_map/all_to_all | solution.py:453
  19.8 1.2 %copy-done.2 = f32[6,384,96]{1,2,0:T(8,128)S(1)} copy-done((f32[6,384,96]{1,2,0:T(8,128)S(1)}, f32[6,384,96]{1,2,0:T(8,128)}, u32[]{:S(2)}) %copy-start.2) | copy-done | bytes 884760
  21.0 1.1 %copy-done.4 = f32[384,384]{1,0:T(8,128)S(1)} copy-done((f32[384,384]{1,0:T(8,128)S(1)}, f32[384,384]{1,0:T(8,128)}, u32[]{:S(2)}) %copy-start.4) | copy-done | bytes 589848
  22.0 1.1 %copy-done.6 = bf16[768,384]{1,0:T(8,128)(2,1)S(1)} copy-done((bf16[768,384]{1,0:T(8,128)(2,1)S(1)}, bf16[768,384]{1,0:T(8,128)(2,1)}, u32[]{:S(2)}) %copy-start.6) | copy-done | bytes 589848
  23.1 4.1 %shard_map.94 = (bf16[256,256]{1,0:T(8,128)(2,1)S(1)}, bf16[2304,384]{1,0:T(8,128)(2,1)S(1)}, f32[3,256,384]{2,1,0:T(8,128)}, bf16[2304,384]{1,0:T(8,128)(2,1)}) custom-call(s32[2]{0:T(128)S(1)} %pad_add_fusion.place, s32[2]{0:T(128)S(1)} %get-tuple-element.32.shift, f32[32,8,256]{2,1,0:T(8,128)S(1)} %get-tuple-element.33.placed_order, ...), custom_call_target="tpu_custom_call" | custom-call | flops 1132462080 | bytes 7768592 | tf_op jit(solution)/shard_map/pallas_call | solution.py:412
  27.2 7.7 %all-to-all-done.1 = f32[16,32,384]{2,1,0:T(8,128)S(1)} async-done(((f32[16,32,384]{2,1,0:T(8,128)}), f32[16,32,384]{2,1,0:T(8,128)S(1)}, u32[]{:S(2)}, u32[]{:S(2)}) %all-to-all-start.1) | async-done | bytes 786464 | tf_op jit(solution)/shard_map/all_to_all | solution.py:453
  34.9 3.0 %shard_map.95 = (f32[512,384]{1,0:T(8,128)S(1)}, bf16[512,384]{1,0:T(8,128)(2,1)S(1)}, bf16[512,384]{1,0:T(8,128)(2,1)S(1)}, f32[2,256,128]{2,1,0:T(8,128)S(1)},...) custom-call(s32[2]{0:T(128)S(1)} %pad_add_fusion.place, ...), custom_call_target="tpu_custom_call" | custom-call | flops 1056964608 | bytes 6160392 | tf_op jit(solution)/shard_map/pallas_call | solution.py:412
  38.0 0.1 collective-permute-start.2
  38.0 0.9 %collective-permute-start.3 = (f32[384,128]{1,0:T(8,128)S(1)}, f32[384,128]{1,0:T(8,128)S(1)}, u32[]{:S(2)}, u32[]{:S(2)}) collective-permute-start(f32[384,128]{1,0:T(8,128)S(1)} %get-tuple-element.39), channel_id=1, source_target_pairs={{8,32},{40,64},{72,96},{104,112},{120,80},{88,48},{56,16},{24,0},{... | collective-permute-start | bytes 589832 | tf_op jit(solution)/shard_map/ppermute | solution.py:476
  39.0 3.2 %collective-permute-start.1 = (f32[192,128]{1,0:T(8,128)S(1)}, f32[192,128]{1,0:T(8,128)S(1)}, u32[]{:S(2)}, u32[]{:S(2)}) collective-permute-start(f32[192,128]{1,0:T(8,128)S(1)} %get-tuple-element.37), channel_id=1, source_target_pairs={{1,2},{2,1},{3,4},{4,3},{5,6},{6,5},{9,10},{10,9},{11,12},{12,11},... | collective-permute-start | bytes 294920 | tf_op jit(solution)/shard_map/ppermute | solution.py:474
  42.2 1.5 %shard_map.96.base = f32[512,384]{1,0:T(8,128)S(1)} custom-call(f32[512,384]{1,0:T(8,128)S(1)} %get-tuple-element.40.modal, bf16[512,384]{1,0:T(8,128)(2,1)S(1)} %get-tuple-element.41.solved_h, bf16[512,384]{1,0:T(8,128)(2,1)S(1)} %get-tuple-element.42.solved_l, bf16[2304,384]{1,0:T(8,128)(2,1)S(1)} %get-tuple-element.34.first_set, bf16[2304,384]{1,0:T(8,128)(2,1)S(1)} %copy-done), custom_call_target="tpu_custom_call" | custom-call | flops 603979776 | bytes 5898240 | tf_op jit(solution)/shard_map/pallas_call | solution.py:412
  43.8 1.0 %collective-permute-done.3.from_next = f32[384,128]{1,0:T(8,128)S(1)} collective-permute-done((f32[384,128]{1,0:T(8,128)S(1)}, f32[384,128]{1,0:T(8,128)S(1)}, u32[]{:S(2)}, u32[]{:S(2)}) %collective-permute-start.3) | collective-permute-done | bytes 196640 | tf_op jit(solution)/shard_map/ppermute | solution.py:476
  44.7 1.6 %shard_map.97.base = f32[32,2,8,384]{3,2,1,0:T(8,128)S(1)} custom-call(s32[2]{0:T(128)S(1)} %pad_add_fusion.place, f32[384,128]{1,0:T(8,128)S(1)} %collective-permute-done.2.from_chip, f32[384,128]{1,0:T(8,128)S(1)} %collective-permute-done.3.from_next, f32[512,384]{1,0:T(8,128)S(1)} %shard_map.96.base, f32[2,256,128]{2,1,0:T(8,128)S(1)} %get-tuple-element.44.inner, ...), custom_call_target="tpu_custom_call" | custom-call | flops 603979776 | bytes 3997704 | tf_op jit(solution)/shard_map/pallas_call | solution.py:412
  46.3 0.5 collective-permute-done.from_even
  46.8 2.3 %shard_map.98 = (bf16[512,384]{1,0:T(8,128)(2,1)S(1)}, bf16[512,384]{1,0:T(8,128)(2,1)S(1)}, f32[2,256,128]{2,1,0:T(8,128)S(1)}, f32[384,128]{1,0:T(8,128)S(1)},...) custom-call(s32[2]{0:T(128)S(1)} %pad_add_fusion.place, ...), custom_call_target="tpu_custom_call" | custom-call | flops 603979776 | bytes 7340040 | tf_op jit(solution)/shard_map/pallas_call | solution.py:412
  49.1 0.1 collective-permute-start.6
  49.2 1.6 %collective-permute-start.7 = (f32[384,128]{1,0:T(8,128)S(1)}, f32[384,128]{1,0:T(8,128)S(1)}, u32[]{:S(2)}, u32[]{:S(2)}) collective-permute-start(f32[384,128]{1,0:T(8,128)S(1)} %get-tuple-element.48), channel_id=1, source_target_pairs={{8,32},{40,64},{72,96},{104,112},{120,80},{88,48},{56,16},{24,0},{... | collective-permute-start | bytes 589832 | tf_op jit(solution)/shard_map/ppermute | solution.py:476
  50.8 0.5 collective-permute-start.4
  51.3 3.5 %collective-permute-start.5 = (f32[192,128]{1,0:T(8,128)S(1)}, f32[192,128]{1,0:T(8,128)S(1)}, u32[]{:S(2)}, u32[]{:S(2)}) collective-permute-start(f32[192,128]{1,0:T(8,128)S(1)} %get-tuple-element.46), channel_id=1, source_target_pairs={{1,2},{2,1},{3,4},{4,3},{5,6},{6,5},{9,10},{10,9},{11,12},{12,11},... | collective-permute-start | bytes 294920 | tf_op jit(solution)/shard_map/ppermute | solution.py:474
  54.8 1.5 %shard_map.99.base = f32[512,384]{1,0:T(8,128)S(1)} custom-call(f32[512,384]{1,0:T(8,128)S(1)} %get-tuple-element.40.modal, bf16[512,384]{1,0:T(8,128)(2,1)S(1)} %get-tuple-element.49.solved_h, bf16[512,384]{1,0:T(8,128)(2,1)S(1)} %get-tuple-element.50.solved_l, bf16[2304,384]{1,0:T(8,128)(2,1)S(1)} %get-tuple-element.34.first_set, bf16[2304,384]{1,0:T(8,128)(2,1)S(1)} %copy-done), custom_call_target="tpu_custom_call" | custom-call | flops 603979776 | bytes 5898240 | tf_op jit(solution)/shard_map/pallas_call | solution.py:412
  56.3 0.6 collective-permute-done.7.from_next
  57.0 1.6 %shard_map.100.base = f32[32,2,8,384]{3,2,1,0:T(8,128)S(1)} custom-call(s32[2]{0:T(128)S(1)} %pad_add_fusion.place, f32[384,128]{1,0:T(8,128)S(1)} %collective-permute-done.6.from_chip, f32[384,128]{1,0:T(8,128)S(1)} %collective-permute-done.7.from_next, f32[512,384]{1,0:T(8,128)S(1)} %shard_map.99.base, f32[2,256,128]{2,1,0:T(8,128)S(1)} %get-tuple-element.51.inner, ...), custom_call_target="tpu_custom_call" | custom-call | flops 603979776 | bytes 3997704 | tf_op jit(solution)/shard_map/pallas_call | solution.py:412
  58.6 0.9 %collective-permute-done.5.from_odd = f32[192,128]{1,0:T(8,128)S(1)} collective-permute-done((f32[192,128]{1,0:T(8,128)S(1)}, f32[192,128]{1,0:T(8,128)S(1)}, u32[]{:S(2)}, u32[]{:S(2)}) %collective-permute-start.5) | collective-permute-done | bytes 98336 | tf_op jit(solution)/shard_map/ppermute | solution.py:474
  59.4 2.2 %shard_map.101 = f32[512,384]{1,0:T(8,128)S(1)} custom-call(s32[2]{0:T(128)S(1)} %pad_add_fusion.place, f32[192,128]{1,0:T(8,128)S(1)} %collective-permute-done.4.from_even, f32[192,128]{1,0:T(8,128)S(1)} %collective-permute-done.5.from_odd, f32[32,2,8,384]{3,2,1,0:T(8,128)S(1)} %shard_map.100.base, bf16[2304,384]{1,0:T(8,128)(2,1)S(1)} %copy-done, ...), custom_call_target="tpu_custom_call" | custom-call | flops 452984832 | bytes 4718600 | tf_op jit(solution)/shard_map/pallas_call | solution.py:412
  61.6 19.7 %all_to_all.15.arrived = f32[16,32,384]{2,1,0:T(8,128)S(1)} all-to-all(f32[16,32,384]{2,1,0:T(8,128)S(1)} %bitcast.6), channel_id=1, replica_groups=mesh['tm'=16,'space'=8] {'tm'}, dimensions={0} | all-to-all | bytes 1572864 | tf_op jit(solution)/shard_map/all_to_all | solution.py:523
  81.4 1.3 %shard_map.102 = f32[2,384,256]{2,1,0:T(8,128)} custom-call(f32[16,32,384]{2,1,0:T(8,128)S(1)} %all_to_all.15.arrived, bf16[256,256]{1,0:T(8,128)(2,1)S(1)} %get-tuple-element.52.order), custom_call_target="tpu_custom_call" | custom-call | flops 201326592 | bytes 1703936 | tf_op jit(solution)/shard_map/pallas_call | solution.py:412
  (19 shorter events, 0.0 us)
Async XLA Ops:
  0.0 19.8 %copy-start.7 = (f32[384]{0:T(512)S(1)}, f32[384]{0:T(512)}, u32[]{:S(2)}) copy-start(f32[384]{0:T(512)} %param.11) | copy-start | bytes 4612
  0.0 19.8 %copy-start.3 = (f32[384,384]{1,0:T(8,128)S(1)}, f32[384,384]{1,0:T(8,128)}, u32[]{:S(2)}) copy-start(f32[384,384]{1,0:T(8,128)} %modes_in.1) | copy-start | bytes 1769476
  0.0 19.8 %copy-start.5 = (f32[256]{0:T(256)S(1)}, f32[256]{0:T(256)}, u32[]{:S(2)}) copy-start(f32[256]{0:T(256)} %param.10) | copy-start | bytes 3076
  2.0 8.2 %all-to-all-start = ((s32[4,4,128]{2,1,0:T(4,128)}), s32[4,4,128]{2,1,0:T(4,128)S(1)}, u32[]{:S(2)}, u32[]{:S(2)}) async-start(s32[4,4,128]{2,1,0:T(4,128)} %shard_map.92), calls=%async_computation | async-start | bytes 16384 | tf_op jit(solution)/shard_map/all_to_all | solution.py:432
  11.9 23.0 %all-to-all-start.1 = ((f32[16,32,384]{2,1,0:T(8,128)}), f32[16,32,384]{2,1,0:T(8,128)S(1)}, u32[]{:S(2)}, u32[]{:S(2)}) async-start(f32[16,32,384]{2,1,0:T(8,128)} %get-tuple-element.31), calls=%async_computation.1 | async-start | bytes 1572864 | tf_op jit(solution)/shard_map/all_to_all | solution.py:453
  19.8 1.2 %copy-start.2 = (f32[6,384,96]{1,2,0:T(8,128)S(1)}, f32[6,384,96]{1,2,0:T(8,128)}, u32[]{:S(2)}) copy-start(f32[6,384,96]{1,2,0:T(8,128)} %param.14) | copy-start | bytes 2654212
  21.0 1.1 %copy-start.4 = (f32[384,384]{1,0:T(8,128)S(1)}, f32[384,384]{1,0:T(8,128)}, u32[]{:S(2)}) copy-start(f32[384,384]{1,0:T(8,128)} %modes_out.1) | copy-start | bytes 1769476
  22.0 1.1 %copy-start.6 = (bf16[768,384]{1,0:T(8,128)(2,1)S(1)}, bf16[768,384]{1,0:T(8,128)(2,1)}, u32[]{:S(2)}) copy-start(bf16[768,384]{1,0:T(8,128)(2,1)} %constant.11.clone.pick) | copy-start | bytes 1769476
  34.9 7.3 %copy-start = (bf16[2304,384]{1,0:T(8,128)(2,1)S(1)}, bf16[2304,384]{1,0:T(8,128)(2,1)}, u32[]{:S(2)}) copy-start(bf16[2304,384]{1,0:T(8,128)(2,1)} %get-tuple-element.43.second_set) | copy-start | bytes 5308420
  38.0 5.8 %collective-permute-start.2 = (f32[384,128]{1,0:T(8,128)S(1)}, f32[384,128]{1,0:T(8,128)S(1)}, u32[]{:S(2)}, u32[]{:S(2)}) collective-permute-start(f32[384,128]{1,0:T(8,128)S(1)} %get-tuple-element.38), channel_id=1, source_target_pairs={{0,8},{8,0},{16,24},{24,16},{32,40},{40,32},{48,56},{56,48},{64,72... | collective-permute-start | bytes 589832 | tf_op jit(solution)/shard_map/ppermute | solution.py:477
  38.0 6.7 %collective-permute-start.3 = (f32[384,128]{1,0:T(8,128)S(1)}, f32[384,128]{1,0:T(8,128)S(1)}, u32[]{:S(2)}, u32[]{:S(2)}) collective-permute-start(f32[384,128]{1,0:T(8,128)S(1)} %get-tuple-element.39), channel_id=1, source_target_pairs={{8,32},{40,64},{72,96},{104,112},{120,80},{88,48},{56,16},{24,0},{... | collective-permute-start | bytes 589832 | tf_op jit(solution)/shard_map/ppermute | solution.py:476
  39.0 7.9 %collective-permute-start = (f32[192,128]{1,0:T(8,128)S(1)}, f32[192,128]{1,0:T(8,128)S(1)}, u32[]{:S(2)}, u32[]{:S(2)}) collective-permute-start(f32[192,128]{1,0:T(8,128)S(1)} %get-tuple-element.36), channel_id=1, source_target_pairs={{0,1},{1,0},{2,3},{3,2},{4,5},{5,4},{6,7},{7,6},{8,9},{9,8},{10,11... | collective-permute-start | bytes 294920 | tf_op jit(solution)/shard_map/ppermute | solution.py:475
  39.0 7.9 %collective-permute-start.1 = (f32[192,128]{1,0:T(8,128)S(1)}, f32[192,128]{1,0:T(8,128)S(1)}, u32[]{:S(2)}, u32[]{:S(2)}) collective-permute-start(f32[192,128]{1,0:T(8,128)S(1)} %get-tuple-element.37), channel_id=1, source_target_pairs={{1,2},{2,1},{3,4},{4,3},{5,6},{6,5},{9,10},{10,9},{11,12},{12,11},... | collective-permute-start | bytes 294920 | tf_op jit(solution)/shard_map/ppermute | solution.py:474
  44.7 2.1 %copy-start.1 = (f32[3,256,384]{2,1,0:T(8,128)S(1)}, f32[3,256,384]{2,1,0:T(8,128)}, u32[]{:S(2)}) copy-start(f32[3,256,384]{2,1,0:T(8,128)} %get-tuple-element.35.factors_far.factors) | copy-start | bytes 3538948
  49.1 7.2 %collective-permute-start.6 = (f32[384,128]{1,0:T(8,128)S(1)}, f32[384,128]{1,0:T(8,128)S(1)}, u32[]{:S(2)}, u32[]{:S(2)}) collective-permute-start(f32[384,128]{1,0:T(8,128)S(1)} %get-tuple-element.47), channel_id=1, source_target_pairs={{0,8},{8,0},{16,24},{24,16},{32,40},{40,32},{48,56},{56,48},{64,72... | collective-permute-start | bytes 589832 | tf_op jit(solution)/shard_map/ppermute | solution.py:477
  49.2 7.7 %collective-permute-start.7 = (f32[384,128]{1,0:T(8,128)S(1)}, f32[384,128]{1,0:T(8,128)S(1)}, u32[]{:S(2)}, u32[]{:S(2)}) collective-permute-start(f32[384,128]{1,0:T(8,128)S(1)} %get-tuple-element.48), channel_id=1, source_target_pairs={{8,32},{40,64},{72,96},{104,112},{120,80},{88,48},{56,16},{24,0},{... | collective-permute-start | bytes 589832 | tf_op jit(solution)/shard_map/ppermute | solution.py:476
  50.8 7.7 %collective-permute-start.4 = (f32[192,128]{1,0:T(8,128)S(1)}, f32[192,128]{1,0:T(8,128)S(1)}, u32[]{:S(2)}, u32[]{:S(2)}) collective-permute-start(f32[192,128]{1,0:T(8,128)S(1)} %get-tuple-element.45), channel_id=1, source_target_pairs={{0,1},{1,0},{2,3},{3,2},{4,5},{5,4},{6,7},{7,6},{8,9},{9,8},{10,11... | collective-permute-start | bytes 294920 | tf_op jit(solution)/shard_map/ppermute | solution.py:475
  51.3 8.1 %collective-permute-start.5 = (f32[192,128]{1,0:T(8,128)S(1)}, f32[192,128]{1,0:T(8,128)S(1)}, u32[]{:S(2)}, u32[]{:S(2)}) collective-permute-start(f32[192,128]{1,0:T(8,128)S(1)} %get-tuple-element.46), channel_id=1, source_target_pairs={{1,2},{2,1},{3,4},{4,3},{5,6},{6,5},{9,10},{10,9},{11,12},{12,11},... | collective-permute-start | bytes 294920 | tf_op jit(solution)/shard_map/ppermute | solution.py:474
